TPU v7x, 128 devices: a whole 4x4x4 slice. The times are simulated.
128 devices in a mesh: section: 2 (over core), dp: 64 (over x, y, z).
Axes of the slice: x: 4, y: 4, z: 4, core: 2. Of those that a mesh axis runs over, the one named last changes fastest.
Arguments:
- latents_in: bfloat16 [3, 64, 64, 1024], P(None, 'dp'), may hold values from -6 to 6
- media: bfloat16 [3, 64, 512, 1024], P(None, 'dp'), may hold values from -6 to 6
- frame_count: int32 [3, 64], P(None, 'dp'), may hold values from 1 to 8, as said below
- gains: float32 [2, 3, 1024], P('section'), may hold values from 0.25 to 1.75
- biases: float32 [2, 3, 1024], P('section'), may hold values from -2 to 2
- w_query: bfloat16 [2, 1024, 512], P('section'), may hold values from -0.1875 to 0.1875
- w_keyval: bfloat16 [2, 1024, 1024], P('section'), may hold values from -0.1875 to 0.1875
- w_out: bfloat16 [2, 512, 1024], P('section'), may hold values from -4 to 4
- w_up: bfloat16 [2, 1024, 4096], P('section'), may hold values from -0.1875 to 0.1875
- w_down: bfloat16 [2, 4096, 1024], P('section'), may hold values from -0.09375 to 0.09375
- cotangent: bfloat16 [3, 64, 64, 1024], P(None, 'dp'), may hold values from -6 to 6
Outputs:
- resampled: float32 [3, 64, 64, 1024], P(None, 'dp', None, 'section')
- latents_grad: float32 [3, 64, 64, 1024], P(None, 'dp', None, 'section')
- media_grad: float32 [3, 64, 512, 1024], P(None, 'dp', None, 'section')
- gains_grad: float32 [2, 3, 1024], P('section', None, 'dp')
- biases_grad: float32 [2, 3, 1024], P('section', None, 'dp')
- w_query_grad: float32 [2, 1024, 512], P('section', 'dp')
- w_keyval_grad: float32 [2, 1024, 1024], P('section', 'dp')
- w_out_grad: float32 [2, 512, 1024], P('section', 'dp')
- w_up_grad: float32 [2, 1024, 4096], P('section', 'dp')
- w_down_grad: float32 [2, 4096, 1024], P('section', 'dp')
Inputs may be any that keep to these rules, and one draw needn't show every extreme that they name: The first frame_count frame slots of a video, 64 patches each, are real and the rest are padding.
All inputs are finite; a program needn't handle non-finite values.
Results may differ from a plain program's by a relative error of at most 0.015.
Values sent between devices are 32-bit elements; how exact they have to be, the bound alone decides.
A program may use at most 320 MiB of HBM per device.

v0:
```python
import jax
import jax.numpy as jnp
from jax import lax
from jax.sharding import PartitionSpec as P

HEADS = 8
PATCHES = 64


NORM_EPS = 1e-05
MASK_FILL = -1e30
ROOT_HALF = 0.7071067811865476
INV_ROOT_TAU = 0.3989422804014327


def passed_along(block, axis, distance):
    devices = range(lax.axis_size(axis))
    route = [((i - distance) % len(devices), i) for i in devices]
    return lax.ppermute(block, axis, route)


def matmul(left, right):
    return jnp.dot(left, right, preferred_element_type=jnp.float32)


def cross_rows(left, right):
    return lax.dot_general(
        left, right, (((0,), (0,)), ((), ())), preferred_element_type=jnp.float32
    )


def against_rows(left, right):
    return lax.dot_general(
        left, right, (((1,), (1,)), ((), ())), preferred_element_type=jnp.float32
    )


def norm_parts(values_in, gain_row, bias_row):
    average = jnp.mean(values_in, -1, keepdims=True)
    centred = values_in - average
    inverse = lax.rsqrt(jnp.mean(centred * centred, -1, keepdims=True) + NORM_EPS)
    normed = centred * inverse
    return (normed * gain_row + bias_row, normed, inverse)


def norm_back(grad_rows, normed, inverse, gain_row):
    scaled = grad_rows * gain_row
    inner_mean = jnp.mean(scaled, -1, keepdims=True)
    along_mean = jnp.mean(scaled * normed, -1, keepdims=True)
    grad_in = inverse * (scaled - inner_mean - normed * along_mean)
    return (grad_in, jnp.sum(grad_rows * normed, 0), jnp.sum(grad_rows, 0))


def gelu_slope(pre_act):
    return (
        0.5 * (1.0 + lax.erf(pre_act * ROOT_HALF))
        + pre_act * jnp.exp(-0.5 * pre_act * pre_act) * INV_ROOT_TAU
    )


def layer_forward(layer_input, media_rows, key_valid, norm_gains, norm_biases, weights, head_count):
    w_query, w_keyval, w_out, w_up, w_down = weights
    inner_width = w_query.shape[1]
    head_width = inner_width // head_count
    score_scale = head_width ** (-0.5)
    latent_rows = layer_input.shape[0]
    media_full, media_normed, media_inverse = norm_parts(
        media_rows.astype(jnp.float32), norm_gains[0], norm_biases[0]
    )
    media_in = media_full.astype(jnp.bfloat16)
    latent_full, latent_normed, latent_inverse = norm_parts(
        layer_input, norm_gains[1], norm_biases[1]
    )
    latent_in = latent_full.astype(jnp.bfloat16)
    queries = (matmul(latent_in, w_query) * score_scale).astype(jnp.bfloat16)
    keyvals = jnp.concatenate([matmul(media_in, w_keyval), matmul(latent_in, w_keyval)], 0).astype(
        jnp.bfloat16
    )
    key_count = keyvals.shape[0]
    query_heads = queries.reshape(latent_rows, head_count, head_width)
    key_heads = keyvals[:, :inner_width].reshape(key_count, head_count, head_width)
    value_heads = keyvals[:, inner_width:].reshape(key_count, head_count, head_width)
    scores = jnp.einsum("lhe,khe->hlk", query_heads, key_heads, preferred_element_type=jnp.float32)
    scores = jnp.where(key_valid, scores, MASK_FILL)
    attention = jnp.exp(scores - jnp.max(scores, -1, keepdims=True))
    attention = attention / jnp.sum(attention, -1, keepdims=True)
    attention_low = attention.astype(jnp.bfloat16)
    attended = jnp.einsum(
        "hlk,khe->lhe", attention_low, value_heads, preferred_element_type=jnp.float32
    )
    attended = attended.reshape(latent_rows, inner_width).astype(jnp.bfloat16)
    mixed = layer_input + matmul(attended, w_out)
    ff_full, ff_normed, ff_inverse = norm_parts(mixed, norm_gains[2], norm_biases[2])
    ff_in = ff_full.astype(jnp.bfloat16)
    pre_act = matmul(ff_in, w_up)
    activated = jax.nn.gelu(pre_act, approximate=False).astype(jnp.bfloat16)
    layer_out = mixed + matmul(activated, w_down)
    kept_state = (
        media_in,
        media_normed,
        media_inverse,
        latent_in,
        latent_normed,
        latent_inverse,
        query_heads,
        key_heads,
        value_heads,
        attention,
        attention_low,
        attended,
        ff_in,
        ff_normed,
        ff_inverse,
        pre_act,
        activated,
    )
    return (layer_out, kept_state)


def layer_backward(grad_y, kept_state, norm_gains, weights, head_count):
    (
        media_in,
        media_normed,
        media_inverse,
        latent_in,
        latent_normed,
        latent_inverse,
        query_heads,
        key_heads,
        value_heads,
        attention,
        attention_low,
        attended,
        ff_in,
        ff_normed,
        ff_inverse,
        pre_act,
        activated,
    ) = kept_state
    w_query, w_keyval, w_out, w_up, w_down = weights
    inner_width = w_query.shape[1]
    head_width = inner_width // head_count
    score_scale = head_width ** (-0.5)
    latent_rows = grad_y.shape[0]
    key_count = key_heads.shape[0]
    slot_count = media_in.shape[0]
    grad_out = grad_y.astype(jnp.bfloat16)
    w_down_term = cross_rows(activated, grad_out)
    grad_pre = (against_rows(grad_out, w_down) * gelu_slope(pre_act)).astype(jnp.bfloat16)
    w_up_term = cross_rows(ff_in, grad_pre)
    grad_ffn, ff_gain_term, ff_bias_term = norm_back(
        against_rows(grad_pre, w_up), ff_normed, ff_inverse, norm_gains[2]
    )
    grad_mixed = grad_y + grad_ffn
    grad_attn = grad_mixed.astype(jnp.bfloat16)
    w_out_term = cross_rows(attended, grad_attn)
    grad_att = (
        against_rows(grad_attn, w_out)
        .astype(jnp.bfloat16)
        .reshape(latent_rows, head_count, head_width)
    )
    grad_probs = jnp.einsum(
        "lhe,khe->hlk", grad_att, value_heads, preferred_element_type=jnp.float32
    )
    grad_scores = attention * (grad_probs - jnp.sum(attention * grad_probs, -1, keepdims=True))
    grad_scores = grad_scores.astype(jnp.bfloat16)
    grad_queries = jnp.einsum(
        "hlk,khe->lhe", grad_scores, key_heads, preferred_element_type=jnp.float32
    )
    grad_queries = grad_queries.astype(jnp.bfloat16).reshape(latent_rows, inner_width)
    grad_keys = jnp.einsum(
        "hlk,lhe->khe", grad_scores, query_heads, preferred_element_type=jnp.float32
    )
    grad_values = jnp.einsum(
        "hlk,lhe->khe", attention_low, grad_att, preferred_element_type=jnp.float32
    )
    grad_keyvals = jnp.concatenate(
        [grad_keys.reshape(key_count, inner_width), grad_values.reshape(key_count, inner_width)], 1
    ).astype(jnp.bfloat16)
    grad_media_kv = grad_keyvals[:slot_count]
    grad_latent_kv = grad_keyvals[slot_count:]
    w_keyval_term = cross_rows(media_in, grad_media_kv) + cross_rows(latent_in, grad_latent_kv)
    w_query_term = cross_rows(latent_in, grad_queries) * score_scale
    grad_media_in = against_rows(grad_media_kv, w_keyval)
    grad_latent_in = against_rows(grad_queries, w_query) * score_scale + against_rows(
        grad_latent_kv, w_keyval
    )
    grad_media, media_gain_term, media_bias_term = norm_back(
        grad_media_in, media_normed, media_inverse, norm_gains[0]
    )
    grad_latent, latent_gain_term, latent_bias_term = norm_back(
        grad_latent_in, latent_normed, latent_inverse, norm_gains[1]
    )
    grad_input = grad_mixed + grad_latent
    gain_terms = jnp.stack([media_gain_term, latent_gain_term, ff_gain_term])
    bias_terms = jnp.stack([media_bias_term, latent_bias_term, ff_bias_term])
    return (
        grad_input,
        grad_media,
        (gain_terms, bias_terms, w_query_term, w_keyval_term, w_out_term, w_up_term, w_down_term),
    )


def body(
    latents_in, media, frame_count, gains, biases, w_query, w_keyval, w_out, w_up, w_down, cotangent
):
    section_index = lax.axis_index("section")
    micro_count = media.shape[0]
    slot_count = media.shape[2]
    model_width = media.shape[3]
    latent_rows = latents_in.shape[2]
    half_width = model_width // 2
    head_count = HEADS
    norm_gains = gains[0]
    norm_biases = biases[0]
    weights = (w_query[0], w_keyval[0], w_out[0], w_up[0], w_down[0])
    frame_of_slot = jnp.arange(slot_count) // PATCHES

    def key_mask(micro_index):
        frames_real = lax.dynamic_index_in_dim(frame_count, micro_index, 0, keepdims=False)[0]
        return jnp.concatenate([frame_of_slot < frames_real, jnp.ones((latent_rows,), dtype=bool)])

    def media_of(micro_index):
        return lax.dynamic_index_in_dim(media, micro_index, 0, keepdims=False)[0]

    received = jnp.zeros((latent_rows, model_width), jnp.float32)
    section_inputs = jnp.zeros((micro_count, latent_rows, model_width), jnp.float32)
    resampled = jnp.zeros((micro_count, latent_rows, half_width), jnp.float32)
    for moment in range(micro_count + 1):
        micro_index = jnp.clip(moment - section_index, 0, micro_count - 1)
        given_latents = lax.dynamic_index_in_dim(latents_in, micro_index, 0, keepdims=False)[
            0
        ].astype(jnp.float32)
        layer_input = jnp.where(section_index == 0, given_latents, received)
        section_inputs = lax.dynamic_update_index_in_dim(
            section_inputs, layer_input, micro_index, 0
        )
        layer_out, unused_state = layer_forward(
            layer_input,
            media_of(micro_index),
            key_mask(micro_index),
            norm_gains,
            norm_biases,
            weights,
            head_count,
        )
        received = passed_along(layer_out, "section", 1)
        if moment > 0:
            complete = jnp.where(section_index == 1, layer_out, received)
            resampled = resampled.at[moment - 1].set(
                lax.dynamic_slice_in_dim(complete, section_index * half_width, half_width, 1)
            )
    received = jnp.zeros((latent_rows, model_width), jnp.float32)
    latents_grad = jnp.zeros((micro_count, latent_rows, half_width), jnp.float32)
    media_terms = jnp.zeros((micro_count, slot_count, model_width), jnp.float32)
    totals = (
        jnp.zeros(gains.shape[1:], jnp.float32),
        jnp.zeros(biases.shape[1:], jnp.float32),
        jnp.zeros(w_query.shape[1:], jnp.float32),
        jnp.zeros(w_keyval.shape[1:], jnp.float32),
        jnp.zeros(w_out.shape[1:], jnp.float32),
        jnp.zeros(w_up.shape[1:], jnp.float32),
        jnp.zeros(w_down.shape[1:], jnp.float32),
    )
    for moment in range(micro_count + 1):
        position = moment - 1 + section_index
        is_valid = (position >= 0) & (position < micro_count)
        micro_index = jnp.clip(position, 0, micro_count - 1)
        given_grad = lax.dynamic_index_in_dim(cotangent, micro_index, 0, keepdims=False)[0].astype(
            jnp.float32
        )
        grad_y = jnp.where(section_index == 1, given_grad, received)
        layer_input = lax.dynamic_index_in_dim(section_inputs, micro_index, 0, keepdims=False)
        layer_out, kept_state = layer_forward(
            layer_input,
            media_of(micro_index),
            key_mask(micro_index),
            norm_gains,
            norm_biases,
            weights,
            head_count,
        )
        grad_input, grad_media, grad_terms = layer_backward(
            grad_y, kept_state, norm_gains, weights, head_count
        )
        received = passed_along(grad_input, "section", 1)
        if moment > 0:
            complete = jnp.where(section_index == 0, grad_input, received)
            latents_grad = latents_grad.at[moment - 1].set(
                lax.dynamic_slice_in_dim(complete, section_index * half_width, half_width, 1)
            )
        media_terms = media_terms.at[micro_index].add(jnp.where(is_valid, grad_media, 0.0))
        grad_terms = tuple((jnp.where(is_valid, term, 0.0) for term in grad_terms))
        totals = tuple(
            (left_term + right_term for left_term, right_term in zip(totals, grad_terms))
        )
    shards = (
        lax.psum_scatter(totals[0], "dp", scatter_dimension=1, tiled=True),
        lax.psum_scatter(totals[1], "dp", scatter_dimension=1, tiled=True),
        lax.psum_scatter(totals[2], "dp", scatter_dimension=0, tiled=True),
        lax.psum_scatter(totals[3], "dp", scatter_dimension=0, tiled=True),
        lax.psum_scatter(totals[4], "dp", scatter_dimension=0, tiled=True),
        lax.psum_scatter(totals[5], "dp", scatter_dimension=0, tiled=True),
        lax.psum_scatter(totals[6], "dp", scatter_dimension=0, tiled=True),
    )
    media_grad = lax.psum_scatter(media_terms, "section", scatter_dimension=2, tiled=True)
    return (
        resampled[:, None],
        latents_grad[:, None],
        media_grad[:, None],
        shards[0][None],
        shards[1][None],
        shards[2][None],
        shards[3][None],
        shards[4][None],
        shards[5][None],
        shards[6][None],
    )


def solution(mesh):
    placed = (
        P(None, "dp", None, None),
        P(None, "dp", None, None),
        P(None, "dp"),
        P("section", None, None),
        P("section", None, None),
        P("section", None, None),
        P("section", None, None),
        P("section", None, None),
        P("section", None, None),
        P("section", None, None),
        P(None, "dp", None, None),
    )
    return jax.shard_map(
        body,
        mesh=mesh,
        in_specs=placed,
        out_specs=(
            P(None, "dp", None, "section"),
            P(None, "dp", None, "section"),
            P(None, "dp", None, "section"),
            P("section", None, "dp"),
            P("section", None, "dp"),
            P("section", "dp", None),
            P("section", "dp", None),
            P("section", "dp", None),
            P("section", "dp", None),
            P("section", "dp", None),
        ),
        check_vma=False,
    )
```

profile of v0, /device:TPU:0, one launch (start us, length us, event | category | flops | bytes accessed | tf_op | source)
XLA Modules:
  0.0 2919.7 jit_solution(15823087490812173842)
XLA Ops:
  12.6 4.7 convert_reduce_fusion
  17.4 3.4 fusion.181
  38.0 11.7 fusion.285
  53.3 3.7 fusion.247
  83.1 3.2 fusion.1231
  89.6 11.9 fusion.288
  120.9 3.2 fusion.1235
  127.3 11.7 fusion.291
  139.4 3.5 fusion.262
  157.6 2.7 fusion.1243
  164.1 5.2 fusion.38
  169.3 6.5 fusion.69
  175.8 3.3 multiply_reduce_fusion.14
  187.3 3.2 multiply_reduce_fusion.15
  207.2 3.3 fusion.1245
  215.0 5.2 fusion.34
  223.7 2.7 fusion.66
  226.4 3.3 multiply_reduce_fusion.12
  238.8 3.2 multiply_reduce_fusion.13
  246.2 2.7 fusion.189
  259.6 3.3 fusion.1247
  267.4 5.2 fusion.30
  275.9 2.7 fusion.63
  278.7 3.3 multiply_reduce_fusion.10
  291.1 3.2 multiply_reduce_fusion.11
  298.4 2.6 fusion.187
  312.2 3.3 fusion.1249
  320.0 5.2 fusion.26
  328.0 2.7 fusion.60
  330.8 3.3 multiply_reduce_fusion.8
  343.6 4.2 multiply_reduce_fusion.9
  348.0 6.6 fusion.118
  360.4 4.3 select_add_fusion.3
  370.3 3.3 select_add_fusion.4
  373.7 5.0 fusion.380
  381.0 3.5 fusion.376
  386.6 3.5 fusion.372
  390.1 3.8 fusion.831
  394.0 3.9 fusion.832
  397.9 10.5 select_add_fusion.2
  410.1 3.8 broadcast_in_dim.256
  414.5 2.9 fusion.117
  417.3 4.6 fusion.182
  422.0 4.6 fusion.183
  426.6 4.5 fusion.184
  431.1 11.2 fusion.553
  442.4 7.9 fusion.551
  450.3 7.9 fusion.549
  458.2 17.6 select_add_fusion
  476.7 9.3 fusion.1218
  486.1 8.2 fusion.1219
  494.3 8.2 fusion.1220
  502.5 18.3 select_add_fusion.1
  521.5 3.6 fusion.250
  537.6 11.9 fusion.294
  549.5 10.7 collective-permute-start.3
  567.0 143.7 %reduce-scatter.25.cloned.1.call-done = f32[16,3]{1,0:T(8,128)} async-done(((f32[1024,3]{1,0:T(8,128)}), f32[16,3]{1,0:T(8,128)}) %reduce-scatter.25.cloned.1.call-update) | async-done | bytes 208
  712.1 346.8 %reduce-scatter.27.cloned.1.call-done = f32[16,3]{1,0:T(8,128)} async-done(((f32[1024,3]{1,0:T(8,128)}), f32[16,3]{1,0:T(8,128)}) %reduce-scatter.27.cloned.1.call-update) | async-done | bytes 208
  1060.3 350.0 %reduce-scatter.19.cloned.1.call-done = f32[8,1024]{1,0:T(8,128)} async-done(((f32[512,1024]{1,0:T(8,128)}), f32[8,1024]{1,0:T(8,128)}) %reduce-scatter.19.cloned.1.call-update) | async-done | bytes 32784 | tf_op jit(solution)/shard_map/reduce_scatter | solution.py:302
  1410.3 351.3 %reduce-scatter.15.cloned.1.call-done = f32[16,512]{1,0:T(8,128)} async-done(((f32[1024,512]{1,0:T(8,128)}), f32[16,512]{1,0:T(8,128)}) %reduce-scatter.15.cloned.1.call-update) | async-done | bytes 32784 | tf_op jit(solution)/shard_map/reduce_scatter | solution.py:300
  1761.5 355.8 %reduce-scatter.17.cloned.1.call-done = f32[16,1024]{1,0:T(8,128)} async-done(((f32[1024,1024]{1,0:T(8,128)}), f32[16,1024]{1,0:T(8,128)}) %reduce-scatter.17.cloned.1.call-update) | async-done | bytes 65552 | tf_op jit(solution)/shard_map/reduce_scatter | solution.py:301
  2117.3 14.8 reduce-scatter.13.cloned.1.call-done
  2132.1 393.7 %reduce-scatter.23.cloned.1.call-done = f32[64,1024]{1,0:T(8,128)} async-done(((f32[4096,1024]{1,0:T(8,128)}), f32[64,1024]{1,0:T(8,128)}) %reduce-scatter.23.cloned.1.call-update) | async-done | bytes 262160 | tf_op jit(solution)/shard_map/reduce_scatter | solution.py:304
  2525.8 386.8 %reduce-scatter.21.cloned.1.call-done = f32[16,4096]{1,0:T(8,128)} async-done(((f32[1024,4096]{1,0:T(8,128)}), f32[16,4096]{1,0:T(8,128)}) %reduce-scatter.21.cloned.1.call-update) | async-done | bytes 262160 | tf_op jit(solution)/shard_map/reduce_scatter | solution.py:303
  (804 shorter events, 242.4 us)
Async XLA Ops:
  7.2 15.1 copy-start
  7.2 703.6 %reduce-scatter.25.cloned.1.call-start = ((), (), s32[]{:S(2)}) async-start(), calls=%async_computation.14 | async-start | bytes 532480
  10.3 57.4 %copy-start.117 = (f32[1,1,1024]{2,0,1:T(1,128)}, f32[1,1,1024]{2,0,1:T(1,128)S(1)}, u32[]{:S(2)}) copy-start(f32[1,1,1024]{2,0,1:T(1,128)S(1)} %get-tuple-element.264) | copy-start | bytes 12292
  11.0 56.7 %copy-start.203 = (f32[1,1,1024]{2,0,1:T(1,128)}, f32[1,1,1024]{2,0,1:T(1,128)S(1)}, u32[]{:S(2)}) copy-start(f32[1,1,1024]{2,0,1:T(1,128)S(1)} %get-tuple-element.267) | copy-start | bytes 12292
  17.3 42.0 %copy-start.179 = (f32[512]{0:T(512)}, f32[512]{0:T(512)S(1)}, u32[]{:S(2)}) copy-start(f32[512]{0:T(512)S(1)} %get-tuple-element.337) | copy-start | bytes 6148
  17.4 44.3 %copy-start.182 = (f32[512]{0:T(512)}, f32[512]{0:T(512)S(1)}, u32[]{:S(2)}) copy-start(f32[512]{0:T(512)S(1)} %get-tuple-element.338) | copy-start | bytes 6148
  17.4 50.3 %copy-start.186 = (f32[512]{0:T(512)}, f32[512]{0:T(512)S(1)}, u32[]{:S(2)}) copy-start(f32[512]{0:T(512)S(1)} %get-tuple-element.339) | copy-start | bytes 6148
  49.6 20.4 collective-permute-start
  50.7 17.0 copy-start.217
  89.6 14.3 copy-start.236
  89.6 14.8 copy-start.234
  89.6 15.4 copy-start.237
  89.6 15.9 copy-start.235
  89.6 17.0 copy-start.221
  101.5 5.6 collective-permute-start.1
  127.3 12.1 copy-start.118
  127.3 12.1 copy-start.129
  127.3 12.1 copy-start.165
  127.3 12.1 copy-start.204
  139.1 3.9 collective-permute-start.2
  160.3 15.5 slice-start
  163.8 15.3 copy-start.14
  163.8 15.3 copy-start.132
  164.0 15.1 copy-start.154
  164.1 11.7 slice-start.1
  204.7 17.3 collective-permute-start.4
  210.5 13.2 slice-start.8
  210.5 15.9 slice-start.2
  214.8 15.0 copy-start.16
  214.8 15.0 copy-start.134
  215.0 14.7 copy-start.156
  215.0 11.4 slice-start.3
  257.4 16.9 collective-permute-start.5
  262.9 13.1 slice-start.10
  262.9 15.8 slice-start.4
  267.1 14.9 copy-start.18
  267.1 14.9 copy-start.136
  267.4 14.7 copy-start.163
  267.4 11.3 slice-start.5
  310.0 17.0 collective-permute-start.6
  315.4 12.5 slice-start.12
  315.4 15.3 slice-start.6
  319.7 14.4 copy-start.20
  319.7 14.4 copy-start.189
  319.9 14.2 copy-start.208
  335.2 25.2 copy-start.46
  357.1 701.8 %reduce-scatter.27.cloned.1.call-start = ((), (), s32[]{:S(2)}) async-start(), calls=%async_computation.15 | async-start | bytes 532480
  360.3 1049.9 %reduce-scatter.19.cloned.1.call-start = ((), (), s32[]{:S(2)}) async-start(), calls=%async_computation.11 | async-start | bytes 2129920 | tf_op jit(solution)/shard_map/reduce_scatter | solution.py:302
  364.7 1396.8 %reduce-scatter.15.cloned.1.call-start = ((), (), s32[]{:S(2)}) async-start(), calls=%async_computation.9 | async-start | bytes 2129920 | tf_op jit(solution)/shard_map/reduce_scatter | solution.py:300
  373.6 1743.7 %reduce-scatter.17.cloned.1.call-start = ((), (), s32[]{:S(2)}) async-start(), calls=%async_computation.10 | async-start | bytes 4259840 | tf_op jit(solution)/shard_map/reduce_scatter | solution.py:301
  408.5 1723.6 %reduce-scatter.13.cloned.1.call-start = ((), (), s32[]{:S(2)}) async-start(), calls=%async_computation.8 | async-start | bytes 9437184 | tf_op jit(solution)/shard_map/reduce_scatter | solution.py:306
  431.1 2094.8 %reduce-scatter.23.cloned.1.call-start = ((), (), s32[]{:S(2)}) async-start(), calls=%async_computation.13 | async-start | bytes 17039360 | tf_op jit(solution)/shard_map/reduce_scatter | solution.py:304
  475.8 2436.8 %reduce-scatter.21.cloned.1.call-start = ((), (), s32[]{:S(2)}) async-start(), calls=%async_computation.12 | async-start | bytes 17039360 | tf_op jit(solution)/shard_map/reduce_scatter | solution.py:303
  537.6 22.6 copy-start.101
  537.6 23.6 copy-start.103
  537.6 25.5 copy-start.239
  537.6 25.5 copy-start.238
  537.6 26.2 copy-start.47
  537.6 26.2 copy-start.89
  537.6 26.2 copy-start.142
  537.6 26.2 copy-start.162
  549.5 12.6 collective-permute-start.3
  564.9 495.3 %collective-permute-start.7 = (f32[64,1024]{1,0:T(8,128)S(1)}, f32[64,1024]{1,0:T(8,128)S(1)}, u32[]{:S(2)}, u32[]{:S(2)}) collective-permute-start(f32[64,1024]{1,0:T(8,128)S(1)} %multiply_add_fusion), channel_id=1, source_target_pairs={{64,0},{0,64},{65,1},{1,65},{66,2},{2,66},{67,3},{3,67},{68,4},{4,... | collective-permute-start | bytes 786440 | tf_op jit(solution)/shard_map/ppermute | solution.py:19
  1060.3 1852.4 %copy-start.116 = (f32[3,1,64,512]{3,2,1,0:T(8,128)}, f32[3,1,64,512]{3,2,1,0:T(8,128)S(1)}, u32[]{:S(2)}) copy-start(f32[3,1,64,512]{3,2,1,0:T(8,128)S(1)} %fusion.834) | copy-start | bytes 1179652
  (210 other events, 815.4 us)
Sparse Core Ops, SparseCore 0:
  357.2 353.4 reduce-scatter.24
  713.2 345.6 reduce-scatter.26
  1061.9 348.3 reduce-scatter.18
  1413.2 348.3 reduce-scatter.14
  1764.3 352.9 reduce-scatter.16
  2120.2 11.8 reduce-scatter.12
  2135.1 390.6 reduce-scatter.22
  2528.8 383.8 reduce-scatter.20
where the time goes:
time: 2930 us; the launch traced here: 2920 us
  waiting for transfers between devices  2340 us (80%)
  matrix products  379 us (13%)
  other arithmetic  90.5 us (3%)
  local copies, waits for them, and re-layouts  76.2 us (3%)
    unnamed x10, waiting for transfers between devices  491 us
    reduce_scatter x1, waiting for transfers between devices, body(): lax.psum_scatter(totals[6], 'dp', scatter_dimension=0, tiled=True)  394 us
    reduce_scatter x1, waiting for transfers between devices, body(): lax.psum_scatter(totals[5], 'dp', scatter_dimension=0, tiled=True)  387 us
    reduce_scatter x1, waiting for transfers between devices, body(): lax.psum_scatter(totals[3], 'dp', scatter_dimension=0, tiled=True)  356 us
    reduce_scatter x1, waiting for transfers between devices, body(): lax.psum_scatter(totals[2], 'dp', scatter_dimension=0, tiled=True)  351 us
    reduce_scatter x1, waiting for transfers between devices, body(): lax.psum_scatter(totals[4], 'dp', scatter_dimension=0, tiled=True)  350 us
    dot_general x24, matrix products, cross_rows(): lax.dot_general(left, right, (((0,), (0,)), ((), ())), preferred_element_...  140 us
    dot_general x40, matrix products, matmul(): return jnp.dot(left, right, preferred_element_type=jnp.float32)  125 us
  transfers between devices with their start and end apart: 16, of which 8 were waited for; matrix products, arithmetic and copies ran while one was open for 9% of the time, Pallas kernels for 0%

commit v1 on v0

--- a/solution.py
+++ b/solution.py
@@ -1,6 +1,8 @@
 import jax
 import jax.numpy as jnp
 from jax import lax
+from jax.experimental import pallas as pl
+from jax.experimental.pallas import tpu as pltpu
 from jax.sharding import PartitionSpec as P
 
 HEADS = 8
@@ -145,15 +147,12 @@
     key_count = key_heads.shape[0]
     slot_count = media_in.shape[0]
     grad_out = grad_y.astype(jnp.bfloat16)
-    w_down_term = cross_rows(activated, grad_out)
     grad_pre = (against_rows(grad_out, w_down) * gelu_slope(pre_act)).astype(jnp.bfloat16)
-    w_up_term = cross_rows(ff_in, grad_pre)
     grad_ffn, ff_gain_term, ff_bias_term = norm_back(
         against_rows(grad_pre, w_up), ff_normed, ff_inverse, norm_gains[2]
     )
     grad_mixed = grad_y + grad_ffn
     grad_attn = grad_mixed.astype(jnp.bfloat16)
-    w_out_term = cross_rows(attended, grad_attn)
     grad_att = (
         against_rows(grad_attn, w_out)
         .astype(jnp.bfloat16)
@@ -179,8 +178,6 @@
     ).astype(jnp.bfloat16)
     grad_media_kv = grad_keyvals[:slot_count]
     grad_latent_kv = grad_keyvals[slot_count:]
-    w_keyval_term = cross_rows(media_in, grad_media_kv) + cross_rows(latent_in, grad_latent_kv)
-    w_query_term = cross_rows(latent_in, grad_queries) * score_scale
     grad_media_in = against_rows(grad_media_kv, w_keyval)
     grad_latent_in = against_rows(grad_queries, w_query) * score_scale + against_rows(
         grad_latent_kv, w_keyval
@@ -197,8 +194,188 @@
     return (
         grad_input,
         grad_media,
-        (gain_terms, bias_terms, w_query_term, w_keyval_term, w_out_term, w_up_term, w_down_term),
-    )
+        (ff_in, activated, attended, media_in, latent_in, grad_out, grad_pre, grad_attn, grad_queries, grad_keyvals, gain_terms, bias_terms),
+    )
+
+
+MESH = pl.DeviceIdType.MESH
+CHUNKS = 41
+GROUPS = 14
+TICKS = GROUPS + 6
+ROWS = (256, 64, 16)
+COLS = 256
+
+
+def chunk_plan(c):
+    left = jnp.where(c < 16, c // 4, jnp.where(c < 32, 4, jnp.where(c < 34, 5, jnp.where(c < 35, 7, jnp.where(c < 37, 14, 8)))))
+    right = jnp.where(c < 16, c % 4, jnp.where(c < 32, c - 12, jnp.where(c < 34, 20 + 2 * (c - 32), jnp.where(c < 35, 24, jnp.where(c < 37, c - 10, 27 + 7 * (c - 37))))))
+    steps = jnp.where(c < 32, 1, jnp.where(c < 34, 2, jnp.where(c < 37, 1, 7)))
+    return left, right, steps
+
+
+def shard_kernel(left_ref, right_ref, out_ref, own1, own2, own3, a1, a2, a3, b1, b2, b3, send_sem, recv_sem):
+    me = lax.axis_index("dp")
+    coords = (me // 16, (me // 4) % 4, me % 4)
+    strides = (16, 4, 1)
+
+    def at(axis, shift):
+        return (coords[axis] + shift) % 4
+
+    def neighbour(axis, shift):
+        return me + (at(axis, shift) - coords[axis]) * strides[axis]
+
+    barrier = pltpu.get_barrier_semaphore()
+    for axis in range(3):
+        for shift in (1, 3):
+            pl.semaphore_signal(barrier, inc=1, device_id={"dp": neighbour(axis, shift)}, device_id_type=MESH)
+    pl.semaphore_wait(barrier, 6)
+
+    own = (own1, own2, own3)
+    got_a = (a1, a2, a3)
+    got_b = (b1, b2, b3)
+
+    def copy(order, stage, step, way, group, tick):
+        axis = (order + stage) % 3
+        half = ROWS[stage] // 2
+        place = own[stage].at[order, group % 3]
+        turn = tick % 2
+        sem = (((order * 3 + stage) * 2 + step) * 2 + way) * 2 + turn
+        shift = 1 if way == 0 else 3
+        if step == 0:
+            source = place.at[at(axis, 2), pl.ds(way * half, half)]
+            target = got_a[stage].at[order, way, turn]
+        else:
+            source = place.at[at(axis, shift)]
+            target = got_b[stage].at[order, way, turn]
+        return pltpu.make_async_remote_copy(
+            src_ref=source,
+            dst_ref=target,
+            send_sem=send_sem.at[sem],
+            recv_sem=recv_sem.at[sem],
+            device_id={"dp": neighbour(axis, shift)},
+            device_id_type=MESH,
+        )
+
+    def terms(order, group):
+        chunk = 3 * group + order
+        left, right, steps = chunk_plan(chunk)
+        slot = group % 3
+
+        def place(step, first):
+            for i in range(4):
+                block = jnp.dot(
+                    left_ref[left + step, pl.ds(256 * i, 256), :], right_ref[right + step], preferred_element_type=jnp.float32
+                )
+                for j in range(4):
+                    for k in range(4):
+                        spot = ((i, j, k), (j, k, i), (k, i, j))[order]
+                        rows = pl.ds((spot[1] * 4 + spot[2]) * 16, 16)
+                        part = block[(j * 4 + k) * 16 : (j * 4 + k) * 16 + 16]
+                        if first:
+                            own1[order, slot, spot[0], rows, :] = part
+                        else:
+                            own1[order, slot, spot[0], rows, :] += part
+
+        place(0, True)
+
+        def more(step, carry):
+            place(step, False)
+            return carry
+
+        lax.fori_loop(1, steps, more, 0)
+
+    def valid(order, group):
+        return (group >= 0) & (group * 3 + order < CHUNKS)
+
+    def tick(t, carry):
+        for order in range(3):
+
+            @pl.when(valid(order, t))
+            def _():
+                terms(order, t)
+
+        for stage in range(3):
+            for order in range(3):
+                axis = (order + stage) % 3
+                half = ROWS[stage] // 2
+                turn = (t - 1) % 2
+                group_a = t - 1 - 2 * stage
+
+                @pl.when(valid(order, group_a))
+                def _():
+                    for way in range(2):
+                        done = copy(order, stage, 0, way, group_a, t - 1)
+                        done.wait()
+                        spot = at(axis, 1 if way == 0 else 3)
+                        own[stage][order, group_a % 3, spot, pl.ds(way * half, half), :] += got_a[stage][order, way, turn]
+
+                group_b = t - 2 - 2 * stage
+
+                @pl.when(valid(order, group_b))
+                def _():
+                    for way in range(2):
+                        done = copy(order, stage, 1, way, group_b, t - 1)
+                        done.wait()
+                    total = (
+                        own[stage][order, group_b % 3, at(axis, 0)]
+                        + got_b[stage][order, 0, turn]
+                        + got_b[stage][order, 1, turn]
+                    )
+                    if stage < 2:
+                        own[stage + 1][order, group_b % 3] = total.reshape(4, ROWS[stage + 1], COLS)
+                    else:
+                        out_ref[group_b * 3 + order] = total
+
+        for stage in range(3):
+            for order in range(3):
+                group_a = t - 2 * stage
+                group_b = t - 1 - 2 * stage
+
+                @pl.when(valid(order, group_a))
+                def _():
+                    for way in range(2):
+                        copy(order, stage, 0, way, group_a, t).start()
+
+                @pl.when(valid(order, group_b))
+                def _():
+                    for way in range(2):
+                        copy(order, stage, 1, way, group_b, t).start()
+
+        return carry
+
+    lax.fori_loop(0, TICKS, tick, 0)
+
+
+def scattered_terms(left, right):
+    vmem = pl.BlockSpec(memory_space=pltpu.VMEM)
+    f32 = jnp.float32
+    return pl.pallas_call(
+        shard_kernel,
+        out_shape=jax.ShapeDtypeStruct((CHUNKS, 16, COLS), f32),
+        in_specs=[vmem, vmem],
+        out_specs=vmem,
+        scratch_shapes=[pltpu.VMEM((3, 3, 4, r, COLS), f32) for r in ROWS]
+        + [pltpu.VMEM((3, 2, 2, r // 2, COLS), f32) for r in ROWS]
+        + [pltpu.VMEM((3, 2, 2, r, COLS), f32) for r in ROWS]
+        + [pltpu.SemaphoreType.DMA((72,)), pltpu.SemaphoreType.DMA((72,))],
+        compiler_params=pltpu.CompilerParams(collective_id=1, has_side_effects=True, vmem_limit_bytes=50 * 2**20),
+        name="scatter_terms",
+    )(left, right)
+
+
+def rows_deep(block):
+    rows = block.shape[0]
+    full = -(-rows // 256) * 256
+    return jnp.pad(block, ((0, full - rows), (0, 0))).reshape(full // 256, 256, block.shape[1])
+
+
+def column_blocks(block):
+    deep = rows_deep(block)[0]
+    return deep.reshape(256, -1, 256).transpose(1, 0, 2)
+
+
+def flat_rows(block):
+    return block.reshape(-1, block.shape[-1])
 
 
 def body(
@@ -207,114 +384,94 @@
     section_index = lax.axis_index("section")
     micro_count = media.shape[0]
     slot_count = media.shape[2]
-    model_width = media.shape[3]
+    half_width = media.shape[3] // 2
     latent_rows = latents_in.shape[2]
-    half_width = model_width // 2
-    head_count = HEADS
     norm_gains = gains[0]
     norm_biases = biases[0]
     weights = (w_query[0], w_keyval[0], w_out[0], w_up[0], w_down[0])
     frame_of_slot = jnp.arange(slot_count) // PATCHES
-
-    def key_mask(micro_index):
-        frames_real = lax.dynamic_index_in_dim(frame_count, micro_index, 0, keepdims=False)[0]
-        return jnp.concatenate([frame_of_slot < frames_real, jnp.ones((latent_rows,), dtype=bool)])
-
-    def media_of(micro_index):
-        return lax.dynamic_index_in_dim(media, micro_index, 0, keepdims=False)[0]
-
-    received = jnp.zeros((latent_rows, model_width), jnp.float32)
-    section_inputs = jnp.zeros((micro_count, latent_rows, model_width), jnp.float32)
-    resampled = jnp.zeros((micro_count, latent_rows, half_width), jnp.float32)
-    for moment in range(micro_count + 1):
-        micro_index = jnp.clip(moment - section_index, 0, micro_count - 1)
-        given_latents = lax.dynamic_index_in_dim(latents_in, micro_index, 0, keepdims=False)[
-            0
-        ].astype(jnp.float32)
-        layer_input = jnp.where(section_index == 0, given_latents, received)
-        section_inputs = lax.dynamic_update_index_in_dim(
-            section_inputs, layer_input, micro_index, 0
-        )
-        layer_out, unused_state = layer_forward(
-            layer_input,
-            media_of(micro_index),
-            key_mask(micro_index),
-            norm_gains,
-            norm_biases,
-            weights,
-            head_count,
-        )
-        received = passed_along(layer_out, "section", 1)
-        if moment > 0:
-            complete = jnp.where(section_index == 1, layer_out, received)
-            resampled = resampled.at[moment - 1].set(
-                lax.dynamic_slice_in_dim(complete, section_index * half_width, half_width, 1)
-            )
-    received = jnp.zeros((latent_rows, model_width), jnp.float32)
-    latents_grad = jnp.zeros((micro_count, latent_rows, half_width), jnp.float32)
-    media_terms = jnp.zeros((micro_count, slot_count, model_width), jnp.float32)
-    totals = (
-        jnp.zeros(gains.shape[1:], jnp.float32),
-        jnp.zeros(biases.shape[1:], jnp.float32),
-        jnp.zeros(w_query.shape[1:], jnp.float32),
-        jnp.zeros(w_keyval.shape[1:], jnp.float32),
-        jnp.zeros(w_out.shape[1:], jnp.float32),
-        jnp.zeros(w_up.shape[1:], jnp.float32),
-        jnp.zeros(w_down.shape[1:], jnp.float32),
-    )
-    for moment in range(micro_count + 1):
-        position = moment - 1 + section_index
-        is_valid = (position >= 0) & (position < micro_count)
-        micro_index = jnp.clip(position, 0, micro_count - 1)
-        given_grad = lax.dynamic_index_in_dim(cotangent, micro_index, 0, keepdims=False)[0].astype(
-            jnp.float32
-        )
-        grad_y = jnp.where(section_index == 1, given_grad, received)
-        layer_input = lax.dynamic_index_in_dim(section_inputs, micro_index, 0, keepdims=False)
-        layer_out, kept_state = layer_forward(
-            layer_input,
-            media_of(micro_index),
-            key_mask(micro_index),
-            norm_gains,
-            norm_biases,
-            weights,
-            head_count,
-        )
-        grad_input, grad_media, grad_terms = layer_backward(
-            grad_y, kept_state, norm_gains, weights, head_count
-        )
-        received = passed_along(grad_input, "section", 1)
-        if moment > 0:
-            complete = jnp.where(section_index == 0, grad_input, received)
-            latents_grad = latents_grad.at[moment - 1].set(
-                lax.dynamic_slice_in_dim(complete, section_index * half_width, half_width, 1)
-            )
-        media_terms = media_terms.at[micro_index].add(jnp.where(is_valid, grad_media, 0.0))
-        grad_terms = tuple((jnp.where(is_valid, term, 0.0) for term in grad_terms))
-        totals = tuple(
-            (left_term + right_term for left_term, right_term in zip(totals, grad_terms))
-        )
-    shards = (
-        lax.psum_scatter(totals[0], "dp", scatter_dimension=1, tiled=True),
-        lax.psum_scatter(totals[1], "dp", scatter_dimension=1, tiled=True),
-        lax.psum_scatter(totals[2], "dp", scatter_dimension=0, tiled=True),
-        lax.psum_scatter(totals[3], "dp", scatter_dimension=0, tiled=True),
-        lax.psum_scatter(totals[4], "dp", scatter_dimension=0, tiled=True),
-        lax.psum_scatter(totals[5], "dp", scatter_dimension=0, tiled=True),
-        lax.psum_scatter(totals[6], "dp", scatter_dimension=0, tiled=True),
-    )
-    media_grad = lax.psum_scatter(media_terms, "section", scatter_dimension=2, tiled=True)
+    key_valid = jnp.concatenate(
+        [frame_of_slot[None] < frame_count, jnp.ones((micro_count, latent_rows), dtype=bool)], 1
+    )
+
+    def forward(x):
+        return jax.vmap(
+            lambda a, b, c: layer_forward(a, b, c, norm_gains, norm_biases, weights, HEADS)
+        )(x, media[:, 0], key_valid)
+
+    given = latents_in[:, 0].astype(jnp.float32)
+    first, unused_state = forward(given)
+    x = jnp.where(section_index == 0, given, passed_along(first, "section", 1))
+    y, state = forward(x)
+    complete = jnp.where(section_index == 1, y, passed_along(y, "section", 1))
+    resampled = lax.dynamic_slice_in_dim(complete, section_index * half_width, half_width, 2)
+
+    def backward(g):
+        return jax.vmap(lambda a, b: layer_backward(a, b, norm_gains, weights, HEADS))(g, state)
+
+    given_grad = cotangent[:, 0].astype(jnp.float32)
+    first_grad = backward(given_grad)[0]
+    grad_y = jnp.where(section_index == 1, given_grad, passed_along(first_grad, "section", 1))
+    grad_x, grad_media, terms = backward(grad_y)
+    complete = jnp.where(section_index == 0, grad_x, passed_along(grad_x, "section", 1))
+    latents_grad = lax.dynamic_slice_in_dim(complete, section_index * half_width, half_width, 2)
+    ff_in, activated, attended, media_in, latent_in, grad_out, grad_pre, grad_attn, grad_queries, grad_keyvals = [
+        flat_rows(t) for t in terms[:10]
+    ]
+    grad_media_kv = flat_rows(terms[9][:, :slot_count])
+    grad_latent_kv = flat_rows(terms[9][:, slot_count:])
+    gain_terms, bias_terms = jnp.sum(terms[10], 0), jnp.sum(terms[11], 0)
+
+    def deep_left(block):
+        return rows_deep(block).transpose(0, 2, 1)
+
+    low_columns = jnp.concatenate([gain_terms, bias_terms], 0)
+    high = low_columns.astype(jnp.bfloat16)
+    low = (low_columns - high.astype(jnp.float32)).astype(jnp.bfloat16)
+    act_left = deep_left(activated)[0].reshape(64, 4, 16, 256).transpose(1, 0, 2, 3).reshape(4, 1024, 256)
+    att_left = deep_left(attended)[0].reshape(64, 8, 256)
+    none = jnp.zeros_like(att_left)
+    left = jnp.concatenate(
+        [
+            act_left,
+            deep_left(ff_in),
+            jnp.concatenate([att_left, none], 1).reshape(1, 1024, 256),
+            jnp.concatenate([none, att_left], 1).reshape(1, 1024, 256),
+            deep_left(jnp.concatenate([high, low], 0)),
+            deep_left(media_in),
+            deep_left(latent_in),
+        ],
+        0,
+    )
+    eye = (jnp.arange(256)[:, None] % 6 == jnp.arange(256)[None, :]) & (jnp.arange(256)[:, None] < 12)
+    right = jnp.concatenate(
+        [
+            column_blocks(grad_out),
+            column_blocks(grad_pre),
+            column_blocks(grad_attn),
+            eye.astype(jnp.bfloat16)[None],
+            column_blocks(grad_queries),
+            jnp.concatenate([rows_deep(grad_media_kv), rows_deep(grad_latent_kv)], 0)
+            .reshape(7, 256, 4, 256)
+            .transpose(2, 0, 1, 3)
+            .reshape(28, 256, 256),
+        ],
+        0,
+    )
+    got = scattered_terms(left, right)
+    media_grad = lax.psum_scatter(grad_media, "section", scatter_dimension=2, tiled=True)
+    small = got[34, :, :6].T
     return (
         resampled[:, None],
         latents_grad[:, None],
         media_grad[:, None],
-        shards[0][None],
-        shards[1][None],
-        shards[2][None],
-        shards[3][None],
-        shards[4][None],
-        shards[5][None],
-        shards[6][None],
+        small[None, :3],
+        small[None, 3:],
+        got[35:37].transpose(1, 0, 2).reshape(1, 16, 512) * 0.125,
+        got[37:41].transpose(1, 0, 2).reshape(1, 16, 1024),
+        got[32:34].reshape(2, 2, 8, 256).transpose(2, 0, 1, 3).reshape(1, 8, 1024),
+        got[16:32].transpose(1, 0, 2).reshape(1, 16, 4096),
+        got[0:16].reshape(4, 4, 16, 256).transpose(0, 2, 1, 3).reshape(1, 64, 1024),
     )
 
 

time: 2930 us -> 516 us (0.18)
  waiting for transfers between devices: 2340 us -> 4.66 us
  matrix products: 379 us -> 106 us
  Pallas kernels: 0 us -> 202 us
  local copies, waits for them, and re-layouts: 76.2 us -> 122 us
  other arithmetic: 90.5 us -> 56.9 us
    reduce_scatter x6 -> x1, waiting for transfers between devices: 1850 us -> 0.01 us  [body(): lax.psum_scatter(grad_media, 'section', scatter_dimension=2, tiled=True)]
    unnamed x10 -> x1, waiting for transfers between devices: 491 us -> 0.02 us
    pallas_call x0 -> x1, Pallas kernels: none -> 202 us  [scattered_terms(): pl.pallas_call(shard_kernel, out_shape=jax.ShapeDtypeStruct((CHUNKS, 16,...]
    dot_general x24 -> x1, matrix products: 140 us -> 2.19 us  [layer_forward(): jnp.einsum('lhe,khe->hlk', query_heads, key_heads, preferred_element_type...]
    dot_general x40 -> x11, matrix products: 125 us -> 34.8 us  [matmul(): return jnp.dot(left, right, preferred_element_type=jnp.float32)]
    reshape x0 -> x14, local copies, waits for them, and re-layouts: none -> 31.7 us  [the longest x7 13.5 us: flat_rows(): return block.reshape(-1, block.shape[-1])]
    dot_general x24 -> x10, matrix products: 61.1 us -> 40.5 us  [against_rows(): lax.dot_general(left, right, (((1,), (1,)), ((), ())), preferred_element_...]
  transfers between devices with their start and end apart: 16 -> 5, of which waited for: 8 -> 2; matrix products, arithmetic and copies ran while one was open for 9% -> 21% of each run, Pallas kernels for 0% -> 40%
where the time goes in v1:
time: 516 us; the launch traced here: 509 us
  Pallas kernels  202 us (39%)
  local copies, waits for them, and re-layouts  122 us (24%)
  matrix products  106 us (21%)
  other arithmetic  56.9 us (11%)
  between operations  15.5 us (3%)
    pallas_call x1, Pallas kernels, scattered_terms(): pl.pallas_call(shard_kernel, out_shape=jax.ShapeDtypeStruct((CHUNKS, 16,...  202 us
    dot_general x10, matrix products, against_rows(): lax.dot_general(left, right, (((1,), (1,)), ((), ())), preferred_element_...  40.5 us
    dot_general x11, matrix products, matmul(): return jnp.dot(left, right, preferred_element_type=jnp.float32)  34.8 us
    unnamed x179, local copies, waits for them, and re-layouts  23.5 us
    reshape x7, local copies, waits for them, and re-layouts, flat_rows(): return block.reshape(-1, block.shape[-1])  13.5 us
  transfers between devices with their start and end apart: 5, of which 2 were waited for; matrix products, arithmetic and copies ran while one was open for 21% of the time, Pallas kernels for 40%

profile of v1, /device:TPU:0, one launch (start us, length us, event | category | flops | bytes accessed | tf_op | source)
XLA Modules:
  0.0 508.7 jit_solution(7720685145880844175)
XLA Ops:
  7.8 1.7 fusion.247
  12.7 2.4 convert_reduce_fusion
  16.9 3.8 fusion.69
  20.7 2.8 pad_maximum_fusion.3
  23.5 4.0 copy.206
  27.5 3.9 copy.207
  31.4 1.8 fusion.151
  34.5 2.2 fusion.182
  36.8 1.8 fusion.248
  41.3 2.8 fusion.169
  44.2 8.4 %fusion.134 = f32[3,64,1024]{2,1,0:T(8,128)S(1)} fusion(f32[3,64,1024]{2,1,0:T(8,128)S(1)} %get-tuple-element.105, bf16[1,4096,1024]{2,1,0:T(8,128)(2,1)S(1)} %bitcast.419, f32[3,64,4096]{2,1,0:T(8,128)S(1)} %get-tuple-element.106, u8[64,4096]{1,0:T(8,128)(4,1)S(1)} %get-tuple-element.67, u8[64,4096]{1,0:T(8,128)(4,1)S(1)} %get-tuple-element.66), kind=kOutput, calls=%fused_computation.172 | convolution fusion | flops 1665859584 | bytes 13631488 | tf_op jit(solution)/shard_map/vmap()/dot_general | solution.py:25
  52.8 2.4 collective-permute-done
  57.4 2.7 pad_maximum_fusion.2
  60.1 3.9 copy.210
  64.2 3.9 copy.211
  68.1 4.7 fusion.250
  72.8 3.6 convolution_convert_fusion.6
  78.1 8.6 %fusion.170 = (u8[64,4096]{1,0:T(8,128)(4,1)}, u8[64,4096]{1,0:T(8,128)(4,1)}, f32[3,64,4096]{2,1,0:T(8,128)}) fusion(bf16[3,64,1024]{2,1,0:T(8,128)(2,1)S(1)} %add_convert_fusion.2, bf16[1,1024,4096]{2,1,0:T(8,128)(2,1)} %param.19), kind=kOutput, calls=%fused_computation.225 | convolution fusion | flops 1620312064 | bytes 12451840 | tf_op jit(solution)/shard_map/vmap()/dot_general | solution.py:25
  86.7 11.9 %fusion.239 = (f32[3,64]{1,0:T(4,128)S(1)}, f32[3,64]{1,0:T(4,128)S(1)}, f32[3,64,1024]{2,1,0:T(8,128)}) fusion(f32[3,64]{1,0:T(4,128)S(1)} %add_rsqrt_fusion.1, f32[3,64,1024]{2,1,0:T(8,128)} %copy-done.7, f32[3,64]{1,0:T(4,128)S(1)} %broadcast_multiply_fusion.11, f32[1024]{0:T(1024)S(1)} %bitcast.399, bf16[1,1024,4096]{2,1,0:T(8,128)(2,1)} %param.19, ...), kind=kOutput, calls=%fused_computation.344 | convolution fusion | flops 3230268928 | bytes 21896192 | tf_op jit(solution)/shard_map/vmap()/dot_general | solution.py:35
  98.7 2.4 convolution_convert_fusion.8
  102.0 3.9 multiply_reduce_fusion.5
  106.0 2.0 convolution_convert_fusion.2
  110.3 2.0 convolution_convert_fusion.3
  112.4 1.6 convolution_multiply_fusion.1
  114.0 3.9 copy.219
  117.9 3.9 copy.218
  121.7 2.4 fusion.238
  127.0 2.3 collective-permute-done.2
  131.3 6.3 %fusion.25 = bf16[3,64,4096]{2,1,0:T(8,128)(2,1)S(1)} fusion(bf16[3,64,1024]{2,1,0:T(8,128)(2,1)S(1)} %fusion.173, bf16[1,4096,1024]{2,1,0:T(8,128)(2,1)} %param.20, f32[3,64,4096]{2,1,0:T(8,128)} %get-tuple-element.111), kind=kOutput, calls=%fused_computation.30 | convolution fusion | flops 1618477056 | bytes 13500416 | tf_op jit(solution)/shard_map/vmap()/dot_general | solution.py:35
  137.7 7.7 %multiply_reduce_fusion.6 = (f32[3,1024]{1,0:T(4,128)}, f32[3,64]{1,0:T(4,128)S(1)}, f32[3,64]{1,0:T(4,128)S(1)}, f32[3,1024]{1,0:T(4,128)}, f32[3,64,1024]{2,1,0:T(8,128)S(1)}) fusion(f32[3,64]{1,0:T(4,128)S(1)} %add_rsqrt_fusion.1, f32[3,64,1024]{2,1,0:T(8,128)S(1)} %copy-done.9, f32[3,64]{1,0:T(4,128)S(1)} %broadcast_multiply_fusion.11, ...), kind=kOutput, calls=%fused_computation.207 | convolution fusion | flops 1612375552 | bytes 11566080 | tf_op jit(solution)/shard_map/vmap()/dot_general | solution.py:35
  145.4 2.4 fusion.240
  150.0 5.7 %multiply_reduce_fusion.4 = (f32[3,8,64]{2,1,0:T(8,128)S(1)}, f32[3,8,64,576]{3,2,1,0:T(8,128)}) fusion(f32[3,8,64,576]{3,2,1,0:T(8,128)} %get-tuple-element.108, f32[3,8,64]{2,1,0:T(8,128)S(1)} %get-tuple-element.107, bf16[3,64,8,64]{1,3,2,0:T(8,128)(2,1)} %bitcast.380, bf16[3,576,8,64]{1,3,2,0:T(8,128)(2,1)} %bitcast.367), kind=kOutput, calls=%fused_computation.36 | convolution fusion | flops 115898880 | bytes 9056256 | tf_op jit(solution)/shard_map/vmap(lhe,khe->hlk)/dot_general | solution.py:161
  155.7 2.0 convolution_convert_fusion
  157.7 3.9 copy.225
  161.6 3.7 multiply_convert_fusion
  166.6 1.9 convolution_convert_fusion.1
  168.5 4.3 copy.224
  172.8 2.4 pad_maximum_fusion.1
  175.6 5.8 %multiply_reduce_fusion = (f32[3,1024]{1,0:T(4,128)}, f32[3,512]{1,0:T(4,128)S(1)}, f32[3,512]{1,0:T(4,128)S(1)}, f32[3,1024]{1,0:T(4,128)}, f32[3,512,1024]{2,1,0:T(8,128)S(1)}) fusion(bf16[3,1,512,1024]{3,2,1,0:T(8,128)(2,1)S(1)} %copy-done.2, f32[3,512]{1,0:T(4,128)S(1)} %copy-done.55, f32[3,512]{1,0:T(4,128)S(1)} %broadcast_multiply_fusion.2, ...), kind=kOutput, calls=%fused_computation.20 | convolution fusion | flops 3236944896 | bytes 14733312 | tf_op jit(solution)/shard_map/vmap()/dot_general | solution.py:35
  181.5 3.6 subtract_multiply_fusion
  186.3 5.3 %bitcast_convert_fusion = f32[3,1,512,1024]{3,2,0,1:T(8,128)} fusion(bf16[3,1,512,1024]{3,2,1,0:T(8,128)(2,1)} %param.12), kind=kLoop, calls=%fused_computation.75 | loop fusion | flops 1572864 | bytes 9437184 | tf_op jit(solution)/shard_map/vmap()/convert_element_type | solution.py:70
  191.6 6.8 %copy.232 = f32[6,256,1024]{1,2,0:T(8,128)} copy(f32[6,256,1024]{2,1,0:T(8,128)} %bitcast.343) | data formatting | bytes 12582912 | tf_op jit(solution)/shard_map/vmap()/convert_element_type | solution.py:70
  198.5 8.5 %fusion.42 = bf16[3,64,4096]{2,1,0:T(8,128)(2,1)S(1)} fusion(f32[3,64,4096]{2,1,0:T(8,128)} %get-tuple-element.111, u8[64,4096]{1,0:T(8,128)(4,1)S(1)} %copy-done.51, u8[64,4096]{1,0:T(8,128)(4,1)S(1)} %copy-done.50), kind=kLoop, calls=%fused_computation.55 | loop fusion | flops 55050240 | bytes 5242880 | tf_op jit(solution)/shard_map/vmap()/convert_element_type | solution.py:98
  207.0 6.7 %fusion.139 = f32[3,64,1024]{2,1,0:T(8,128)} fusion(f32[3,64,1024]{2,1,0:T(8,128)S(1)} %copy-done.10, bf16[3,64,4096]{2,1,0:T(8,128)(2,1)S(1)} %fusion.42, bf16[1,4096,1024]{2,1,0:T(8,128)(2,1)} %param.20), kind=kOutput, calls=%fused_computation.173 | convolution fusion | flops 1610809344 | bytes 11534336 | tf_op jit(solution)/shard_map/vmap()/dot_general | solution.py:25
  213.8 4.0 copy.226
  217.8 1.9 pad.37
  219.7 1.5 copy.227
  221.3 2.0 copy.228
  223.3 2.0 copy.229
  229.4 3.1 constant_dynamic-update-slice_fusion
  235.1 6.2 %concatenate.55 = bf16[6,256,4,256]{3,2,1,0:T(4,128)(2,1)} reshape(bf16[3,512,1024]{2,1,0:T(8,128)(2,1)} %copy-done.18) | data formatting | bytes 6291456 | tf_op jit(solution)/shard_map/concatenate | solution.py:454
  251.8 2.0 copy.235
  253.8 4.1 copy.236
  257.8 3.2 pad.43
  261.1 4.0 copy.237
  266.0 1.9 pad.44
  268.0 2.0 copy.239
  271.2 1.5 reshape.438
  276.0 2.5 copy.244
  279.4 4.7 fusion.51
  287.8 3.0 copy-done.24
  290.8 201.8 %scatter_terms.1 = f32[41,16,256]{2,1,0:T(8,128)S(1)} custom-call(bf16[15,1024,256]{2,1,0:T(8,128)(2,1)} %bitcast_dynamic-update-slice_fusion.1.left_ref, bf16[55,256,256]{2,1,0:T(8,128)(2,1)} %copy-done.24), custom_call_target="tpu_custom_call" | custom-call | tf_op jit(solution)/shard_map/scatter_terms/pallas_call | solution.py:352
  497.8 1.9 fusion.179
  499.7 1.9 fusion.177
  (280 shorter events, 58.9 us)
Async XLA Ops:
  7.2 9.1 %copy-start = (bf16[1,1024,1024]{2,1,0:T(8,128)(2,1)S(1)}, bf16[1,1024,1024]{2,1,0:T(8,128)(2,1)}, u32[]{:S(2)}) copy-start(bf16[1,1024,1024]{2,1,0:T(8,128)(2,1)} %param.17) | copy-start | bytes 6291460
  7.2 494.5 %reduce-scatter.2.cloned.1.call-start = ((), (), s32[]{:S(2)}) async-start(), calls=%async_computation.1 | async-start | bytes 9437184 | tf_op jit(solution)/shard_map/reduce_scatter | solution.py:462
  7.2 7.9 %copy-start.1 = (bf16[3,1,512,1024]{3,2,1,0:T(8,128)(2,1)S(1)}, bf16[3,1,512,1024]{3,2,1,0:T(8,128)(2,1)}, u32[]{:S(2)}) copy-start(bf16[3,1,512,1024]{3,2,1,0:T(8,128)(2,1)} %param.12) | copy-start | bytes 9437188
  9.6 6.6 %copy-start.69 = (f32[1,1,1024]{2,0,1:T(1,128)}, f32[1,1,1024]{2,0,1:T(1,128)S(1)}, u32[]{:S(2)}) copy-start(f32[1,1,1024]{2,0,1:T(1,128)S(1)} %get-tuple-element.99) | copy-start | bytes 12292
  9.6 7.3 %copy-start.65 = (f32[1,1,1024]{2,0,1:T(1,128)}, f32[1,1,1024]{2,0,1:T(1,128)S(1)}, u32[]{:S(2)}) copy-start(f32[1,1,1024]{2,0,1:T(1,128)S(1)} %get-tuple-element.98) | copy-start | bytes 12292
  10.3 6.6 %copy-start.56 = (f32[1,1,1024]{2,0,1:T(1,128)}, f32[1,1,1024]{2,0,1:T(1,128)S(1)}, u32[]{:S(2)}) copy-start(f32[1,1,1024]{2,0,1:T(1,128)S(1)} %get-tuple-element.95) | copy-start | bytes 12292
  10.3 30.3 %copy-start.59 = (f32[1,1,1024]{2,0,1:T(1,128)}, f32[1,1,1024]{2,0,1:T(1,128)S(1)}, u32[]{:S(2)}) copy-start(f32[1,1,1024]{2,0,1:T(1,128)S(1)} %get-tuple-element.94) | copy-start | bytes 12292
  11.4 4.8 copy-start.75
  12.7 3.5 copy-start.77
  12.7 3.5 copy-start.28
  16.2 4.5 copy-start.54
  20.7 2.8 copy-start.16
  23.5 7.9 %copy-start.19 = (bf16[1,1024,512]{2,1,0:T(8,128)(2,1)S(1)}, bf16[1,1024,512]{2,1,0:T(8,128)(2,1)}, u32[]{:S(2)}) copy-start(bf16[1,1024,512]{2,1,0:T(8,128)(2,1)} %param.16) | copy-start | bytes 3145732
  34.4 2.2 copy-start.76
  36.8 3.8 slice-start
  38.6 2.7 slice-start.1
  39.8 4.4 slice-start.2
  41.3 2.8 slice-start.3
  44.2 11.4 %copy-start.70 = (f32[1,1,1024]{2,0,1:T(1,128)S(1)}, f32[1,1,1024]{2,0,1:T(1,128)}, u32[]{:S(2)}) copy-start(f32[1,1,1024]{2,0,1:T(1,128)} %copy-done.69) | copy-start | bytes 12292
  52.7 2.5 collective-permute-start
  52.8 3.8 copy-start.20
  55.6 68.6 %copy-start.52 = (f32[3,64]{1,0:T(4,128)}, f32[3,64]{1,0:T(4,128)S(1)}, u32[]{:S(2)}) copy-start(f32[3,64]{1,0:T(4,128)S(1)} %add_rsqrt_fusion.2) | copy-start | bytes 2308
  60.1 8.0 %copy-start.64 = (pred[3,576]{1,0:T(4,128)(4,1)S(1)}, pred[3,576]{1,0:T(4,128)(4,1)}, u32[]{:S(2)}) copy-start(pred[3,576]{1,0:T(4,128)(4,1)} %copy-done.63) | copy-start | bytes 5188
  72.8 3.7 copy-start.14
  76.4 10.3 %copy-start.44 = (bf16[3,8,64,64]{3,2,1,0:T(8,128)(2,1)}, bf16[3,8,64,64]{3,2,1,0:T(8,128)(2,1)S(1)}, u32[]{:S(2)}) copy-start(bf16[3,8,64,64]{3,2,1,0:T(8,128)(2,1)S(1)} %convolution_convert_fusion.6) | copy-start | bytes 589828
  78.1 8.7 %copy-start.45 = (bf16[3,64,1024]{2,1,0:T(8,128)(2,1)}, bf16[3,64,1024]{2,1,0:T(8,128)(2,1)S(1)}, u32[]{:S(2)}) copy-start(bf16[3,64,1024]{2,1,0:T(8,128)(2,1)S(1)} %add_convert_fusion.2) | copy-start | bytes 1179652
  102.0 4.0 copy-start.3
  102.0 4.0 copy-start.49
  121.7 2.5 copy-start.8
  121.7 2.5 copy-start.26
  121.7 2.5 copy-start.36
  125.7 3.5 collective-permute-start.2
  131.3 6.3 %copy-start.9 = (f32[3,64,1024]{2,1,0:T(8,128)S(1)}, f32[3,64,1024]{2,1,0:T(8,128)}, u32[]{:S(2)}) copy-start(f32[3,64,1024]{2,1,0:T(8,128)} %copy-done.7) | copy-start | bytes 2359300
  137.6 7.7 %copy-start.42 = (bf16[3,64,4096]{2,1,0:T(8,128)(2,1)}, bf16[3,64,4096]{2,1,0:T(8,128)(2,1)S(1)}, u32[]{:S(2)}) copy-start(bf16[3,64,4096]{2,1,0:T(8,128)(2,1)S(1)} %fusion.25) | copy-start | bytes 4718596
  137.6 7.7 %copy-start.27 = (bf16[3,1,64,1024]{3,2,1,0:T(8,128)(2,1)S(1)}, bf16[3,1,64,1024]{3,2,1,0:T(8,128)(2,1)}, u32[]{:S(2)}) copy-start(bf16[3,1,64,1024]{3,2,1,0:T(8,128)(2,1)} %param.21) | copy-start | bytes 1179652
  145.3 3.2 copy-start.15
  150.0 5.7 %copy-start.4 = (f32[3,8,64,576]{3,2,1,0:T(8,128)S(1)}, f32[3,8,64,576]{3,2,1,0:T(8,128)}, u32[]{:S(2)}) copy-start(f32[3,8,64,576]{3,2,1,0:T(8,128)} %get-tuple-element.108) | copy-start | bytes 10616836
  150.0 5.7 %copy-start.48 = (bf16[3,64,512]{1,2,0:T(8,128)(2,1)S(1)}, bf16[3,64,512]{1,2,0:T(8,128)(2,1)}, u32[]{:S(2)}) copy-start(bf16[3,64,512]{1,2,0:T(8,128)(2,1)} %copy.263) | copy-start | bytes 589828
  172.8 2.8 copy-start.2
  172.8 2.8 copy-start.55
  172.8 2.8 copy-start.57
  175.6 5.8 %copy-start.18 = (bf16[3,512,1024]{2,1,0:T(8,128)(2,1)}, bf16[3,512,1024]{2,1,0:T(8,128)(2,1)S(1)}, u32[]{:S(2)}) copy-start(bf16[3,512,1024]{2,1,0:T(8,128)(2,1)S(1)} %pad_maximum_fusion.1) | copy-start | bytes 9437188
  191.6 6.9 %copy-start.50 = (u8[64,4096]{1,0:T(8,128)(4,1)S(1)}, u8[64,4096]{1,0:T(8,128)(4,1)}, u32[]{:S(2)}) copy-start(u8[64,4096]{1,0:T(8,128)(4,1)} %get-tuple-element.64) | copy-start | bytes 786436
  191.6 6.9 %copy-start.51 = (u8[64,4096]{1,0:T(8,128)(4,1)S(1)}, u8[64,4096]{1,0:T(8,128)(4,1)}, u32[]{:S(2)}) copy-start(u8[64,4096]{1,0:T(8,128)(4,1)} %get-tuple-element.65) | copy-start | bytes 786436
  198.5 8.5 %copy-start.10 = (f32[3,64,1024]{2,1,0:T(8,128)S(1)}, f32[3,64,1024]{2,1,0:T(8,128)}, u32[]{:S(2)}) copy-start(f32[3,64,1024]{2,1,0:T(8,128)} %copy-done.7) | copy-start | bytes 2359300
  207.0 6.8 %copy-start.25 = (bf16[3,64,4096]{2,1,0:T(8,128)(2,1)}, bf16[3,64,4096]{2,1,0:T(8,128)(2,1)S(1)}, u32[]{:S(2)}) copy-start(bf16[3,64,4096]{2,1,0:T(8,128)(2,1)S(1)} %fusion.42) | copy-start | bytes 4718596
  213.8 284.0 %collective-permute-start.1 = (f32[3,64,1024]{2,1,0:T(8,128)}, f32[3,64,1024]{2,1,0:T(8,128)}, u32[]{:S(2)}, u32[]{:S(2)}) collective-permute-start(f32[3,64,1024]{2,1,0:T(8,128)} %fusion.139), channel_id=1, source_target_pairs={{64,0},{0,64},{65,1},{1,65},{66,2},{2,66},{67,3},{3,67},{68,4},{4,... | collective-permute-start | bytes 2359304 | tf_op jit(solution)/shard_map/ppermute | solution.py:21
  219.7 8.6 %copy-start.30 = (bf16[3,64,1024]{2,1,0:T(8,128)(2,1)S(1)}, bf16[3,64,1024]{2,1,0:T(8,128)(2,1)}, u32[]{:S(2)}) copy-start(bf16[3,64,1024]{2,1,0:T(8,128)(2,1)} %copy-done.29) | copy-start | bytes 1179652
  229.4 3.1 copy-start.38
  241.3 2.3 copy-start.12
  245.7 3.0 copy-start.72
  245.7 3.0 copy-start.74
  245.7 3.0 copy-start.71
  245.7 3.0 copy-start.73
  248.1 251.6 %collective-permute-start.3 = (f32[3,64,1024]{2,1,0:T(8,128)}, f32[3,64,1024]{2,1,0:T(8,128)}, u32[]{:S(2)}, u32[]{:S(2)}) collective-permute-start(f32[3,64,1024]{2,1,0:T(8,128)} %multiply_add_fusion), channel_id=1, source_target_pairs={{64,0},{0,64},{65,1},{1,65},{66,2},{2,66},{67,3},{3,67},{68,4},{4,... | collective-permute-start | bytes 2359304 | tf_op jit(solution)/shard_map/ppermute | solution.py:21
  261.1 4.0 copy-start.32
  265.0 8.5 %copy-start.34 = (bf16[3,64,1024]{2,1,0:T(8,128)(2,1)S(1)}, bf16[3,64,1024]{2,1,0:T(8,128)(2,1)}, u32[]{:S(2)}) copy-start(bf16[3,64,1024]{2,1,0:T(8,128)(2,1)} %copy-done.33) | copy-start | bytes 1179652
  275.9 2.5 copy-start.46
  276.0 3.4 copy-start.58
  276.0 3.4 copy-start.61
  276.0 3.4 copy-start.62
  276.0 3.4 copy-start.66
  279.4 4.7 copy-start.37
  287.8 3.0 copy-start.24
  (24 other events, 36.5 us)
Sparse Core Ops, SparseCore 0:
  185.2 19.5 reduce-scatter.1

commit v2 on v1

v2 whole, which is shorter than its diff:
```python
import jax
import jax.numpy as jnp
from jax import lax
from jax.experimental import pallas as pl
from jax.experimental.pallas import tpu as pltpu
from jax.sharding import PartitionSpec as P

MESH = pl.DeviceIdType.MESH
F32 = jnp.float32
BF16 = jnp.bfloat16
NORM_EPS = 1e-05
MASK_FILL = -1e30
ROOT_HALF = 0.7071067811865476
INV_ROOT_TAU = 0.3989422804014327
ROWS_ALL = 192
KEYS = 640
FF_STEPS = 8


def mm(left, right):
    return jnp.dot(left, right, preferred_element_type=F32)


def mm_nt(left, right):
    return lax.dot_general(left, right, (((1,), (1,)), ((), ())), preferred_element_type=F32)


def mm_tn(left, right):
    return lax.dot_general(left, right, (((0,), (0,)), ((), ())), preferred_element_type=F32)


def normed_rows(values):
    average = jnp.mean(values, -1, keepdims=True)
    centred = values - average
    inverse = lax.rsqrt(jnp.mean(centred * centred, -1, keepdims=True) + NORM_EPS)
    return centred * inverse, inverse


def norm_back(grad, normed, inverse, gain):
    scaled = grad * gain
    inner = jnp.mean(scaled, -1, keepdims=True)
    along = jnp.mean(scaled * normed, -1, keepdims=True)
    back = inverse * (scaled - inner - normed * along)
    return back, jnp.sum(grad * normed, 0, keepdims=True), jnp.sum(grad, 0, keepdims=True)


def turned(block):
    rows = block.shape[0]
    if rows < 256:
        block = jnp.concatenate([block, jnp.zeros((256 - rows, block.shape[1]), block.dtype)], 0)
    return block.T.astype(BF16)


def head_stack(block):
    lane = lax.broadcasted_iota(jnp.int32, (64, 256), 1) // 64
    return jnp.concatenate([jnp.where(lane == h, block, jnp.zeros_like(block)) for h in range(4)], 0)


def head_merge(block):
    lane = lax.broadcasted_iota(jnp.int32, (64, 256), 1) // 64
    return sum(jnp.where(lane == h, block[64 * h : 64 * h + 64], 0.0) for h in range(4))


def layers_kernel(
    latents, media, mask, gains, biases, w_query, w_keyval, w_out, w_up, w_down, cotangent,
    resampled, latents_grad, media_grad, left, right,
    xs, x1s, gys, n1s, n2s, inv, accs, lin, ffin, qs, kv, probs, att, gatt, pres, sums, stage, got, sent,
    wu, wd, w_sem, x_sem, g_sem, r_sem, l_sem, m_send, m_recv,
):
    section = lax.axis_index("section")
    other = 1 - section
    barrier = pltpu.get_barrier_semaphore()
    pl.semaphore_signal(barrier, inc=1, device_id={"section": other}, device_id_type=MESH)
    pl.semaphore_wait(barrier, 1)

    def to_other(source, target, sem):
        return pltpu.make_async_remote_copy(
            src_ref=source, dst_ref=target, send_sem=sem.at[0], recv_sem=sem.at[1],
            device_id={"section": other}, device_id_type=MESH,
        )

    def weights(step):
        slot = step % 2
        at = pl.ds(pl.multiple_of(step * 512, 512), 512)
        return (
            pltpu.make_async_copy(w_up.at[:, at], wu.at[slot], w_sem.at[0, slot]),
            pltpu.make_async_copy(w_down.at[at, :], wd.at[slot], w_sem.at[1, slot]),
        )

    def fetch(step):
        for c in weights(step):
            c.start()

    def fetched(step):
        for c in weights(step):
            c.wait()

    fetch(0)
    def media_block(i, carry):
        rows = pl.ds(pl.multiple_of(i * 256, 256), 256)
        normed, _ = normed_rows(media[rows, :].astype(F32))
        media_in = (normed * gains[0:1, :] + biases[0:1, :]).astype(BF16)
        left[8 + i] = turned(media_in.astype(F32))
        at = pl.ds(pl.multiple_of((i % 2) * 256, 256), 256)
        kv[i // 2, at, :] = mm(media_in, w_keyval[...]).astype(BF16)
        return carry

    lax.fori_loop(0, 6, media_block, 0)
    for v in range(3):
        kv[v, pl.ds(576, 64), :] = jnp.zeros((64, 1024), BF16)
    for k in range(55):
        if k != 24 and not (k >= 27 and (k - 27) % 7 != 6):
            right[k, pl.ds(192, 64), :] = jnp.zeros((64, 256), BF16)
    row = lax.broadcasted_iota(jnp.int32, (256, 256), 0)
    col = lax.broadcasted_iota(jnp.int32, (256, 256), 1)
    right[24] = jnp.where(((row == col) & (row < 6)) | ((row == col + 6) & (row >= 6) & (row < 12)), 1.0, 0.0).astype(BF16)

    @pl.when(section == 0)
    def _():
        xs[...] = latents[...].astype(F32)

    @pl.when(section == 1)
    def _():
        to_other(accs, xs, x_sem).wait_recv()

    normed, inverse = normed_rows(xs[...])
    n1s[...] = normed
    inv[0] = jnp.broadcast_to(inverse, (ROWS_ALL, 128))
    latent_in = (normed * gains[1:2, :] + biases[1:2, :]).astype(BF16)
    lin[...] = latent_in
    left[14] = turned(latent_in.astype(F32))
    qs[...] = (mm(lin[...], w_query[...]) * 0.125).astype(BF16)
    latent_kv = mm(lin[...], w_keyval[...]).astype(BF16)
    for v in range(3):
        kv[v, pl.ds(512, 64), :] = latent_kv[64 * v : 64 * v + 64]

    def attend(v, carry):
        rows = pl.ds(pl.multiple_of(v * 64, 64), 64)
        for g in range(2):
            cols = pl.ds(256 * g, 256)
            stacked = head_stack(qs[rows, cols])
            scores = mm_nt(stacked, kv[v, :, cols])
            scores = jnp.where(mask[v] > 0.0, scores, MASK_FILL)
            raised = jnp.exp(scores - jnp.max(scores, -1, keepdims=True))
            p = raised * (1.0 / jnp.sum(raised, -1, keepdims=True))
            probs[v, g] = p
            mixed = mm(p.astype(BF16), kv[v, :, pl.ds(512 + 256 * g, 256)])
            att[rows, cols] = head_merge(mixed).astype(BF16)
        return carry

    lax.fori_loop(0, 3, attend, 0)

    x1 = xs[...] + mm(att[...], w_out[...])
    x1s[...] = x1
    normed, inverse = normed_rows(x1)
    n2s[...] = normed
    inv[1] = jnp.broadcast_to(inverse, (ROWS_ALL, 128))
    ffin[...] = (normed * gains[2:3, :] + biases[2:3, :]).astype(BF16)
    left[4] = turned(ffin[...].astype(F32))
    att_rows = att[...].astype(F32)
    att_t = jnp.concatenate([att_rows, jnp.zeros((64, 512), F32)], 0).T.reshape(64, 8, 256)
    none = jnp.zeros_like(att_t)
    left[5] = jnp.concatenate([att_t, none], 1).reshape(1024, 256).astype(BF16)
    left[6] = jnp.concatenate([none, att_t], 1).reshape(1024, 256).astype(BF16)

    accs[...] = x1s[...]

    def ff_forward(j, carry):
        fetched(j)

        @pl.when(j + 1 < FF_STEPS)
        def _():
            fetch(j + 1)

        pre = mm(ffin[...], wu[j % 2])
        pres[j] = pre
        act = (pre * (0.5 * (1.0 + lax.erf(pre * ROOT_HALF)))).astype(BF16)
        act_t = turned(act.astype(F32)).reshape(8, 4, 16, 256)
        at = pl.ds(pl.multiple_of(j * 128, 128), 128)
        for i in range(4):
            left[i, at, :] = act_t[:, i].reshape(128, 256)
        accs[...] += mm(act, wd[j % 2])
        return carry

    lax.fori_loop(0, FF_STEPS, ff_forward, 0)
    fetch(0)

    @pl.when(section == 0)
    def _():
        to_other(accs, xs, x_sem).start()
        to_other(sent, resampled, r_sem).wait_recv()
        to_other(accs, xs, x_sem).wait_send()
        to_other(accs, gys, g_sem).wait_recv()

    @pl.when(section == 1)
    def _():
        sent[...] = accs[:, pl.ds(0, 512)]
        to_other(sent, resampled, r_sem).start()
        resampled[...] = accs[:, pl.ds(512, 512)]
        gys[...] = cotangent[...].astype(F32)
        to_other(sent, resampled, r_sem).wait_send()

    grad_out = gys[...].astype(BF16)
    for k in range(4):
        right[k, pl.ds(0, 192), :] = grad_out[:, 256 * k : 256 * k + 256]
    ffin[...] = grad_out
    accs[...] = jnp.zeros((ROWS_ALL, 1024), F32)

    def ff_backward(j, carry):
        fetched(j)

        @pl.when(j + 1 < FF_STEPS)
        def _():
            fetch(j + 1)

        grad_act = mm_nt(ffin[...], wd[j % 2])
        pre = pres[j]
        slope = 0.5 * (1.0 + lax.erf(pre * ROOT_HALF)) + pre * jnp.exp(-0.5 * pre * pre) * INV_ROOT_TAU
        grad_pre = (grad_act * slope).astype(BF16)
        right[4 + 2 * j, pl.ds(0, 192), :] = grad_pre[:, :256]
        right[5 + 2 * j, pl.ds(0, 192), :] = grad_pre[:, 256:]
        accs[...] += mm_nt(grad_pre, wu[j % 2])
        return carry

    lax.fori_loop(0, FF_STEPS, ff_backward, 0)

    back, gain_sum, bias_sum = norm_back(accs[...], n2s[...], inv[1][:, :1], gains[2:3, :])
    sums[pl.ds(2, 1), :] = gain_sum
    sums[pl.ds(5, 1), :] = bias_sum
    grad_x1 = gys[...] + back
    gys[...] = grad_x1
    grad_attn = grad_x1.astype(BF16)
    for k in range(4):
        right[20 + k, pl.ds(0, 192), :] = grad_attn[:, 256 * k : 256 * k + 256]
    gatt[...] = mm_nt(grad_attn, w_out[...]).astype(BF16)

    def attend_back(v, carry):
        rows = pl.ds(pl.multiple_of(v * 64, 64), 64)
        for g in range(2):
            cols = pl.ds(256 * g, 256)
            q_stack = head_stack(qs[rows, cols])
            g_stack = head_stack(gatt[rows, cols])
            p = probs[v, g]
            grad_p = mm_nt(g_stack, kv[v, :, pl.ds(512 + 256 * g, 256)])
            weighted = p * grad_p
            grad_s = (weighted - p * jnp.sum(weighted, -1, keepdims=True)).astype(BF16)
            right[25 + g, rows, :] = head_merge(mm(grad_s, kv[v, :, cols])).astype(BF16)
            for base, value in (
                (27 + 7 * g, mm_tn(grad_s, q_stack)),
                (41 + 7 * g, mm_tn(p.astype(BF16), g_stack)),
            ):
                value = value.astype(BF16)
                right[base + 2 * v] = value[:256]
                right[base + 2 * v + 1] = value[256:512]
                right[base + 6, rows, :] = value[512:576]
        return carry

    lax.fori_loop(0, 3, attend_back, 0)

    grad_in = mm_nt(right[25, pl.ds(0, 192), :], w_query[:, pl.ds(0, 256)]) + mm_nt(
        right[26, pl.ds(0, 192), :], w_query[:, pl.ds(256, 256)]
    )
    grad_in = grad_in * 0.125
    for k in range(4):
        grad_in += mm_nt(right[33 + 7 * k, pl.ds(0, 192), :], w_keyval[:, pl.ds(256 * k, 256)])
    back, gain_sum, bias_sum = norm_back(grad_in, n1s[...], inv[0][:, :1], gains[1:2, :])
    sums[pl.ds(1, 1), :] = gain_sum
    sums[pl.ds(4, 1), :] = bias_sum
    accs[...] = gys[...] + back

    @pl.when(section == 1)
    def _():
        to_other(accs, gys, g_sem).start()
        to_other(accs, gys, g_sem).wait_send()

    @pl.when(section == 0)
    def _():
        sent[...] = accs[:, pl.ds(512, 512)]
        to_other(sent, latents_grad, l_sem).start()
        latents_grad[...] = accs[:, pl.ds(0, 512)]
        to_other(sent, latents_grad, l_sem).wait_send()

    def media_copy(i):
        return pltpu.make_async_remote_copy(
            src_ref=stage.at[i, other], dst_ref=got.at[i], send_sem=m_send.at[i], recv_sem=m_recv.at[i],
            device_id={"section": other}, device_id_type=MESH,
        )

    sums[pl.ds(0, 1), :] = jnp.zeros((1, 1024), F32)
    sums[pl.ds(3, 1), :] = jnp.zeros((1, 1024), F32)

    def media_back(i, carry):
        rows = pl.ds(pl.multiple_of(i * 256, 256), 256)
        normed, inverse = normed_rows(media[rows, :].astype(F32))
        grad_media = jnp.zeros((256, 1024), F32)
        for k in range(4):
            grad_media += mm_nt(right[27 + 7 * k + i], w_keyval[:, pl.ds(256 * k, 256)])
        back, gain_sum, bias_sum = norm_back(grad_media, normed, inverse, gains[0:1, :])
        sums[pl.ds(0, 1), :] += gain_sum
        sums[pl.ds(3, 1), :] += bias_sum
        stage[i, 0] = back[:, :512]
        stage[i, 1] = back[:, 512:]
        media_copy(i).start()
        return carry

    lax.fori_loop(0, 6, media_back, 0)

    total = sums[pl.ds(0, 6), :]
    high = total.astype(BF16).astype(F32)
    left[7] = turned(jnp.concatenate([high, total - high, jnp.zeros((244, 1024), F32)], 0))

    def media_sum(i, carry):
        media_copy(i).wait()
        rows = pl.ds(pl.multiple_of(i * 256, 256), 256)
        media_grad[rows, :] = stage[i, section] + got[i]
        return carry

    lax.fori_loop(0, 6, media_sum, 0)

    @pl.when(section == 1)
    def _():
        to_other(sent, latents_grad, l_sem).wait_recv()


def run_layers(latents, media, mask, gains, biases, w_query, w_keyval, w_out, w_up, w_down, cotangent):
    vmem = pl.BlockSpec(memory_space=pltpu.VMEM)
    hbm = pl.BlockSpec(memory_space=pl.ANY)
    sds = jax.ShapeDtypeStruct
    return pl.pallas_call(
        layers_kernel,
        out_shape=[
            sds((192, 512), F32), sds((192, 512), F32), sds((1536, 512), F32), sds((15, 1024, 256), BF16), sds((55, 256, 256), BF16),
        ],
        in_specs=[vmem] * 8 + [hbm, hbm, vmem],
        out_specs=[vmem] * 5,
        scratch_shapes=[
            pltpu.VMEM((192, 1024), F32),
            pltpu.VMEM((192, 1024), F32),
            pltpu.VMEM((192, 1024), F32),
            pltpu.VMEM((192, 1024), F32),
            pltpu.VMEM((192, 1024), F32),
            pltpu.VMEM((2, 192, 128), F32),
            pltpu.VMEM((192, 1024), F32),
            pltpu.VMEM((192, 1024), BF16),
            pltpu.VMEM((192, 1024), BF16),
            pltpu.VMEM((192, 512), BF16),
            pltpu.VMEM((3, KEYS, 1024), BF16),
            pltpu.VMEM((3, 2, 256, KEYS), F32),
            pltpu.VMEM((192, 512), BF16),
            pltpu.VMEM((192, 512), BF16),
            pltpu.VMEM((FF_STEPS, 192, 512), F32),
            pltpu.VMEM((8, 1024), F32),
            pltpu.VMEM((6, 2, 256, 512), F32),
            pltpu.VMEM((6, 256, 512), F32),
            pltpu.VMEM((192, 512), F32),
            pltpu.VMEM((2, 1024, 512), BF16),
            pltpu.VMEM((2, 512, 1024), BF16),
            pltpu.SemaphoreType.DMA((2, 2)),
            pltpu.SemaphoreType.DMA((2,)),
            pltpu.SemaphoreType.DMA((2,)),
            pltpu.SemaphoreType.DMA((2,)),
            pltpu.SemaphoreType.DMA((2,)),
            pltpu.SemaphoreType.DMA((6,)),
            pltpu.SemaphoreType.DMA((6,)),
        ],
        compiler_params=pltpu.CompilerParams(collective_id=2, has_side_effects=True, vmem_limit_bytes=60 * 2**20),
        name="layers",
    )(latents, media, mask, gains, biases, w_query, w_keyval, w_out, w_up, w_down, cotangent)


CHUNKS = 41
GROUPS = 14
TICKS = GROUPS + 6
ROWS = (256, 64, 16)
COLS = 256


def chunk_plan(c):
    left = jnp.where(c < 16, c // 4, jnp.where(c < 32, 4, jnp.where(c < 34, 5, jnp.where(c < 35, 7, jnp.where(c < 37, 14, 8)))))
    right = jnp.where(c < 16, c % 4, jnp.where(c < 32, c - 12, jnp.where(c < 34, 20 + 2 * (c - 32), jnp.where(c < 35, 24, jnp.where(c < 37, c - 10, 27 + 7 * (c - 37))))))
    steps = jnp.where(c < 32, 1, jnp.where(c < 34, 2, jnp.where(c < 37, 1, 7)))
    return left, right, steps


def shard_kernel(left_ref, right_ref, out_ref, own1, own2, own3, a1, a2, a3, b1, b2, b3, send_sem, recv_sem):
    me = lax.axis_index("dp")
    coords = (me // 16, (me // 4) % 4, me % 4)
    strides = (16, 4, 1)

    def at(axis, shift):
        return (coords[axis] + shift) % 4

    def neighbour(axis, shift):
        return me + (at(axis, shift) - coords[axis]) * strides[axis]

    barrier = pltpu.get_barrier_semaphore()
    for axis in range(3):
        for shift in (1, 3):
            pl.semaphore_signal(barrier, inc=1, device_id={"dp": neighbour(axis, shift)}, device_id_type=MESH)
    pl.semaphore_wait(barrier, 6)

    own = (own1, own2, own3)
    got_a = (a1, a2, a3)
    got_b = (b1, b2, b3)

    def copy(order, stage, step, way, group, tick):
        axis = (order + stage) % 3
        half = ROWS[stage] // 2
        place = own[stage].at[order, group % 3]
        turn = tick % 2
        sem = (((order * 3 + stage) * 2 + step) * 2 + way) * 2 + turn
        shift = 1 if way == 0 else 3
        if step == 0:
            source = place.at[at(axis, 2), pl.ds(way * half, half)]
            target = got_a[stage].at[order, way, turn]
        else:
            source = place.at[at(axis, shift)]
            target = got_b[stage].at[order, way, turn]
        return pltpu.make_async_remote_copy(
            src_ref=source,
            dst_ref=target,
            send_sem=send_sem.at[sem],
            recv_sem=recv_sem.at[sem],
            device_id={"dp": neighbour(axis, shift)},
            device_id_type=MESH,
        )

    def terms(order, group):
        chunk = 3 * group + order
        left, right, steps = chunk_plan(chunk)
        slot = group % 3

        def place(step, first):
            for i in range(4):
                block = jnp.dot(
                    left_ref[left + step, pl.ds(256 * i, 256), :], right_ref[right + step], preferred_element_type=jnp.float32
                )
                for j in range(4):
                    for k in range(4):
                        spot = ((i, j, k), (j, k, i), (k, i, j))[order]
                        rows = pl.ds((spot[1] * 4 + spot[2]) * 16, 16)
                        part = block[(j * 4 + k) * 16 : (j * 4 + k) * 16 + 16]
                        if first:
                            own1[order, slot, spot[0], rows, :] = part
                        else:
                            own1[order, slot, spot[0], rows, :] += part

        place(0, True)

        def more(step, carry):
            place(step, False)
            return carry

        lax.fori_loop(1, steps, more, 0)

    def valid(order, group):
        return (group >= 0) & (group * 3 + order < CHUNKS)

    def tick(t, carry):
        for order in range(3):

            @pl.when(valid(order, t))
            def _():
                terms(order, t)

        for stage in range(3):
            for order in range(3):
                axis = (order + stage) % 3
                half = ROWS[stage] // 2
                turn = (t - 1) % 2
                group_a = t - 1 - 2 * stage

                @pl.when(valid(order, group_a))
                def _():
                    for way in range(2):
                        done = copy(order, stage, 0, way, group_a, t - 1)
                        done.wait()
                        spot = at(axis, 1 if way == 0 else 3)
                        own[stage][order, group_a % 3, spot, pl.ds(way * half, half), :] += got_a[stage][order, way, turn]

                group_b = t - 2 - 2 * stage

                @pl.when(valid(order, group_b))
                def _():
                    for way in range(2):
                        done = copy(order, stage, 1, way, group_b, t - 1)
                        done.wait()
                    total = (
                        own[stage][order, group_b % 3, at(axis, 0)]
                        + got_b[stage][order, 0, turn]
                        + got_b[stage][order, 1, turn]
                    )
                    if stage < 2:
                        own[stage + 1][order, group_b % 3] = total.reshape(4, ROWS[stage + 1], COLS)
                    else:
                        out_ref[group_b * 3 + order] = total

        for stage in range(3):
            for order in range(3):
                group_a = t - 2 * stage
                group_b = t - 1 - 2 * stage

                @pl.when(valid(order, group_a))
                def _():
                    for way in range(2):
                        copy(order, stage, 0, way, group_a, t).start()

                @pl.when(valid(order, group_b))
                def _():
                    for way in range(2):
                        copy(order, stage, 1, way, group_b, t).start()

        return carry

    lax.fori_loop(0, TICKS, tick, 0)


def scattered_terms(left, right):
    vmem = pl.BlockSpec(memory_space=pltpu.VMEM)
    f32 = jnp.float32
    return pl.pallas_call(
        shard_kernel,
        out_shape=jax.ShapeDtypeStruct((CHUNKS, 16, COLS), f32),
        in_specs=[vmem, vmem],
        out_specs=vmem,
        scratch_shapes=[pltpu.VMEM((3, 3, 4, r, COLS), f32) for r in ROWS]
        + [pltpu.VMEM((3, 2, 2, r // 2, COLS), f32) for r in ROWS]
        + [pltpu.VMEM((3, 2, 2, r, COLS), f32) for r in ROWS]
        + [pltpu.SemaphoreType.DMA((72,)), pltpu.SemaphoreType.DMA((72,))],
        compiler_params=pltpu.CompilerParams(collective_id=1, has_side_effects=True, vmem_limit_bytes=50 * 2**20),
        name="scatter_terms",
    )(left, right)


def body(
    latents_in, media, frame_count, gains, biases, w_query, w_keyval, w_out, w_up, w_down, cotangent
):
    key = jnp.arange(KEYS)
    valid = (key[None] < 64 * frame_count) | ((key[None] >= 512) & (key[None] < 576))
    mask = valid.astype(F32)[:, None, :]
    resampled, latents_grad, media_grad, left, right = run_layers(
        latents_in.reshape(192, 1024), media.reshape(1536, 1024), mask, gains[0], biases[0],
        w_query[0], w_keyval[0], w_out[0], w_up[0], w_down[0], cotangent.reshape(192, 1024),
    )
    got = scattered_terms(left, right)
    small = got[34, :, :6].T
    return (
        resampled.reshape(3, 1, 64, 512),
        latents_grad.reshape(3, 1, 64, 512),
        media_grad.reshape(3, 1, 512, 512),
        small[None, :3],
        small[None, 3:],
        got[35:37].transpose(1, 0, 2).reshape(1, 16, 512) * 0.125,
        got[37:41].transpose(1, 0, 2).reshape(1, 16, 1024),
        got[32:34].reshape(2, 2, 8, 256).transpose(2, 0, 1, 3).reshape(1, 8, 1024),
        got[16:32].transpose(1, 0, 2).reshape(1, 16, 4096),
        got[0:16].reshape(4, 4, 16, 256).transpose(0, 2, 1, 3).reshape(1, 64, 1024),
    )


def solution(mesh):
    placed = (
        P(None, "dp", None, None),
        P(None, "dp", None, None),
        P(None, "dp"),
        P("section", None, None),
        P("section", None, None),
        P("section", None, None),
        P("section", None, None),
        P("section", None, None),
        P("section", None, None),
        P("section", None, None),
        P(None, "dp", None, None),
    )
    return jax.shard_map(
        body,
        mesh=mesh,
        in_specs=placed,
        out_specs=(
            P(None, "dp", None, "section"),
            P(None, "dp", None, "section"),
            P(None, "dp", None, "section"),
            P("section", None, "dp"),
            P("section", None, "dp"),
            P("section", "dp", None),
            P("section", "dp", None),
            P("section", "dp", None),
            P("section", "dp", None),
            P("section", "dp", None),
        ),
        check_vma=False,
    )
```

time: 516 us -> 321 us (0.62); the launches traced: 509 us -> 320 us
  local copies, waits for them, and re-layouts: 122 us -> 11.3 us
  matrix products: 106 us -> 0 us
  Pallas kernels: 202 us -> 306 us
  other arithmetic: 56.9 us -> 1.96 us
  between operations: 15.5 us -> 0.71 us
    pallas_call x0 -> x1, Pallas kernels: none -> 103 us  [run_layers(): pl.pallas_call(layers_kernel, out_shape=[sds((192, 512), F32), sds((192,...]
    dot_general x32 -> x0, matrix products: 101 us -> none  [the longest x10 40.5 us: against_rows(): lax.dot_general(left, right, (((1,), (1,)), ((), ())), preferred_element_...]
    reshape x15 -> x0, local copies, waits for them, and re-layouts: 32.6 us -> none  [the longest x7 13.5 us: flat_rows(): return block.reshape(-1, block.shape[-1])]
    convert_element_type x10 -> x1, other arithmetic: 22.6 us -> 0.67 us  [body(): mask = valid.astype(F32)[:, None, :]]
    slice x6 -> x0, local copies, waits for them, and re-layouts: 18.1 us -> none  [the longest x2 7.9 us: layer_forward(): keyvals[:, inner_width:].reshape(key_count, head_count, head_width)]
    unnamed x179 -> x10, local copies, waits for them, and re-layouts: 23.5 us -> 7.83 us
    concatenate x8 -> x0, local copies, waits for them, and re-layouts: 12.1 us -> none  [the longest x3 9.87 us: body(): jnp.concatenate([rows_deep(grad_media_kv), rows_deep(grad_latent_kv)], 0)]
    convert_element_type x3 -> x0, local copies, waits for them, and re-layouts: 10.1 us -> none  [the longest x1 6.85 us: layer_forward(): media_rows.astype(jnp.float32)]
  transfers between devices with their start and end apart: 5 -> 0, of which waited for: 2 -> 0; matrix products, arithmetic and copies ran while one was open for 21% -> 0% of each run, Pallas kernels for 40% -> 0%
where the time goes in v2:
time: 321 us; the launch traced here: 320 us
  Pallas kernels  306 us (95%)
  local copies, waits for them, and re-layouts  11.3 us (4%)
    pallas_call x1, Pallas kernels, scattered_terms(): pl.pallas_call(shard_kernel, out_shape=jax.ShapeDtypeStruct((CHUNKS, 16,...  203 us
    pallas_call x1, Pallas kernels, run_layers(): pl.pallas_call(layers_kernel, out_shape=[sds((192, 512), F32), sds((192,...  103 us
    unnamed x10, local copies, waits for them, and re-layouts  7.83 us

profile of v2, /device:TPU:0, one launch (start us, length us, event | category | flops | bytes accessed | tf_op | source)
XLA Modules:
  0.0 320.0 jit_solution(2194371293651596896)
XLA Ops:
  0.6 0.7 multiply_bitcast_fusion.1
  1.3 0.7 or_convert_fusion.mask
  2.0 1.3 copy_bitcast_fusion
  3.3 102.9 %layers.1 = (f32[192,512]{1,0:T(8,128)}, f32[192,512]{1,0:T(8,128)}, f32[1536,512]{1,0:T(8,128)}, bf16[15,1024,256]{2,1,0:T(8,128)(2,1)}, bf16[55,256,256]{2,1,0:T(8,128)(2,1)}) custom-call(bf16[192,1024]{1,0:T(8,128)(2,1)} %bitcast.54, bf16[1536,1024]{1,0:T(8,128)(2,1)} %bitcast.46, f32[3,1,640]{2,1,0:T(1,128)} %or_convert_fusion.mask, ...), custom_call_target="tpu_custom_call" | custom-call | tf_op jit(solution)/shard_map/layers/pallas_call | solution.py:329
  106.2 0.0 copy-start.1
  106.2 0.0 copy-start
  106.2 203.2 %scatter_terms.1 = f32[41,16,256]{2,1,0:T(8,128)S(1)} custom-call(bf16[15,1024,256]{2,1,0:T(8,128)(2,1)} %get-tuple-element.18.left_ref, bf16[55,256,256]{2,1,0:T(8,128)(2,1)} %get-tuple-element.19.right_ref), custom_call_target="tpu_custom_call" | custom-call | tf_op jit(solution)/shard_map/scatter_terms/pallas_call | solution.py:521
  309.4 0.1 copy.28
  309.5 0.6 copy.37
  310.1 0.6 copy.36
  310.7 0.7 reshape.145
  311.3 0.6 fusion.2
  312.0 0.2 copy.32
  312.2 0.8 reshape.150
  313.0 0.6 mul.30
  313.7 0.2 copy.31
  313.8 0.8 reshape.148
  314.6 0.0 copy-done.1
  314.6 0.7 copy.45
  315.3 0.0 copy-done
  315.4 0.7 copy.46
  316.1 3.9 %copy.47 = f32[3,1,512,512]{3,2,1,0:T(8,128)} copy(f32[3,1,512,512]{3,2,1,0:T(8,128)} %bitcast.47) | data formatting | bytes 6291456
  (7 shorter events, 0.1 us)
Async XLA Ops:
  106.2 208.4 %copy-start.1 = (f32[192,512]{1,0:T(8,128)S(1)}, f32[192,512]{1,0:T(8,128)}, u32[]{:S(2)}) copy-start(f32[192,512]{1,0:T(8,128)} %get-tuple-element.15) | copy-start | bytes 1179652
  106.2 209.2 %copy-start = (f32[192,512]{1,0:T(8,128)S(1)}, f32[192,512]{1,0:T(8,128)}, u32[]{:S(2)}) copy-start(f32[192,512]{1,0:T(8,128)} %get-tuple-element.16) | copy-start | bytes 1179652

commit v3 on v2

v3 whole, which is shorter than its diff:
```python
import jax
import jax.numpy as jnp
from jax import lax
from jax.experimental import pallas as pl
from jax.experimental.pallas import tpu as pltpu
from jax.sharding import PartitionSpec as P

VMEM_BYTES = 63 * 2**20
MESH = pl.DeviceIdType.MESH
F32 = jnp.float32
BF16 = jnp.bfloat16
NORM_EPS = 1e-05
MASK_FILL = -1e30
ROOT_HALF = 0.7071067811865476
INV_ROOT_TAU = 0.3989422804014327
ROWS_ALL = 192
KEYS = 640
FF_STEPS = 8
RING_ROWS = (256, 64, 16)
COLS = 256
X, Y, Z = 0, 1, 2
FF_IN, ACT, G_OUT, G_PRE = 0, 1, 2, 3
L_LATENT, L_SMALL, L_FF, L_ACT, L_ATT = 6, 7, 8, 12, 16
R_PRE, R_OUT, R_ATT, R_QUERY, R_SMALL, R_KV = 0, 16, 32, 36, 38, 39
ABC, BCA, CBA, BAC = (0, 1, 2), (1, 2, 0), (2, 1, 0), (1, 0, 2)
PLAN = (
    (
        ("down", 0, (X, Z), ABC),
        ("down", 1, (X, Z), ABC),
        ("query", 0, (X, Y, Z), ABC),
        ("query", 1, (X, Y, Z), ABC),
        ("keyval", 0, (X, Y, Z), ABC),
        ("keyval", 2, (X, Y, Z), ABC),
    ),
    (
        ("out", 0, (Y, Z, X), BCA),
        ("out", 1, (Y, Z, X), BCA),
        ("up", 0, (Y, Z), BCA),
        ("up", 1, (Y, Z), BCA),
        ("keyval", 1, (Y, Z, X), BCA),
        ("keyval", 3, (Y, Z, X), BCA),
    ),
    (
        ("down", 2, (Z, X), BAC),
        ("down", 3, (Z, X), BAC),
        ("up", 2, (Z, Y), CBA),
        ("up", 3, (Z, Y), CBA),
        ("small", 0, (Z, Y, X), CBA),
        None,
    ),
)
GROUPS = 6
TICKS = GROUPS + 6


def mm(left, right):
    return jnp.dot(left, right, preferred_element_type=F32)


def mm_nt(left, right):
    return lax.dot_general(left, right, (((1,), (1,)), ((), ())), preferred_element_type=F32)


def mm_tn(left, right):
    return lax.dot_general(left, right, (((0,), (0,)), ((), ())), preferred_element_type=F32)


def normed_rows(values):
    average = jnp.mean(values, -1, keepdims=True)
    centred = values - average
    inverse = lax.rsqrt(jnp.mean(centred * centred, -1, keepdims=True) + NORM_EPS)
    return centred * inverse, inverse


def norm_back(grad, normed, inverse, gain):
    scaled = grad * gain
    inner = jnp.mean(scaled, -1, keepdims=True)
    along = jnp.mean(scaled * normed, -1, keepdims=True)
    back = inverse * (scaled - inner - normed * along)
    return back, jnp.sum(grad * normed, 0, keepdims=True), jnp.sum(grad, 0, keepdims=True)


def turned(block):
    rows = block.shape[0]
    if rows < 256:
        block = jnp.concatenate([block, jnp.zeros((256 - rows, block.shape[1]), block.dtype)], 0)
    return block.T.astype(BF16)


def head_stack(block):
    lane = lax.broadcasted_iota(jnp.int32, (64, 256), 1) // 64
    return jnp.concatenate([jnp.where(lane == h, block, jnp.zeros_like(block)) for h in range(4)], 0)


def head_merge(block):
    lane = lax.broadcasted_iota(jnp.int32, (64, 256), 1) // 64
    return sum(jnp.where(lane == h, block[64 * h : 64 * h + 64], 0.0) for h in range(4))


def column(block, k):
    return block[:, COLS * k : COLS * k + COLS]


def resampler_kernel(
    latents, media, mask, gains, biases, w_query, w_keyval, w_out, w_up, w_down, cotangent,
    resampled, latents_grad, out_small, out_query, out_keyval, out_out, out_up, out_down, m_own, m_got, land,
    xs, x1s, gys, accs, lin, ffin, qs, att, gatt, pres, sums, sent, m_stage, m_buf, wu, wd, gave,
    lefts, rights, own1, own2, own3, far1, far2, far3, near1, near2, near3, up_sum, up_got,
    w_sem, b_sem, x_sem, g_sem, r_sem, l_sem, m_send, m_recv, m_local, e_send, e_recv, c_sem, t_send, t_recv, u_send, u_recv,
):
    section = lax.axis_index("section")
    other = 1 - section
    me = lax.axis_index("dp")
    coords = (me // 16, (me // 4) % 4, me % 4)
    strides = (16, 4, 1)

    def at(axis, shift):
        return (coords[axis] + shift) % 4

    def peer(axis, shift):
        return me + (at(axis, shift) - coords[axis]) * strides[axis]

    barrier = pltpu.get_barrier_semaphore()
    pl.semaphore_signal(barrier, inc=1, device_id={"section": other}, device_id_type=MESH)
    greeted = [(X, 1), (X, 2), (X, 3), (Y, 1), (Y, 2), (Y, 3), (Z, 1), (Z, 3)]
    for axis, shift in greeted:
        pl.semaphore_signal(barrier, inc=1, device_id={"dp": peer(axis, shift)}, device_id_type=MESH)
    pl.semaphore_wait(barrier, 1 + len(greeted))

    def to_other(source, target, sem):
        return pltpu.make_async_remote_copy(
            src_ref=source, dst_ref=target, send_sem=sem.at[0], recv_sem=sem.at[1],
            device_id={"section": other}, device_id_type=MESH,
        )

    def weights(step):
        slot = step % 2
        cols = pl.ds(pl.multiple_of(step * 512, 512), 512)
        return (
            pltpu.make_async_copy(w_up.at[:, cols], wu.at[slot], w_sem.at[0, slot]),
            pltpu.make_async_copy(w_down.at[cols, :], wd.at[slot], w_sem.at[1, slot]),
        )

    def fetch(step):
        for c in weights(step):
            c.start()

    def fetched(step):
        for c in weights(step):
            c.wait()

    def media_rows(i):
        return pltpu.make_async_copy(
            media.at[pl.ds(pl.multiple_of(i * 256, 256), 256), :], m_buf.at[i % 2], b_sem.at[i % 2]
        )

    def exchange(kind, shift):
        axis = X if kind in (FF_IN, G_PRE) else Y
        if kind == FF_IN:
            source = gave.at[0]
        elif kind == G_OUT:
            source = gave.at[1]
        elif kind == ACT:
            source = own1.at[pl.ds(18 + 4 * at(axis, shift), 4), pl.ds(0, ROWS_ALL), :]
        else:
            source = pres.at[pl.ds(4 * at(axis, shift), 4)]
        return pltpu.make_async_remote_copy(
            src_ref=source, dst_ref=land.at[kind, shift - 1], send_sem=e_send.at[kind, shift - 1], recv_sem=e_recv.at[kind, shift - 1],
            device_id={"dp": peer(axis, shift)}, device_id_type=MESH,
        )

    def give(kind):
        for shift in (1, 3, 2):
            exchange(kind, shift).start()

    def taken(kind, use):
        def held(s):
            if kind == G_PRE:
                return own1.at[pl.ds(8 + 12 * (s % 2), 4), pl.ds(0, ROWS_ALL), :]
            return m_stage.at[s % 2, :, pl.ds(0, ROWS_ALL), :]

        def load(s):
            return pltpu.make_async_copy(land.at[kind, s], held(s), c_sem.at[s % 2])

        exchange(kind, 1).wait()
        load(0).start()
        for s in range(3):
            if s < 2:
                exchange(kind, s + 2).wait()
                load(s + 1).start()
            load(s).wait()
            use(s + 1, held(s))

    fetch(0)
    media_rows(0).start()

    def to_rows(ref, value):
        for k in range(4):
            ref[k] = column(value, k)

    @pl.when(section == 0)
    def _():
        given = pltpu.make_async_copy(latents, lin, c_sem.at[0])
        given.start()
        given.wait()
        xs[...] = lin[...].astype(F32)

    @pl.when(section == 1)
    def _():
        given = pltpu.make_async_copy(cotangent, lin, c_sem.at[0])
        given.start()
        given.wait()
        gys[...] = lin[...].astype(F32)
        to_rows(gave.at[1], lin[...].astype(F32))
        give(G_OUT)

    def media_block(i, carry):
        @pl.when(i < 5)
        def _():
            media_rows(i + 1).start()

        media_rows(i).wait()
        normed, _ = normed_rows(m_buf[i % 2].astype(F32))
        media_in = (normed * gains[0:1, :] + biases[0:1, :]).astype(BF16)
        keyval = mm(media_in, w_keyval[...]).astype(BF16)
        for j in range(4):
            lefts[i, j] = column(keyval, j)
        return carry

    lax.fori_loop(0, 6, media_block, 0)
    for k in list(range(38)) + [R_KV + 7 * j + 6 for j in range(4)]:
        rights[k, pl.ds(192, 64), :] = jnp.zeros((64, COLS), BF16)
    row = lax.broadcasted_iota(jnp.int32, (256, COLS), 0)
    col = lax.broadcasted_iota(jnp.int32, (256, COLS), 1)
    rights[R_SMALL] = jnp.where(((row == col) & (row < 6)) | ((row == col + 6) & (row >= 6) & (row < 12)), 1.0, 0.0).astype(BF16)

    @pl.when(section == 1)
    def _():
        to_other(accs, xs, x_sem).wait_recv()

    normed, _ = normed_rows(xs[...])
    lin[...] = (normed * gains[1:2, :] + biases[1:2, :]).astype(BF16)
    qs[...] = (mm(lin[...], w_query[...]) * 0.125).astype(BF16)
    latent_kv = mm(lin[...], w_keyval[...]).astype(BF16)
    for v in range(3):
        for j in range(4):
            rows = pl.ds((v % 2) * 128, 64)
            lefts[6 + v // 2, j, rows, :] = latent_kv[64 * v : 64 * v + 64, COLS * j : COLS * j + COLS]
            lefts[6 + v // 2, j, pl.ds((v % 2) * 128 + 64, 64), :] = jnp.zeros((64, COLS), BF16)

    def keyvals_of(v, j):
        tail = pl.ds(pl.multiple_of((v % 2) * 128, 128), 128)
        return lefts[2 * v, j], lefts[2 * v + 1, j], lefts[6 + v // 2, j, tail, :]

    def attend(v, carry):
        rows = pl.ds(pl.multiple_of(v * 64, 64), 64)
        valid = mask[v] > 0.0
        for g in range(2):
            cols = pl.ds(COLS * g, COLS)
            stacked = head_stack(qs[rows, cols])
            scores = [mm_nt(stacked, k) for k in keyvals_of(v, g)]
            scores = [
                jnp.where(valid[:, 256 * n : 256 * n + s.shape[1]], s, MASK_FILL) for n, s in enumerate(scores)
            ]
            top = jnp.max(jnp.maximum(scores[0], scores[1]), -1, keepdims=True)
            top = jnp.maximum(top, jnp.max(scores[2], -1, keepdims=True))
            raised = [jnp.exp(s - top) for s in scores]
            whole = jnp.sum(raised[0] + raised[1], -1, keepdims=True) + jnp.sum(raised[2], -1, keepdims=True)
            scale = 1.0 / whole
            mixed = jnp.zeros((256, COLS), F32)
            for n, (e, values) in enumerate(zip(raised, keyvals_of(v, 2 + g))):
                p = e * scale
                own1[(v * 2 + g) * 3 + n, :, pl.ds(0, p.shape[1])] = p
                mixed += mm(p.astype(BF16), values)
            att[rows, cols] = head_merge(mixed).astype(BF16)
        return carry

    lax.fori_loop(0, 3, attend, 0)

    x1 = xs[...] + mm(att[...], w_out[...])
    x1s[...] = x1
    accs[...] = x1
    normed, _ = normed_rows(x1)
    ffin[...] = (normed * gains[2:3, :] + biases[2:3, :]).astype(BF16)
    to_rows(gave.at[0], ffin[...].astype(F32))
    give(FF_IN)

    def ff_forward(j, carry):
        fetched(j)

        @pl.when(j + 1 < FF_STEPS)
        def _():
            fetch(j + 1)

        pre = mm(ffin[...], wu[j % 2])
        act = (pre * (0.5 * (1.0 + lax.erf(pre * ROOT_HALF)))).astype(BF16)
        for k in range(2):
            pres[2 * j + k] = column(pre, k)
            own1[18 + 4 * (2 * (j % 2) + k) + j // 2, pl.ds(0, ROWS_ALL), :] = column(act, k).astype(F32)
        accs[...] += mm(act, wd[j % 2])
        return carry

    lax.fori_loop(0, FF_STEPS, ff_forward, 0)
    give(ACT)
    fetch(0)

    def turn_forward():
        for k in range(4):
            lefts[L_FF, k] = turned(gave[0, k])

        def use_ff(s, piece):
            for k in range(4):
                lefts[L_FF + s, k] = turned(piece[k])

        taken(FF_IN, use_ff)
        for k in range(4):
            lefts[L_ACT, k] = turned(own1[18 + 4 * coords[Y] + k, pl.ds(0, ROWS_ALL), :])

        def use_act(s, piece):
            for k in range(4):
                lefts[L_ACT + s, k] = turned(piece[k])

        taken(ACT, use_act)
        for i in range(4):
            part = jnp.concatenate([att[:, pl.ds(128 * i, 128)].astype(F32), jnp.zeros((64, 128), F32)], 0)
            part = part.T.reshape(16, 8, 256)
            none = jnp.zeros_like(part)
            lefts[L_ATT, i] = jnp.concatenate([part, none], 1).reshape(256, 256).astype(BF16)
            lefts[L_ATT + 1, i] = jnp.concatenate([none, part], 1).reshape(256, 256).astype(BF16)

    @pl.when(section == 0)
    def _():
        to_other(accs, xs, x_sem).start()
        turn_forward()
        to_other(accs, xs, x_sem).wait_send()
        to_other(accs, gys, g_sem).wait_recv()
        to_rows(gave.at[1], gys[...].astype(BF16).astype(F32))
        give(G_OUT)

    @pl.when(section == 1)
    def _():
        sent[...] = accs[:, pl.ds(0, 512)]
        to_other(sent, resampled, r_sem).start()
        resampled[...] = accs[:, pl.ds(512, 512)]

    ffin[...] = gys[...].astype(BF16)
    for k in range(4):
        rights[R_OUT + k, pl.ds(0, ROWS_ALL), :] = ffin[:, pl.ds(COLS * k, COLS)]
    accs[...] = jnp.zeros((ROWS_ALL, 1024), F32)

    def ff_backward(j, carry):
        fetched(j)

        @pl.when(j + 1 < FF_STEPS)
        def _():
            fetch(j + 1)

        grad_act = mm_nt(ffin[...], wd[j % 2])
        halves = []
        for k in range(2):
            pre = pres[2 * j + k]
            slope = 0.5 * (1.0 + lax.erf(pre * ROOT_HALF)) + pre * jnp.exp(-0.5 * pre * pre) * INV_ROOT_TAU
            halves.append((column(grad_act, k) * slope).astype(BF16))
            pres[2 * j + k] = halves[k].astype(F32)
        accs[...] += mm_nt(halves[0], wu[j % 2, :, pl.ds(0, 256)]) + mm_nt(halves[1], wu[j % 2, :, pl.ds(256, 256)])
        return carry

    lax.fori_loop(0, FF_STEPS, ff_backward, 0)
    give(G_PRE)

    normed, inverse = normed_rows(x1s[...])
    back, gain_sum, bias_sum = norm_back(accs[...], normed, inverse, gains[2:3, :])
    sums[pl.ds(2, 1), :] = gain_sum
    sums[pl.ds(5, 1), :] = bias_sum
    grad_x1 = gys[...] + back
    gys[...] = grad_x1
    grad_attn = grad_x1.astype(BF16)
    for k in range(4):
        rights[R_ATT + k, pl.ds(0, ROWS_ALL), :] = column(grad_attn, k)
    gatt[...] = mm_nt(grad_attn, w_out[...]).astype(BF16)

    def attend_back(v, carry):
        rows = pl.ds(pl.multiple_of(v * 64, 64), 64)
        for g in range(2):
            cols = pl.ds(COLS * g, COLS)
            q_stack = head_stack(qs[rows, cols])
            g_stack = head_stack(gatt[rows, cols])
            widths = (256, 256, 128)
            probs = [own1[(v * 2 + g) * 3 + n, :, pl.ds(0, widths[n])] for n in range(3)]
            weighted = [p * mm_nt(g_stack, values) for p, values in zip(probs, keyvals_of(v, 2 + g))]
            whole = jnp.sum(weighted[0] + weighted[1], -1, keepdims=True) + jnp.sum(weighted[2], -1, keepdims=True)
            grad_s = [(w - p * whole).astype(BF16) for w, p in zip(weighted, probs)]
            grad_q = sum(mm(s, k) for s, k in zip(grad_s, keyvals_of(v, g)))
            rights[R_QUERY + g, rows, :] = head_merge(grad_q).astype(BF16)
            for base, factors, stack in (
                (R_KV + 7 * g, grad_s, q_stack),
                (R_KV + 14 + 7 * g, [p.astype(BF16) for p in probs], g_stack),
            ):
                rights[base + 2 * v] = mm_tn(factors[0], stack).astype(BF16)
                rights[base + 2 * v + 1] = mm_tn(factors[1], stack).astype(BF16)
                rights[base + 6, rows, :] = mm_tn(factors[2], stack)[:64].astype(BF16)
        return carry

    lax.fori_loop(0, 3, attend_back, 0)

    grad_in = sum(mm_nt(rights[R_QUERY + g, pl.ds(0, ROWS_ALL), :], w_query[:, pl.ds(COLS * g, COLS)]) for g in range(2))
    grad_in = grad_in * 0.125
    for k in range(4):
        grad_in += mm_nt(rights[R_KV + 6 + 7 * k, pl.ds(0, ROWS_ALL), :], w_keyval[:, pl.ds(COLS * k, COLS)])
    normed, inverse = normed_rows(xs[...])
    back, gain_sum, bias_sum = norm_back(grad_in, normed, inverse, gains[1:2, :])
    sums[pl.ds(1, 1), :] = gain_sum
    sums[pl.ds(4, 1), :] = bias_sum
    accs[...] = gys[...] + back

    @pl.when(section == 1)
    def _():
        to_other(accs, gys, g_sem).start()
        turn_forward()

    @pl.when(section == 0)
    def _():
        sent[...] = accs[:, pl.ds(512, 512)]
        to_other(sent, latents_grad, l_sem).start()
        latents_grad[...] = accs[:, pl.ds(0, 512)]

    def use_out(s, piece):
        for k in range(4):
            rights[R_OUT + 4 * s + k, pl.ds(0, ROWS_ALL), :] = piece[k].astype(BF16)

    taken(G_OUT, use_out)

    def turn_pre():
        for k in range(4):
            rights[R_PRE + k, pl.ds(0, ROWS_ALL), :] = pres[4 * coords[X] + k].astype(BF16)

        def use_pre(s, piece):
            for k in range(4):
                rights[R_PRE + 4 * s + k, pl.ds(0, ROWS_ALL), :] = piece[k].astype(BF16)

        taken(G_PRE, use_pre)

    def media_away(i):
        return pltpu.make_async_remote_copy(
            src_ref=m_stage.at[i % 2, pl.ds(2 * other, 2)], dst_ref=m_got.at[i], send_sem=m_send.at[i], recv_sem=m_recv.at[i],
            device_id={"section": other}, device_id_type=MESH,
        )

    def media_home(i):
        return pltpu.make_async_copy(m_stage.at[i % 2, pl.ds(2 * section, 2)], m_own.at[i], m_local.at[i])

    def media_back(i):
        if i < 5:
            media_rows(i + 1).start()
        media_rows(i).wait()
        if i >= 2:
            media_away(i - 2).wait_send()
            media_home(i - 2).wait()
        normed, inverse = normed_rows(m_buf[i % 2].astype(F32))
        media_in = normed * gains[0:1, :] + biases[0:1, :]
        grad_media = mm_nt(rights[R_KV + i], w_keyval[:, pl.ds(0, COLS)])
        for k in range(1, 4):
            grad_media += mm_nt(rights[R_KV + 7 * k + i], w_keyval[:, pl.ds(COLS * k, COLS)])
        back, gain_sum, bias_sum = norm_back(grad_media, normed, inverse, gains[0:1, :])
        if i == 0:
            sums[pl.ds(0, 1), :] = gain_sum
            sums[pl.ds(3, 1), :] = bias_sum
        else:
            sums[pl.ds(0, 1), :] += gain_sum
            sums[pl.ds(3, 1), :] += bias_sum
        for k in range(4):
            m_stage[i % 2, k] = column(back, k)
        media_away(i).start()
        media_home(i).start()
        for k in range(4):
            lefts[i, k] = turned(column(media_in, k).astype(BF16).astype(F32))

    def small_left():
        total = sums[pl.ds(0, 6), :]
        high = total.astype(BF16).astype(F32)
        block = jnp.concatenate([high, total - high, jnp.zeros((244, 1024), F32)], 0)
        for k in range(4):
            lefts[L_SMALL, k] = turned(column(block, k))

    def factors(what, which):
        if what == "up":
            return [(L_FF + s, R_PRE + 4 * s + which) for s in range(4)]
        if what == "down":
            return [(L_ACT + s, R_OUT + 4 * s + which) for s in range(4)]
        if what == "out":
            return [(L_ATT + s, R_ATT + 2 * which + s) for s in range(2)]
        if what == "query":
            return [(L_LATENT, R_QUERY + which)]
        if what == "small":
            return [(L_SMALL, R_SMALL)]
        return [(k, R_KV + 7 * which + k) for k in range(7)]

    own = (own1, own2, own3)
    far = (far1, far2, far3)
    near = (near1, near2, near3)

    def spot(lane, group):
        return (lane * 3 + group % 3) * 4

    def terms(lane, group):
        what, which, _, order = PLAN[lane][group]
        base = spot(lane, group)

        def block(i, carry):
            total = sum(mm(lefts[a, i], rights[b]) for a, b in factors(what, which))
            if order == ABC:
                own1[base + i] = total
            else:
                for b in range(4):
                    for c in range(4):
                        first, second, third = [(i, b, c)[n] for n in order]
                        rows = pl.ds(pl.multiple_of((second * 4 + third) * 16, 16), 16)
                        own1[base + first, rows, :] = total[(b * 4 + c) * 16 : (b * 4 + c) * 16 + 16]
            return carry

        lax.fori_loop(0, 4, block, 0)

    def ring_copy(lane, group, stage, step, way):
        axis = PLAN[lane][group][2][stage]
        half = RING_ROWS[stage] // 2
        shift = 1 if way == 0 else 3
        turn = group % 3 if stage == 0 and step == 0 else group % 2
        sem = (((lane * 3 + stage) * 2 + step) * 2 + way) * 3 + turn
        if step == 0:
            source = own[stage].at[spot(lane, group) + at(axis, 2), pl.ds(way * half, half)]
            target = far[stage].at[lane, way, turn]
        else:
            source = own[stage].at[spot(lane, group) + at(axis, shift)]
            target = near[stage].at[lane, way, turn]
        return pltpu.make_async_remote_copy(
            src_ref=source, dst_ref=target, send_sem=t_send.at[sem], recv_sem=t_recv.at[sem],
            device_id={"dp": peer(axis, shift)}, device_id_type=MESH,
        )

    def runs(lane, group, stage):
        return 0 <= group < GROUPS and PLAN[lane][group] is not None and stage < len(PLAN[lane][group][2])

    def up_copy(shift):
        rows = pl.ds(pl.multiple_of(16 * at(X, shift), 16), 16)
        return pltpu.make_async_remote_copy(
            src_ref=up_sum.at[rows, :], dst_ref=up_got.at[shift - 1], send_sem=u_send.at[shift - 1], recv_sem=u_recv.at[shift - 1],
            device_id={"dp": peer(X, shift)}, device_id_type=MESH,
        )

    def finish(what, which, total):
        cols = pl.ds(COLS * which, COLS)
        if what == "up":
            up_sum[:, cols] = total
        elif what == "down":
            out_down[:, cols] = total
        elif what == "query":
            out_query[:, cols] = total * 0.125
        elif what == "keyval":
            out_keyval[:, cols] = total
        elif what == "out":
            out_out[:, pl.ds(512 * which, COLS)] = total[:8]
            out_out[:, pl.ds(512 * which + COLS, COLS)] = total[8:]
        else:
            out_small[...] = total

    for k in range(4):
        lefts[L_LATENT, k] = turned(lin[:, pl.ds(COLS * k, COLS)].astype(F32))
    media_rows(0).start()
    ups = 0
    for t in range(TICKS):
        for lane in range(3):
            if runs(lane, t, 0):
                terms(lane, t)
                for way in range(2):
                    ring_copy(lane, t, 0, 0, way).start()
        if t == 0:
            media_back(0)
            turn_pre()
        if t == 1:
            media_back(1)
            media_back(2)
        if t == 2:
            media_back(3)
            media_back(4)
        if t == 3:
            media_back(5)
            small_left()
        for stage in range(3):
            for lane in range(3):
                half = RING_ROWS[stage] // 2
                group = t - 1 - 2 * stage
                if runs(lane, group, stage):
                    axis = PLAN[lane][group][2][stage]
                    turn = group % 3 if stage == 0 else group % 2
                    for way in range(2):
                        ring_copy(lane, group, stage, 0, way).wait()
                        own[stage][spot(lane, group) + at(axis, 1 if way == 0 else 3), pl.ds(way * half, half), :] += far[stage][
                            lane, way, turn
                        ]
                group = t - 2 - 2 * stage
                if runs(lane, group, stage):
                    what, which, axes, _ = PLAN[lane][group]
                    for way in range(2):
                        ring_copy(lane, group, stage, 1, way).wait()
                    total = (
                        own[stage][spot(lane, group) + at(axes[stage], 0)]
                        + near[stage][lane, 0, group % 2]
                        + near[stage][lane, 1, group % 2]
                    )
                    if stage + 1 < len(axes):
                        rows = RING_ROWS[stage + 1]
                        for k in range(4):
                            own[stage + 1][spot(lane, group) + k] = total[rows * k : rows * k + rows]
                    else:
                        finish(what, which, total)
                        if what == "up":
                            ups += 1
                            if ups == 4:
                                for shift in (1, 2, 3):
                                    up_copy(shift).start()
        for stage in range(3):
            for lane in range(3):
                if stage > 0 and runs(lane, t - 2 * stage, stage):
                    for way in range(2):
                        ring_copy(lane, t - 2 * stage, stage, 0, way).start()
                if runs(lane, t - 1 - 2 * stage, stage):
                    for way in range(2):
                        ring_copy(lane, t - 1 - 2 * stage, stage, 1, way).start()

    for s in range(4):
        part = up_sum[pl.ds(pl.multiple_of(16 * coords[X], 16), 16), :] if s == 0 else None
        if s > 0:
            up_copy(s).wait()
            part = up_got[s - 1]
        cols = pl.ds(pl.multiple_of(1024 * at(X, 4 - s), 1024), 1024)
        out_up[:, cols] = part

    for i in (4, 5):
        media_away(i).wait_send()
        media_home(i).wait()
    for i in range(6):
        media_away(i).wait_recv()

    @pl.when(section == 0)
    def _():
        to_other(sent, resampled, r_sem).wait_recv()
        to_other(sent, latents_grad, l_sem).wait_send()

    @pl.when(section == 1)
    def _():
        to_other(sent, resampled, r_sem).wait_send()
        to_other(accs, gys, g_sem).wait_send()
        to_other(sent, latents_grad, l_sem).wait_recv()


def run_resampler(latents, media, mask, gains, biases, w_query, w_keyval, w_out, w_up, w_down, cotangent):
    vmem = pl.BlockSpec(memory_space=pltpu.VMEM)
    hbm = pl.BlockSpec(memory_space=pl.ANY)

    def sds(*shape):
        return jax.ShapeDtypeStruct(shape, F32)

    dma = pltpu.SemaphoreType.DMA
    return pl.pallas_call(
        resampler_kernel,
        out_shape=[
            sds(192, 512), sds(192, 512), sds(16, 256), sds(16, 512), sds(16, 1024), sds(8, 1024), sds(16, 4096), sds(64, 1024),
            sds(6, 2, 256, 256), sds(6, 2, 256, 256), sds(4, 3, 4, 192, 256),
        ],
        in_specs=[hbm, hbm] + [vmem] * 6 + [hbm, hbm, hbm],
        out_specs=[vmem] * 8 + [hbm] * 3,
        scratch_shapes=[
            pltpu.VMEM((192, 1024), F32),
            pltpu.VMEM((192, 1024), F32),
            pltpu.VMEM((192, 1024), F32),
            pltpu.VMEM((192, 1024), F32),
            pltpu.VMEM((192, 1024), BF16),
            pltpu.VMEM((192, 1024), BF16),
            pltpu.VMEM((192, 512), BF16),
            pltpu.VMEM((192, 512), BF16),
            pltpu.VMEM((192, 512), BF16),
            pltpu.VMEM((16, 192, 256), F32),
            pltpu.VMEM((8, 1024), F32),
            pltpu.VMEM((192, 512), F32),
            pltpu.VMEM((2, 4, 256, 256), F32),
            pltpu.VMEM((2, 256, 1024), BF16),
            pltpu.VMEM((2, 1024, 512), BF16),
            pltpu.VMEM((2, 512, 1024), BF16),
            pltpu.VMEM((2, 4, 192, 256), F32),
            pltpu.VMEM((18, 4, 256, 256), BF16),
            pltpu.VMEM((67, 256, 256), BF16),
        ]
        + [pltpu.VMEM((36, r, COLS), F32) for r in RING_ROWS]
        + [pltpu.VMEM((3, 2, 3 if r == 256 else 2, r // 2, COLS), F32) for r in RING_ROWS]
        + [pltpu.VMEM((3, 2, 2, r, COLS), F32) for r in RING_ROWS]
        + [
            pltpu.VMEM((64, 1024), F32),
            pltpu.VMEM((3, 16, 1024), F32),
            dma((2, 2)), dma((2,)), dma((2,)), dma((2,)), dma((2,)), dma((2,)), dma((6,)), dma((6,)), dma((6,)),
            dma((4, 3)), dma((4, 3)), dma((2,)), dma((108,)), dma((108,)), dma((3,)), dma((3,)),
        ],
        compiler_params=pltpu.CompilerParams(collective_id=1, has_side_effects=True, vmem_limit_bytes=VMEM_BYTES),
        name="resampler",
    )(latents, media, mask, gains, biases, w_query, w_keyval, w_out, w_up, w_down, cotangent)


def body(
    latents_in, media, frame_count, gains, biases, w_query, w_keyval, w_out, w_up, w_down, cotangent
):
    key = jnp.arange(KEYS)
    valid = (key[None] < 64 * frame_count) | ((key[None] >= 512) & (key[None] < 576))
    mask = valid.astype(F32)[:, None, :]
    resampled, latents_grad, small, query, keyval, out, up, down, mine, theirs, _ = run_resampler(
        latents_in.reshape(192, 1024), media.reshape(1536, 1024), mask, gains[0], biases[0],
        w_query[0], w_keyval[0], w_out[0], w_up[0], w_down[0], cotangent.reshape(192, 1024),
    )
    small = small[:, :6].T
    return (
        resampled.reshape(3, 1, 64, 512),
        latents_grad.reshape(3, 1, 64, 512),
        (mine + theirs).transpose(0, 2, 1, 3).reshape(3, 1, 512, 512),
        small[None, :3],
        small[None, 3:],
        query[None],
        keyval[None],
        out[None],
        up[None],
        down[None],
    )


def solution(mesh):
    placed = (
        P(None, "dp", None, None),
        P(None, "dp", None, None),
        P(None, "dp"),
        P("section", None, None),
        P("section", None, None),
        P("section", None, None),
        P("section", None, None),
        P("section", None, None),
        P("section", None, None),
        P("section", None, None),
        P(None, "dp", None, None),
    )
    return jax.shard_map(
        body,
        mesh=mesh,
        in_specs=placed,
        out_specs=(
            P(None, "dp", None, "section"),
            P(None, "dp", None, "section"),
            P(None, "dp", None, "section"),
            P("section", None, "dp"),
            P("section", None, "dp"),
            P("section", "dp", None),
            P("section", "dp", None),
            P("section", "dp", None),
            P("section", "dp", None),
            P("section", "dp", None),
        ),
        check_vma=False,
    )
```

time: 321 us -> 224 us (0.70)
  Pallas kernels: 306 us -> 198 us
  local copies, waits for them, and re-layouts: 11.3 us -> 19.5 us
    pallas_call x2 -> x1, Pallas kernels: 306 us -> 198 us  [run_resampler(): pl.pallas_call(resampler_kernel, out_shape=[sds(192, 512), sds(192, 512),...]
    unnamed x10 -> x12, local copies, waits for them, and re-layouts: 7.83 us -> 12.7 us
    transpose x0 -> x1, other arithmetic: none -> 3.32 us  [body(): (mine + theirs).transpose(0, 2, 1, 3).reshape(3, 1, 512, 512)]
where the time goes in v3:
time: 224 us; the launch traced here: 222 us
  Pallas kernels  198 us (88%)
  local copies, waits for them, and re-layouts  19.5 us (9%)
  other arithmetic  4.65 us (2%)
    pallas_call x1, Pallas kernels, run_resampler(): pl.pallas_call(resampler_kernel, out_shape=[sds(192, 512), sds(192, 512),...  198 us
    unnamed x12, local copies, waits for them, and re-layouts  12.7 us

profile of v3, /device:TPU:0, one launch (start us, length us, event | category | flops | bytes accessed | tf_op | source)
XLA Modules:
  0.0 222.5 jit_solution(2314571860468270268)
XLA Ops:
  0.6 0.7 multiply_bitcast_fusion
  1.3 0.7 or_convert_fusion.mask
  2.0 1.3 copy_bitcast_fusion
  3.3 197.6 %resampler.1 = (f32[192,512]{1,0:T(8,128)}, f32[192,512]{1,0:T(8,128)}, f32[16,256]{1,0:T(8,128)}, f32[16,512]{1,0:T(8,128)}, f32[16,1024]{1,0:T(8,128)}, /*inde...) custom-call(bf16[192,1024]{1,0:T(8,128)(2,1)} %bitcast.43, ...), custom_call_target="tpu_custom_call" | custom-call | tf_op jit(solution)/shard_map/resampler/pallas_call | solution.py:664
  201.0 0.7 slice_bitcast_fusion.2
  201.7 0.1 slice_bitcast_fusion
  201.7 0.6 copy.34
  202.4 0.6 copy.33
  203.0 3.3 %add_bitcast_fusion = f32[6,256,2,256]{3,1,2,0:T(8,128)S(1)} fusion(f32[6,2,256,256]{3,2,1,0:T(8,128)} %get-tuple-element.22, f32[6,2,256,256]{3,2,1,0:T(8,128)} %get-tuple-element.23), kind=kLoop, calls=%fused_computation | loop fusion | flops 786432 | bytes 9437184 | tf_op jit(solution)/shard_map/transpose | solution.py:721
  206.3 2.4 %copy.27 = f32[6,256,2,256]{3,2,1,0:T(2,128)S(1)} copy(f32[6,256,2,256]{3,1,2,0:T(8,128)S(1)} %add_bitcast_fusion) | data formatting | bytes 6291456 | tf_op jit(solution)/shard_map/transpose | solution.py:721
  208.8 0.0 copy-start
  208.8 3.6 %reshape.111 = f32[3,1,512,512]{3,2,0,1:T(8,128)} reshape(f32[6,256,2,256]{3,2,1,0:T(2,128)S(1)} %copy.27) | data formatting | bytes 6291456 | tf_op jit(solution)/shard_map/reshape | solution.py:721
  212.4 1.8 copy.50
  214.2 0.0 copy-done
  214.2 0.7 copy.51
  214.9 1.4 copy.52
  216.3 1.5 copy.53
  217.8 1.4 copy.54
  219.2 1.7 copy.55
  220.8 1.7 copy.56
  (1 shorter events, 0.0 us)
Async XLA Ops:
  208.8 5.4 %copy-start = (f32[192,512]{1,0:T(8,128)S(1)}, f32[192,512]{1,0:T(8,128)}, u32[]{:S(2)}) copy-start(f32[192,512]{1,0:T(8,128)} %get-tuple-element.21) | copy-start | bytes 1179652

commit v4 on v3

--- a/solution.py
+++ b/solution.py
@@ -18,39 +18,41 @@
 FF_STEPS = 8
 RING_ROWS = (256, 64, 16)
 COLS = 256
-X, Y, Z = 0, 1, 2
+A, B, C = 0, 1, 2
 FF_IN, ACT, G_OUT, G_PRE = 0, 1, 2, 3
 L_LATENT, L_SMALL, L_FF, L_ACT, L_ATT = 6, 7, 8, 12, 16
 R_PRE, R_OUT, R_ATT, R_QUERY, R_SMALL, R_KV = 0, 16, 32, 36, 38, 39
-ABC, BCA, CBA, BAC = (0, 1, 2), (1, 2, 0), (2, 1, 0), (1, 0, 2)
 PLAN = (
     (
-        ("down", 0, (X, Z), ABC),
-        ("down", 1, (X, Z), ABC),
-        ("query", 0, (X, Y, Z), ABC),
-        ("query", 1, (X, Y, Z), ABC),
-        ("keyval", 0, (X, Y, Z), ABC),
-        ("keyval", 2, (X, Y, Z), ABC),
+        ("down", 0, (A, C)),
+        ("query", 0, (A, B, C)),
+        ("query", 1, (A, B, C)),
+        ("keyval", 0, (A, B, C)),
+        ("keyval", 2, (A, B, C)),
+        ("down", 1, (A, C)),
     ),
     (
-        ("out", 0, (Y, Z, X), BCA),
-        ("out", 1, (Y, Z, X), BCA),
-        ("up", 0, (Y, Z), BCA),
-        ("up", 1, (Y, Z), BCA),
-        ("keyval", 1, (Y, Z, X), BCA),
-        ("keyval", 3, (Y, Z, X), BCA),
+        ("out", 0, (B, C, A)),
+        ("up", 0, (B, C)),
+        ("up", 1, (B, C)),
+        ("keyval", 1, (B, C, A)),
+        ("keyval", 3, (B, C, A)),
+        None,
     ),
     (
-        ("down", 2, (Z, X), BAC),
-        ("down", 3, (Z, X), BAC),
-        ("up", 2, (Z, Y), CBA),
-        ("up", 3, (Z, Y), CBA),
-        ("small", 0, (Z, Y, X), CBA),
-        None,
+        ("out", 1, (C, B, A)),
+        ("down", 2, (C, A)),
+        ("up", 2, (C, B)),
+        ("up", 3, (C, B)),
+        ("small", 0, (C, B, A)),
+        ("down", 3, (C, A)),
     ),
 )
 GROUPS = 6
-TICKS = GROUPS + 6
+TICKS = GROUPS + 4
+WIDE = 4
+DEEP = 3
+WU_BASE = 35
 
 
 def mm(left, right):
@@ -102,17 +104,22 @@
 
 
 def resampler_kernel(
-    latents, media, mask, gains, biases, w_query, w_keyval, w_out, w_up, w_down, cotangent,
+    latents, media, frame_count, gains, biases, w_query, w_keyval, w_out, w_up, w_down, cotangent,
     resampled, latents_grad, out_small, out_query, out_keyval, out_out, out_up, out_down, m_own, m_got, land,
-    xs, x1s, gys, accs, lin, ffin, qs, att, gatt, pres, sums, sent, m_stage, m_buf, wu, wd, gave,
-    lefts, rights, own1, own2, own3, far1, far2, far3, near1, near2, near3, up_sum, up_got,
-    w_sem, b_sem, x_sem, g_sem, r_sem, l_sem, m_send, m_recv, m_local, e_send, e_recv, c_sem, t_send, t_recv, u_send, u_recv,
+    wq, wkv, wo, xs, x1s, gys, accs, lin, ffin, qs, att, gatt, pres, sums, sent, m_stage, m_buf, wd, gave,
+    lefts, rights, own1, own2, own3, far1, far2, mine1, summed1, near2, last, up_sum, up_got,
+    a_sem, w_sem, b_sem, x_sem, g_sem, r_sem, l_sem, m_send, m_recv, m_local, e_send, e_recv, c_sem, t_send, t_recv, z_send, z_recv, u_send, u_recv,
 ):
     section = lax.axis_index("section")
     other = 1 - section
     me = lax.axis_index("dp")
-    coords = (me // 16, (me // 4) % 4, me % 4)
-    strides = (16, 4, 1)
+    x, y, z = me // 16, (me // 4) % 4, me % 4
+
+    def by_section(first, second):
+        return first + section * (second - first)
+
+    coords = (by_section(x, z), by_section(y, x), by_section(z, y))
+    strides = (by_section(16, 1), by_section(4, 16), by_section(1, 4))
 
     def at(axis, shift):
         return (coords[axis] + shift) % 4
@@ -120,9 +127,12 @@
     def peer(axis, shift):
         return me + (at(axis, shift) - coords[axis]) * strides[axis]
 
+    held = [pltpu.make_async_copy(*pair, a_sem.at[n]) for n, pair in enumerate(((w_keyval, wkv), (w_query, wq), (w_out, wo)))]
+    for c in held:
+        c.start()
     barrier = pltpu.get_barrier_semaphore()
     pl.semaphore_signal(barrier, inc=1, device_id={"section": other}, device_id_type=MESH)
-    greeted = [(X, 1), (X, 2), (X, 3), (Y, 1), (Y, 2), (Y, 3), (Z, 1), (Z, 3)]
+    greeted = [(axis, shift) for axis in (A, B, C) for shift in (1, 2, 3)]
     for axis, shift in greeted:
         pl.semaphore_signal(barrier, inc=1, device_id={"dp": peer(axis, shift)}, device_id_type=MESH)
     pl.semaphore_wait(barrier, 1 + len(greeted))
@@ -133,17 +143,30 @@
             device_id={"section": other}, device_id_type=MESH,
         )
 
+    def up_block(step):
+        return WU_BASE + 8 * (step % WIDE)
+
     def weights(step):
-        slot = step % 2
-        cols = pl.ds(pl.multiple_of(step * 512, 512), 512)
-        return (
-            pltpu.make_async_copy(w_up.at[:, cols], wu.at[slot], w_sem.at[0, slot]),
-            pltpu.make_async_copy(w_down.at[cols, :], wd.at[slot], w_sem.at[1, slot]),
-        )
+        copies = [pltpu.make_async_copy(w_down.at[pl.ds(pl.multiple_of(step * 512, 512), 512), :], wd.at[step % DEEP], w_sem.at[2, step % DEEP])]
+        for k in range(2):
+            cols = pl.ds(pl.multiple_of(step * 512 + COLS * k, COLS), COLS)
+            copies.append(
+                pltpu.make_async_copy(w_up.at[:, :, cols], rights.at[pl.ds(up_block(step) + 4 * k, 4)], w_sem.at[k, step % WIDE])
+            )
+        return copies
 
     def fetch(step):
         for c in weights(step):
             c.start()
+
+    def fetch_first():
+        for step in range(DEEP - 1):
+            fetch(step)
+
+    def fetch_next(step):
+        @pl.when(step + DEEP - 1 < FF_STEPS)
+        def _():
+            fetch(step + DEEP - 1)
 
     def fetched(step):
         for c in weights(step):
@@ -155,7 +178,7 @@
         )
 
     def exchange(kind, shift):
-        axis = X if kind in (FF_IN, G_PRE) else Y
+        axis = A if kind in (FF_IN, G_PRE) else B
         if kind == FF_IN:
             source = gave.at[0]
         elif kind == G_OUT:
@@ -191,7 +214,7 @@
             load(s).wait()
             use(s + 1, held(s))
 
-    fetch(0)
+    fetch_first()
     media_rows(0).start()
 
     def to_rows(ref, value):
@@ -221,27 +244,24 @@
 
         media_rows(i).wait()
         normed, _ = normed_rows(m_buf[i % 2].astype(F32))
-        media_in = (normed * gains[0:1, :] + biases[0:1, :]).astype(BF16)
-        keyval = mm(media_in, w_keyval[...]).astype(BF16)
+        media_in = (normed * gains[0, 0:1, :] + biases[0, 0:1, :]).astype(BF16)
+        keyval = mm(media_in, wkv[0]).astype(BF16)
         for j in range(4):
             lefts[i, j] = column(keyval, j)
         return carry
 
+    held[0].wait()
     lax.fori_loop(0, 6, media_block, 0)
-    for k in list(range(38)) + [R_KV + 7 * j + 6 for j in range(4)]:
-        rights[k, pl.ds(192, 64), :] = jnp.zeros((64, COLS), BF16)
-    row = lax.broadcasted_iota(jnp.int32, (256, COLS), 0)
-    col = lax.broadcasted_iota(jnp.int32, (256, COLS), 1)
-    rights[R_SMALL] = jnp.where(((row == col) & (row < 6)) | ((row == col + 6) & (row >= 6) & (row < 12)), 1.0, 0.0).astype(BF16)
-
+    held[1].wait()
+    held[2].wait()
     @pl.when(section == 1)
     def _():
         to_other(accs, xs, x_sem).wait_recv()
 
     normed, _ = normed_rows(xs[...])
-    lin[...] = (normed * gains[1:2, :] + biases[1:2, :]).astype(BF16)
-    qs[...] = (mm(lin[...], w_query[...]) * 0.125).astype(BF16)
-    latent_kv = mm(lin[...], w_keyval[...]).astype(BF16)
+    lin[...] = (normed * gains[0, 1:2, :] + biases[0, 1:2, :]).astype(BF16)
+    qs[...] = (mm(lin[...], wq[0]) * 0.125).astype(BF16)
+    latent_kv = mm(lin[...], wkv[0]).astype(BF16)
     for v in range(3):
         for j in range(4):
             rows = pl.ds((v % 2) * 128, 64)
@@ -252,9 +272,11 @@
         tail = pl.ds(pl.multiple_of((v % 2) * 128, 128), 128)
         return lefts[2 * v, j], lefts[2 * v + 1, j], lefts[6 + v // 2, j, tail, :]
 
+    key = lax.broadcasted_iota(jnp.int32, (1, KEYS), 1)
+
     def attend(v, carry):
         rows = pl.ds(pl.multiple_of(v * 64, 64), 64)
-        valid = mask[v] > 0.0
+        valid = (key < 64 * frame_count[v, 0]) | ((key >= 512) & (key < 576))
         for g in range(2):
             cols = pl.ds(COLS * g, COLS)
             stacked = head_stack(qs[rows, cols])
@@ -277,32 +299,31 @@
 
     lax.fori_loop(0, 3, attend, 0)
 
-    x1 = xs[...] + mm(att[...], w_out[...])
+    x1 = xs[...] + mm(att[...], wo[0])
     x1s[...] = x1
     accs[...] = x1
     normed, _ = normed_rows(x1)
-    ffin[...] = (normed * gains[2:3, :] + biases[2:3, :]).astype(BF16)
+    ffin[...] = (normed * gains[0, 2:3, :] + biases[0, 2:3, :]).astype(BF16)
     to_rows(gave.at[0], ffin[...].astype(F32))
     give(FF_IN)
 
     def ff_forward(j, carry):
         fetched(j)
-
-        @pl.when(j + 1 < FF_STEPS)
-        def _():
-            fetch(j + 1)
-
-        pre = mm(ffin[...], wu[j % 2])
-        act = (pre * (0.5 * (1.0 + lax.erf(pre * ROOT_HALF)))).astype(BF16)
+        fetch_next(j)
+        acts = []
         for k in range(2):
-            pres[2 * j + k] = column(pre, k)
-            own1[18 + 4 * (2 * (j % 2) + k) + j // 2, pl.ds(0, ROWS_ALL), :] = column(act, k).astype(F32)
-        accs[...] += mm(act, wd[j % 2])
+            base = up_block(j) + 4 * k
+            pre = sum(mm(ffin[:, pl.ds(COLS * r, COLS)], rights[base + r]) for r in range(4))
+            act = (pre * (0.5 * (1.0 + lax.erf(pre * ROOT_HALF)))).astype(BF16)
+            pres[2 * j + k] = pre
+            own1[18 + by_section(4 * (2 * (j % 2) + k) + j // 2, 2 * j + k), pl.ds(0, ROWS_ALL), :] = act.astype(F32)
+            acts.append(act)
+        accs[...] += mm(jnp.concatenate(acts, 1), wd[j % DEEP])
         return carry
 
     lax.fori_loop(0, FF_STEPS, ff_forward, 0)
     give(ACT)
-    fetch(0)
+    fetch_first()
 
     def turn_forward():
         for k in range(4):
@@ -314,7 +335,7 @@
 
         taken(FF_IN, use_ff)
         for k in range(4):
-            lefts[L_ACT, k] = turned(own1[18 + 4 * coords[Y] + k, pl.ds(0, ROWS_ALL), :])
+            lefts[L_ACT, k] = turned(own1[18 + 4 * coords[B] + k, pl.ds(0, ROWS_ALL), :])
 
         def use_act(s, piece):
             for k in range(4):
@@ -344,32 +365,41 @@
         resampled[...] = accs[:, pl.ds(512, 512)]
 
     ffin[...] = gys[...].astype(BF16)
-    for k in range(4):
-        rights[R_OUT + k, pl.ds(0, ROWS_ALL), :] = ffin[:, pl.ds(COLS * k, COLS)]
     accs[...] = jnp.zeros((ROWS_ALL, 1024), F32)
 
     def ff_backward(j, carry):
         fetched(j)
-
-        @pl.when(j + 1 < FF_STEPS)
-        def _():
-            fetch(j + 1)
-
-        grad_act = mm_nt(ffin[...], wd[j % 2])
+        fetch_next(j)
+        grad_act = mm_nt(ffin[...], wd[j % DEEP])
         halves = []
         for k in range(2):
             pre = pres[2 * j + k]
             slope = 0.5 * (1.0 + lax.erf(pre * ROOT_HALF)) + pre * jnp.exp(-0.5 * pre * pre) * INV_ROOT_TAU
             halves.append((column(grad_act, k) * slope).astype(BF16))
             pres[2 * j + k] = halves[k].astype(F32)
-        accs[...] += mm_nt(halves[0], wu[j % 2, :, pl.ds(0, 256)]) + mm_nt(halves[1], wu[j % 2, :, pl.ds(256, 256)])
+        base = up_block(j)
+        for r in range(4):
+            accs[:, pl.ds(COLS * r, COLS)] += mm_nt(halves[0], rights[base + r]) + mm_nt(halves[1], rights[base + 4 + r])
+        quarter = j // 2
+        shift = (quarter - coords[A] + 4) % 4
+
+        @pl.when((j % 2 == 1) & (shift != 0))
+        def _():
+            exchange(G_PRE, shift).start()
+
         return carry
 
     lax.fori_loop(0, FF_STEPS, ff_backward, 0)
-    give(G_PRE)
+    for k in list(range(38)) + [R_KV + 7 * j + 6 for j in range(4)]:
+        rights[k, pl.ds(192, 64), :] = jnp.zeros((64, COLS), BF16)
+    for k in range(4):
+        rights[R_OUT + k, pl.ds(0, ROWS_ALL), :] = ffin[:, pl.ds(COLS * k, COLS)]
+    row = lax.broadcasted_iota(jnp.int32, (256, COLS), 0)
+    col = lax.broadcasted_iota(jnp.int32, (256, COLS), 1)
+    rights[R_SMALL] = jnp.where(((row == col) & (row < 6)) | ((row == col + 6) & (row >= 6) & (row < 12)), 1.0, 0.0).astype(BF16)
 
     normed, inverse = normed_rows(x1s[...])
-    back, gain_sum, bias_sum = norm_back(accs[...], normed, inverse, gains[2:3, :])
+    back, gain_sum, bias_sum = norm_back(accs[...], normed, inverse, gains[0, 2:3, :])
     sums[pl.ds(2, 1), :] = gain_sum
     sums[pl.ds(5, 1), :] = bias_sum
     grad_x1 = gys[...] + back
@@ -377,7 +407,7 @@
     grad_attn = grad_x1.astype(BF16)
     for k in range(4):
         rights[R_ATT + k, pl.ds(0, ROWS_ALL), :] = column(grad_attn, k)
-    gatt[...] = mm_nt(grad_attn, w_out[...]).astype(BF16)
+    gatt[...] = mm_nt(grad_attn, wo[0]).astype(BF16)
 
     def attend_back(v, carry):
         rows = pl.ds(pl.multiple_of(v * 64, 64), 64)
@@ -403,12 +433,12 @@
 
     lax.fori_loop(0, 3, attend_back, 0)
 
-    grad_in = sum(mm_nt(rights[R_QUERY + g, pl.ds(0, ROWS_ALL), :], w_query[:, pl.ds(COLS * g, COLS)]) for g in range(2))
+    grad_in = sum(mm_nt(rights[R_QUERY + g, pl.ds(0, ROWS_ALL), :], wq[0, :, pl.ds(COLS * g, COLS)]) for g in range(2))
     grad_in = grad_in * 0.125
     for k in range(4):
-        grad_in += mm_nt(rights[R_KV + 6 + 7 * k, pl.ds(0, ROWS_ALL), :], w_keyval[:, pl.ds(COLS * k, COLS)])
+        grad_in += mm_nt(rights[R_KV + 6 + 7 * k, pl.ds(0, ROWS_ALL), :], wkv[0, :, pl.ds(COLS * k, COLS)])
     normed, inverse = normed_rows(xs[...])
-    back, gain_sum, bias_sum = norm_back(grad_in, normed, inverse, gains[1:2, :])
+    back, gain_sum, bias_sum = norm_back(grad_in, normed, inverse, gains[0, 1:2, :])
     sums[pl.ds(1, 1), :] = gain_sum
     sums[pl.ds(4, 1), :] = bias_sum
     accs[...] = gys[...] + back
@@ -432,7 +462,7 @@
 
     def turn_pre():
         for k in range(4):
-            rights[R_PRE + k, pl.ds(0, ROWS_ALL), :] = pres[4 * coords[X] + k].astype(BF16)
+            rights[R_PRE + k, pl.ds(0, ROWS_ALL), :] = pres[4 * coords[A] + k].astype(BF16)
 
         def use_pre(s, piece):
             for k in range(4):
@@ -457,11 +487,11 @@
             media_away(i - 2).wait_send()
             media_home(i - 2).wait()
         normed, inverse = normed_rows(m_buf[i % 2].astype(F32))
-        media_in = normed * gains[0:1, :] + biases[0:1, :]
-        grad_media = mm_nt(rights[R_KV + i], w_keyval[:, pl.ds(0, COLS)])
+        media_in = normed * gains[0, 0:1, :] + biases[0, 0:1, :]
+        grad_media = mm_nt(rights[R_KV + i], wkv[0, :, pl.ds(0, COLS)])
         for k in range(1, 4):
-            grad_media += mm_nt(rights[R_KV + 7 * k + i], w_keyval[:, pl.ds(COLS * k, COLS)])
-        back, gain_sum, bias_sum = norm_back(grad_media, normed, inverse, gains[0:1, :])
+            grad_media += mm_nt(rights[R_KV + 7 * k + i], wkv[0, :, pl.ds(COLS * k, COLS)])
+        back, gain_sum, bias_sum = norm_back(grad_media, normed, inverse, gains[0, 0:1, :])
         if i == 0:
             sums[pl.ds(0, 1), :] = gain_sum
             sums[pl.ds(3, 1), :] = bias_sum
@@ -496,26 +526,29 @@
         return [(k, R_KV + 7 * which + k) for k in range(7)]
 
     own = (own1, own2, own3)
-    far = (far1, far2, far3)
-    near = (near1, near2, near3)
 
     def spot(lane, group):
         return (lane * 3 + group % 3) * 4
 
+    def pieces(what, axes, i, b, c):
+        if what == "down":
+            block = {A: by_section(i, b), C: by_section(b, i)}
+            return block[axes[0]], block[axes[1]] * 4 + c
+        block = {A: by_section(i, c), B: by_section(b, i), C: by_section(c, b)}
+        second, third = {A: (B, C), B: (C, A), C: (B, A)}[axes[0]]
+        return block[axes[0]], block[second] * 4 + block[third]
+
     def terms(lane, group):
-        what, which, _, order = PLAN[lane][group]
+        what, which, axes = PLAN[lane][group]
         base = spot(lane, group)
 
         def block(i, carry):
             total = sum(mm(lefts[a, i], rights[b]) for a, b in factors(what, which))
-            if order == ABC:
-                own1[base + i] = total
-            else:
-                for b in range(4):
-                    for c in range(4):
-                        first, second, third = [(i, b, c)[n] for n in order]
-                        rows = pl.ds(pl.multiple_of((second * 4 + third) * 16, 16), 16)
-                        own1[base + first, rows, :] = total[(b * 4 + c) * 16 : (b * 4 + c) * 16 + 16]
+            for b in range(4):
+                for c in range(4):
+                    first, rest = pieces(what, axes, i, b, c)
+                    rows = pl.ds(pl.multiple_of(rest * 16, 16), 16)
+                    own1[base + first, rows, :] = total[(b * 4 + c) * 16 : (b * 4 + c) * 16 + 16]
             return carry
 
         lax.fori_loop(0, 4, block, 0)
@@ -524,27 +557,41 @@
         axis = PLAN[lane][group][2][stage]
         half = RING_ROWS[stage] // 2
         shift = 1 if way == 0 else 3
-        turn = group % 3 if stage == 0 and step == 0 else group % 2
-        sem = (((lane * 3 + stage) * 2 + step) * 2 + way) * 3 + turn
-        if step == 0:
-            source = own[stage].at[spot(lane, group) + at(axis, 2), pl.ds(way * half, half)]
-            target = far[stage].at[lane, way, turn]
+        place = own[stage].at[spot(lane, group) + at(axis, 2 if step == 0 else shift)]
+        if stage == 0:
+            turn = group % 2 if step == 2 else group % 3
+            source = place.at[pl.ds((1 - way if step == 1 else way) * half, half)]
+            target = (far1, mine1, summed1)[step].at[lane, way, turn]
         else:
-            source = own[stage].at[spot(lane, group) + at(axis, shift)]
-            target = near[stage].at[lane, way, turn]
+            turn = group % 2
+            source = place.at[pl.ds(way * half, half)] if step == 0 else place
+            target = (far2, near2)[step].at[lane, way, turn]
+        sem = (((lane * 2 + stage) * 3 + step) * 2 + way) * 3 + turn
         return pltpu.make_async_remote_copy(
             src_ref=source, dst_ref=target, send_sem=t_send.at[sem], recv_sem=t_recv.at[sem],
             device_id={"dp": peer(axis, shift)}, device_id_type=MESH,
         )
 
+    def last_turn(lane, group):
+        return sum(1 for g in range(group) if runs(lane, g, 2)) % 3
+
+    def last_copy(lane, group, shift):
+        axis = PLAN[lane][group][2][2]
+        sem = (lane * 3 + last_turn(lane, group)) * 3 + shift - 1
+        return pltpu.make_async_remote_copy(
+            src_ref=own3.at[spot(lane, group) + at(axis, shift)], dst_ref=last.at[lane, last_turn(lane, group), shift - 1],
+            send_sem=z_send.at[sem], recv_sem=z_recv.at[sem],
+            device_id={"dp": peer(axis, shift)}, device_id_type=MESH,
+        )
+
     def runs(lane, group, stage):
         return 0 <= group < GROUPS and PLAN[lane][group] is not None and stage < len(PLAN[lane][group][2])
 
     def up_copy(shift):
-        rows = pl.ds(pl.multiple_of(16 * at(X, shift), 16), 16)
+        rows = pl.ds(pl.multiple_of(16 * at(A, shift), 16), 16)
         return pltpu.make_async_remote_copy(
             src_ref=up_sum.at[rows, :], dst_ref=up_got.at[shift - 1], send_sem=u_send.at[shift - 1], recv_sem=u_recv.at[shift - 1],
-            device_id={"dp": peer(X, shift)}, device_id_type=MESH,
+            device_id={"dp": peer(A, shift)}, device_id_type=MESH,
         )
 
     def finish(what, which, total):
@@ -576,63 +623,83 @@
         if t == 0:
             media_back(0)
             turn_pre()
+            media_back(1)
         if t == 1:
-            media_back(1)
             media_back(2)
+            media_back(3)
         if t == 2:
-            media_back(3)
             media_back(4)
-        if t == 3:
             media_back(5)
             small_left()
-        for stage in range(3):
-            for lane in range(3):
+        for lane in range(3):
+            for stage in range(2):
                 half = RING_ROWS[stage] // 2
                 group = t - 1 - 2 * stage
                 if runs(lane, group, stage):
                     axis = PLAN[lane][group][2][stage]
-                    turn = group % 3 if stage == 0 else group % 2
                     for way in range(2):
                         ring_copy(lane, group, stage, 0, way).wait()
-                        own[stage][spot(lane, group) + at(axis, 1 if way == 0 else 3), pl.ds(way * half, half), :] += far[stage][
-                            lane, way, turn
-                        ]
+                        arrived = far1[lane, way, group % 3] if stage == 0 else far2[lane, way, group % 2]
+                        own[stage][spot(lane, group) + at(axis, 1 if way == 0 else 3), pl.ds(way * half, half), :] += arrived
                 group = t - 2 - 2 * stage
                 if runs(lane, group, stage):
-                    what, which, axes, _ = PLAN[lane][group]
+                    what, which, axes = PLAN[lane][group]
                     for way in range(2):
                         ring_copy(lane, group, stage, 1, way).wait()
-                    total = (
-                        own[stage][spot(lane, group) + at(axes[stage], 0)]
-                        + near[stage][lane, 0, group % 2]
-                        + near[stage][lane, 1, group % 2]
-                    )
-                    if stage + 1 < len(axes):
-                        rows = RING_ROWS[stage + 1]
+                        if stage == 0:
+                            ring_copy(lane, group, stage, 2, way).wait()
+                    mine = spot(lane, group) + at(axes[stage], 0)
+                    rows = RING_ROWS[stage + 1]
+                    if stage == 0:
+                        three, two = group % 3, group % 2
+                        total = [
+                            own1[mine, pl.ds(0, 128), :] + summed1[lane, 0, two] + mine1[lane, 1, three],
+                            own1[mine, pl.ds(128, 128), :] + mine1[lane, 0, three] + summed1[lane, 1, two],
+                        ]
                         for k in range(4):
-                            own[stage + 1][spot(lane, group) + k] = total[rows * k : rows * k + rows]
+                            own2[spot(lane, group) + k] = total[k // 2][rows * (k % 2) : rows * (k % 2) + rows]
                     else:
-                        finish(what, which, total)
-                        if what == "up":
-                            ups += 1
-                            if ups == 4:
-                                for shift in (1, 2, 3):
-                                    up_copy(shift).start()
-        for stage in range(3):
-            for lane in range(3):
-                if stage > 0 and runs(lane, t - 2 * stage, stage):
-                    for way in range(2):
-                        ring_copy(lane, t - 2 * stage, stage, 0, way).start()
-                if runs(lane, t - 1 - 2 * stage, stage):
-                    for way in range(2):
-                        ring_copy(lane, t - 1 - 2 * stage, stage, 1, way).start()
+                        total = own2[mine] + near2[lane, 0, group % 2] + near2[lane, 1, group % 2]
+                        if len(axes) == 3:
+                            for k in range(4):
+                                own3[spot(lane, group) + k] = total[rows * k : rows * k + rows]
+                        else:
+                            finish(what, which, total)
+                            if what == "up":
+                                ups += 1
+            group = t - 5
+            if runs(lane, group, 2):
+                what, which, axes = PLAN[lane][group]
+                total = own3[spot(lane, group) + at(axes[2], 0)]
+                for shift in (1, 2, 3):
+                    last_copy(lane, group, shift).wait()
+                    total += last[lane, last_turn(lane, group), shift - 1]
+                finish(what, which, total)
+        for lane in range(3):
+            for way in range(2):
+                if runs(lane, t - 1, 0):
+                    ring_copy(lane, t - 1, 0, 2, way).start()
+                if runs(lane, t - 2, 1):
+                    ring_copy(lane, t - 2, 1, 0, way).start()
+                if runs(lane, t - 3, 1):
+                    ring_copy(lane, t - 3, 1, 1, way).start()
+            if runs(lane, t - 4, 2):
+                for shift in (1, 2, 3):
+                    last_copy(lane, t - 4, shift).start()
+            for way in range(2):
+                if runs(lane, t, 0):
+                    ring_copy(lane, t, 0, 1, way).start()
+        if ups == 4:
+            ups = 0
+            for shift in (1, 2, 3):
+                up_copy(shift).start()
 
     for s in range(4):
-        part = up_sum[pl.ds(pl.multiple_of(16 * coords[X], 16), 16), :] if s == 0 else None
+        part = up_sum[pl.ds(pl.multiple_of(16 * coords[A], 16), 16), :] if s == 0 else None
         if s > 0:
             up_copy(s).wait()
             part = up_got[s - 1]
-        cols = pl.ds(pl.multiple_of(1024 * at(X, 4 - s), 1024), 1024)
+        cols = pl.ds(pl.multiple_of(1024 * at(A, 4 - s), 1024), 1024)
         out_up[:, cols] = part
 
     for i in (4, 5):
@@ -653,7 +720,7 @@
         to_other(sent, latents_grad, l_sem).wait_recv()
 
 
-def run_resampler(latents, media, mask, gains, biases, w_query, w_keyval, w_out, w_up, w_down, cotangent):
+def run_resampler(latents, media, frame_count, gains, biases, w_query, w_keyval, w_out, w_up, w_down, cotangent):
     vmem = pl.BlockSpec(memory_space=pltpu.VMEM)
     hbm = pl.BlockSpec(memory_space=pl.ANY)
 
@@ -667,9 +734,12 @@
             sds(192, 512), sds(192, 512), sds(16, 256), sds(16, 512), sds(16, 1024), sds(8, 1024), sds(16, 4096), sds(64, 1024),
             sds(6, 2, 256, 256), sds(6, 2, 256, 256), sds(4, 3, 4, 192, 256),
         ],
-        in_specs=[hbm, hbm] + [vmem] * 6 + [hbm, hbm, hbm],
+        in_specs=[hbm, hbm, pl.BlockSpec(memory_space=pltpu.SMEM)] + [vmem] * 2 + [hbm] * 6,
         out_specs=[vmem] * 8 + [hbm] * 3,
         scratch_shapes=[
+            pltpu.VMEM((1, 1024, 512), BF16),
+            pltpu.VMEM((1, 1024, 1024), BF16),
+            pltpu.VMEM((1, 512, 1024), BF16),
             pltpu.VMEM((192, 1024), F32),
             pltpu.VMEM((192, 1024), F32),
             pltpu.VMEM((192, 1024), F32),
@@ -684,43 +754,80 @@
             pltpu.VMEM((192, 512), F32),
             pltpu.VMEM((2, 4, 256, 256), F32),
             pltpu.VMEM((2, 256, 1024), BF16),
-            pltpu.VMEM((2, 1024, 512), BF16),
-            pltpu.VMEM((2, 512, 1024), BF16),
+            pltpu.VMEM((DEEP, 512, 1024), BF16),
             pltpu.VMEM((2, 4, 192, 256), F32),
             pltpu.VMEM((18, 4, 256, 256), BF16),
             pltpu.VMEM((67, 256, 256), BF16),
         ]
         + [pltpu.VMEM((36, r, COLS), F32) for r in RING_ROWS]
-        + [pltpu.VMEM((3, 2, 3 if r == 256 else 2, r // 2, COLS), F32) for r in RING_ROWS]
-        + [pltpu.VMEM((3, 2, 2, r, COLS), F32) for r in RING_ROWS]
         + [
+            pltpu.VMEM((3, 2, 3, 128, COLS), F32),
+            pltpu.VMEM((3, 2, 2, 32, COLS), F32),
+            pltpu.VMEM((3, 2, 3, 128, COLS), F32),
+            pltpu.VMEM((3, 2, 2, 128, COLS), F32),
+            pltpu.VMEM((3, 2, 2, 64, COLS), F32),
+            pltpu.VMEM((3, 3, 3, 16, COLS), F32),
             pltpu.VMEM((64, 1024), F32),
             pltpu.VMEM((3, 16, 1024), F32),
-            dma((2, 2)), dma((2,)), dma((2,)), dma((2,)), dma((2,)), dma((2,)), dma((6,)), dma((6,)), dma((6,)),
-            dma((4, 3)), dma((4, 3)), dma((2,)), dma((108,)), dma((108,)), dma((3,)), dma((3,)),
+            dma((3,)), dma((3, 4)), dma((2,)), dma((2,)), dma((2,)), dma((2,)), dma((2,)), dma((6,)), dma((6,)), dma((6,)),
+            dma((4, 3)), dma((4, 3)), dma((2,)), dma((108,)), dma((108,)), dma((27,)), dma((27,)), dma((3,)), dma((3,)),
         ],
         compiler_params=pltpu.CompilerParams(collective_id=1, has_side_effects=True, vmem_limit_bytes=VMEM_BYTES),
         name="resampler",
-    )(latents, media, mask, gains, biases, w_query, w_keyval, w_out, w_up, w_down, cotangent)
+    )(latents, media, frame_count, gains, biases, w_query, w_keyval, w_out, w_up, w_down, cotangent)
+
+
+def results_kernel(mine, theirs, *refs):
+    given, made = refs[:8], refs[8:]
+    total = mine[0] + theirs[0]
+    made[0][:, pl.ds(0, COLS)] = total[0]
+    made[0][:, pl.ds(COLS, COLS)] = total[1]
+
+    @pl.when(pl.program_id(0) == 0)
+    def _():
+        for source, target in zip(given[1:], made[3:]):
+            target[...] = source[...]
+        columns = given[0][...].T
+        made[1][0] = columns[:3]
+        made[2][0] = columns[3:6]
+
+
+def results(mine, theirs, small, resampled, latents_grad, query, keyval, out, up, down):
+    rest = [resampled, latents_grad, query, keyval, out, up, down]
+    whole = [pl.BlockSpec(a.shape, lambda i: (0, 0)) for a in rest]
+
+    def sds(*shape):
+        return jax.ShapeDtypeStruct(shape, F32)
+
+    part = pl.BlockSpec((1, 2, COLS, COLS), lambda i: (i, 0, 0, 0))
+    norms = pl.BlockSpec((1, 3, 16), lambda i: (0, 0, 0))
+    return pl.pallas_call(
+        results_kernel,
+        grid=(6,),
+        out_shape=[sds(1536, 512), sds(1, 3, 16), sds(1, 3, 16)] + [sds(*a.shape) for a in rest],
+        in_specs=[part, part, pl.BlockSpec((16, COLS), lambda i: (0, 0))] + whole,
+        out_specs=[pl.BlockSpec((COLS, 512), lambda i: (i, 0)), norms, norms] + whole,
+        compiler_params=pltpu.CompilerParams(vmem_limit_bytes=32 * 2**20),
+        name="results",
+    )(mine, theirs, small, *rest)
 
 
 def body(
     latents_in, media, frame_count, gains, biases, w_query, w_keyval, w_out, w_up, w_down, cotangent
 ):
-    key = jnp.arange(KEYS)
-    valid = (key[None] < 64 * frame_count) | ((key[None] >= 512) & (key[None] < 576))
-    mask = valid.astype(F32)[:, None, :]
     resampled, latents_grad, small, query, keyval, out, up, down, mine, theirs, _ = run_resampler(
-        latents_in.reshape(192, 1024), media.reshape(1536, 1024), mask, gains[0], biases[0],
-        w_query[0], w_keyval[0], w_out[0], w_up[0], w_down[0], cotangent.reshape(192, 1024),
+        latents_in.reshape(192, 1024), media.reshape(1536, 1024), frame_count, gains, biases,
+        w_query, w_keyval, w_out, w_up.reshape(4, 256, 4096), w_down.reshape(4096, 1024), cotangent.reshape(192, 1024),
     )
-    small = small[:, :6].T
+    media_grad, gains_grad, biases_grad, resampled, latents_grad, query, keyval, out, up, down = results(
+        mine, theirs, small, resampled, latents_grad, query, keyval, out, up, down
+    )
     return (
         resampled.reshape(3, 1, 64, 512),
         latents_grad.reshape(3, 1, 64, 512),
-        (mine + theirs).transpose(0, 2, 1, 3).reshape(3, 1, 512, 512),
-        small[None, :3],
-        small[None, 3:],
+        media_grad.reshape(3, 1, 512, 512),
+        gains_grad,
+        biases_grad,
         query[None],
         keyval[None],
         out[None],

time: 224 us -> 189 us (0.84)
  Pallas kernels: 198 us -> 172 us
  other arithmetic: 4.65 us -> 0 us
  local copies, waits for them, and re-layouts: 19.5 us -> 15.8 us
    pallas_call x1, Pallas kernels: 198 us -> 168 us  [run_resampler(): pl.pallas_call(resampler_kernel, out_shape=[sds(192, 512), sds(192, 512),...]
    reshape x1 -> x0, local copies, waits for them, and re-layouts: 3.63 us -> none  [body(): (mine + theirs).transpose(0, 2, 1, 3).reshape(3, 1, 512, 512)]
    transpose x1 -> x0, other arithmetic: 3.32 us -> none  [body(): (mine + theirs).transpose(0, 2, 1, 3).reshape(3, 1, 512, 512)]
    pallas_call x0 -> x1, Pallas kernels: none -> 3.28 us  [results(): pl.pallas_call(results_kernel, grid=(6,), out_shape=[sds(1536, 512), sds(...]
    transpose x2 -> x0, local copies, waits for them, and re-layouts: 3.13 us -> none  [the longest x1 2.43 us: body(): (mine + theirs).transpose(0, 2, 1, 3).reshape(3, 1, 512, 512)]
    unnamed x12 -> x25, local copies, waits for them, and re-layouts: 12.7 us -> 15.8 us
where the time goes in v4:
time: 189 us; the launch traced here: 188 us
  Pallas kernels  172 us (91%)
  local copies, waits for them, and re-layouts  15.8 us (8%)
    pallas_call x1, Pallas kernels, run_resampler(): pl.pallas_call(resampler_kernel, out_shape=[sds(192, 512), sds(192, 512),...  168 us
    unnamed x25, local copies, waits for them, and re-layouts  15.8 us

profile of v4, /device:TPU:0, one launch (start us, length us, event | category | flops | bytes accessed | tf_op | source)
XLA Modules:
  0.0 188.2 jit_solution(8722318818204948739)
XLA Ops:
  0.6 1.3 copy.21.frame_count
  2.0 1.3 copy.22.gains
  3.3 1.3 copy.23.biases
  4.6 168.4 %resampler.1 = (f32[192,512]{1,0:T(8,128)}, f32[192,512]{1,0:T(8,128)}, f32[16,256]{1,0:T(8,128)}, f32[16,512]{1,0:T(8,128)}, f32[16,1024]{1,0:T(8,128)}, /*inde...) custom-call(bf16[192,1024]{1,0:T(8,128)(2,1)} %bitcast.22, ...), custom_call_target="tpu_custom_call" | custom-call | tf_op jit(solution)/shard_map/resampler/pallas_call | solution.py:731
  173.0 0.0 copy-start
  173.0 1.9 copy-done
  174.9 0.0 copy-start.1
  174.9 1.9 %copy-done.1 = f32[6,2,256,256]{3,2,1,0:T(8,128)S(1)} copy-done((f32[6,2,256,256]{3,2,1,0:T(8,128)S(1)}, f32[6,2,256,256]{3,2,1,0:T(8,128)}, u32[]{:S(2)}) %copy-start.1) | copy-done | bytes 3145752
  176.8 0.0 copy-start.2
  176.8 1.0 copy-done.2
  177.8 0.0 copy-start.3
  177.8 1.0 copy-done.3
  178.8 0.0 copy-start.4
  178.8 0.9 copy-done.4
  179.7 0.0 copy-start.5
  179.7 0.9 copy-done.5
  180.7 0.0 copy-start.6
  180.7 0.8 copy-done.6
  181.5 0.0 copy-start.7
  181.5 0.8 copy-done.7
  182.3 0.0 copy-start.8
  182.3 0.8 copy-done.8
  183.0 0.0 copy-start.9
  183.0 0.7 copy-done.9
  183.8 3.3 %results.1 = (f32[1536,512]{1,0:T(8,128)}, f32[1,3,16]{2,1,0:T(4,128)S(1)}, f32[1,3,16]{2,1,0:T(4,128)S(1)}, f32[192,512]{1,0:T(8,128)}, f32[192,512]{1,0:T(8,12...) custom-call(f32[6,2,256,256]{3,2,1,0:T(8,128)S(1)} %copy-done, ...), custom_call_target="tpu_custom_call" | custom-call | tf_op jit(solution)/shard_map/results/pallas_call | solution.py:804
  187.1 0.6 copy.27
  187.6 0.6 copy.28
Async XLA Ops:
  173.0 1.9 %copy-start = (f32[6,2,256,256]{3,2,1,0:T(8,128)S(1)}, f32[6,2,256,256]{3,2,1,0:T(8,128)}, u32[]{:S(2)}) copy-start(f32[6,2,256,256]{3,2,1,0:T(8,128)} %get-tuple-element.30.mine) | copy-start | bytes 9437188
  174.9 1.9 %copy-start.1 = (f32[6,2,256,256]{3,2,1,0:T(8,128)S(1)}, f32[6,2,256,256]{3,2,1,0:T(8,128)}, u32[]{:S(2)}) copy-start(f32[6,2,256,256]{3,2,1,0:T(8,128)} %get-tuple-element.31.theirs) | copy-start | bytes 9437188
  176.8 1.0 copy-start.2
  177.8 1.0 copy-start.3
  178.8 0.9 copy-start.4
  179.7 0.9 copy-start.5
  180.7 0.8 copy-start.6
  181.5 0.8 copy-start.7
  182.3 0.8 copy-start.8
  183.0 0.7 copy-start.9

commit v5 on v4

--- a/solution.py
+++ b/solution.py
@@ -20,8 +20,8 @@
 COLS = 256
 A, B, C = 0, 1, 2
 FF_IN, ACT, G_OUT, G_PRE = 0, 1, 2, 3
-L_LATENT, L_SMALL, L_FF, L_ACT, L_ATT = 6, 7, 8, 12, 16
-R_PRE, R_OUT, R_ATT, R_QUERY, R_SMALL, R_KV = 0, 16, 32, 36, 38, 39
+L_LATENT, L_FF, L_ACT, L_ATT = 6, 8, 12, 16
+R_PRE, R_OUT, R_ATT, R_QUERY, R_KV = 0, 16, 32, 36, 38
 PLAN = (
     (
         ("down", 0, (A, C)),
@@ -33,26 +33,26 @@
     ),
     (
         ("out", 0, (B, C, A)),
+        ("out", 1, (B, C, A)),
         ("up", 0, (B, C)),
+        ("keyval", 1, (B, C, A)),
         ("up", 1, (B, C)),
-        ("keyval", 1, (B, C, A)),
-        ("keyval", 3, (B, C, A)),
         None,
     ),
     (
-        ("out", 1, (C, B, A)),
         ("down", 2, (C, A)),
+        ("down", 3, (C, A)),
         ("up", 2, (C, B)),
         ("up", 3, (C, B)),
-        ("small", 0, (C, B, A)),
-        ("down", 3, (C, A)),
+        ("keyval", 3, (C, B, A)),
+        None,
     ),
 )
 GROUPS = 6
 TICKS = GROUPS + 4
 WIDE = 4
 DEEP = 3
-WU_BASE = 35
+WU_BASE = 34
 
 
 def mm(left, right):
@@ -104,11 +104,11 @@
 
 
 def resampler_kernel(
-    latents, media, frame_count, gains, biases, w_query, w_keyval, w_out, w_up, w_down, cotangent,
+    latents, media, norms, w_query, w_keyval, w_out, w_up, w_down, cotangent,
     resampled, latents_grad, out_small, out_query, out_keyval, out_out, out_up, out_down, m_own, m_got, land,
     wq, wkv, wo, xs, x1s, gys, accs, lin, ffin, qs, att, gatt, pres, sums, sent, m_stage, m_buf, wd, gave,
-    lefts, rights, own1, own2, own3, far1, far2, mine1, summed1, near2, last, up_sum, up_got,
-    a_sem, w_sem, b_sem, x_sem, g_sem, r_sem, l_sem, m_send, m_recv, m_local, e_send, e_recv, c_sem, t_send, t_recv, z_send, z_recv, u_send, u_recv,
+    lefts, rights, own1, own2, own3, far1, far2, mine1, summed1, near2, last, up_sum, up_got, small_sum, small_got, columns,
+    a_sem, w_sem, b_sem, x_sem, g_sem, r_sem, l_sem, m_send, m_recv, m_local, e_send, e_recv, c_sem, t_send, t_recv, z_send, z_recv, u_send, u_recv, s_send, s_recv,
 ):
     section = lax.axis_index("section")
     other = 1 - section
@@ -196,9 +196,9 @@
         for shift in (1, 3, 2):
             exchange(kind, shift).start()
 
-    def taken(kind, use):
+    def taken(kind, use, late=False):
         def held(s):
-            if kind == G_PRE:
+            if late:
                 return own1.at[pl.ds(8 + 12 * (s % 2), 4), pl.ds(0, ROWS_ALL), :]
             return m_stage.at[s % 2, :, pl.ds(0, ROWS_ALL), :]
 
@@ -244,7 +244,7 @@
 
         media_rows(i).wait()
         normed, _ = normed_rows(m_buf[i % 2].astype(F32))
-        media_in = (normed * gains[0, 0:1, :] + biases[0, 0:1, :]).astype(BF16)
+        media_in = (normed * norms[0:1, :] + norms[3:4, :]).astype(BF16)
         keyval = mm(media_in, wkv[0]).astype(BF16)
         for j in range(4):
             lefts[i, j] = column(keyval, j)
@@ -259,7 +259,7 @@
         to_other(accs, xs, x_sem).wait_recv()
 
     normed, _ = normed_rows(xs[...])
-    lin[...] = (normed * gains[0, 1:2, :] + biases[0, 1:2, :]).astype(BF16)
+    lin[...] = (normed * norms[1:2, :] + norms[4:5, :]).astype(BF16)
     qs[...] = (mm(lin[...], wq[0]) * 0.125).astype(BF16)
     latent_kv = mm(lin[...], wkv[0]).astype(BF16)
     for v in range(3):
@@ -269,14 +269,14 @@
             lefts[6 + v // 2, j, pl.ds((v % 2) * 128 + 64, 64), :] = jnp.zeros((64, COLS), BF16)
 
     def keyvals_of(v, j):
-        tail = pl.ds(pl.multiple_of((v % 2) * 128, 128), 128)
+        tail = pl.ds((v % 2) * 128, 128)
         return lefts[2 * v, j], lefts[2 * v + 1, j], lefts[6 + v // 2, j, tail, :]
 
-    key = lax.broadcasted_iota(jnp.int32, (1, KEYS), 1)
-
-    def attend(v, carry):
-        rows = pl.ds(pl.multiple_of(v * 64, 64), 64)
-        valid = (key < 64 * frame_count[v, 0]) | ((key >= 512) & (key < 576))
+    key = lax.broadcasted_iota(jnp.int32, (1, KEYS), 1).astype(F32)
+
+    def attend(v):
+        rows = pl.ds(v * 64, 64)
+        valid = (key < norms[6:7, 256 * v : 256 * v + 1]) | ((key >= 512.0) & (key < 576.0))
         for g in range(2):
             cols = pl.ds(COLS * g, COLS)
             stacked = head_stack(qs[rows, cols])
@@ -295,15 +295,15 @@
                 own1[(v * 2 + g) * 3 + n, :, pl.ds(0, p.shape[1])] = p
                 mixed += mm(p.astype(BF16), values)
             att[rows, cols] = head_merge(mixed).astype(BF16)
-        return carry
-
-    lax.fori_loop(0, 3, attend, 0)
+
+    for v in range(3):
+        attend(v)
 
     x1 = xs[...] + mm(att[...], wo[0])
     x1s[...] = x1
     accs[...] = x1
     normed, _ = normed_rows(x1)
-    ffin[...] = (normed * gains[0, 2:3, :] + biases[0, 2:3, :]).astype(BF16)
+    ffin[...] = (normed * norms[2:3, :] + norms[5:6, :]).astype(BF16)
     to_rows(gave.at[0], ffin[...].astype(F32))
     give(FF_IN)
 
@@ -325,7 +325,7 @@
     give(ACT)
     fetch_first()
 
-    def turn_forward():
+    def turn_ff(late):
         for k in range(4):
             lefts[L_FF, k] = turned(gave[0, k])
 
@@ -333,15 +333,11 @@
             for k in range(4):
                 lefts[L_FF + s, k] = turned(piece[k])
 
-        taken(FF_IN, use_ff)
+        taken(FF_IN, use_ff, late)
+
+    def turn_act():
         for k in range(4):
             lefts[L_ACT, k] = turned(own1[18 + 4 * coords[B] + k, pl.ds(0, ROWS_ALL), :])
-
-        def use_act(s, piece):
-            for k in range(4):
-                lefts[L_ACT + s, k] = turned(piece[k])
-
-        taken(ACT, use_act)
         for i in range(4):
             part = jnp.concatenate([att[:, pl.ds(128 * i, 128)].astype(F32), jnp.zeros((64, 128), F32)], 0)
             part = part.T.reshape(16, 8, 256)
@@ -349,10 +345,17 @@
             lefts[L_ATT, i] = jnp.concatenate([part, none], 1).reshape(256, 256).astype(BF16)
             lefts[L_ATT + 1, i] = jnp.concatenate([none, part], 1).reshape(256, 256).astype(BF16)
 
+        def use_act(s, piece):
+            for k in range(4):
+                lefts[L_ACT + s, k] = turned(piece[k])
+
+        taken(ACT, use_act)
+
     @pl.when(section == 0)
     def _():
         to_other(accs, xs, x_sem).start()
-        turn_forward()
+        turn_ff(False)
+        turn_act()
         to_other(accs, xs, x_sem).wait_send()
         to_other(accs, gys, g_sem).wait_recv()
         to_rows(gave.at[1], gys[...].astype(BF16).astype(F32))
@@ -390,16 +393,13 @@
         return carry
 
     lax.fori_loop(0, FF_STEPS, ff_backward, 0)
-    for k in list(range(38)) + [R_KV + 7 * j + 6 for j in range(4)]:
+    for k in list(range(R_KV)) + [R_KV + 7 * j + 6 for j in range(4)]:
         rights[k, pl.ds(192, 64), :] = jnp.zeros((64, COLS), BF16)
     for k in range(4):
         rights[R_OUT + k, pl.ds(0, ROWS_ALL), :] = ffin[:, pl.ds(COLS * k, COLS)]
-    row = lax.broadcasted_iota(jnp.int32, (256, COLS), 0)
-    col = lax.broadcasted_iota(jnp.int32, (256, COLS), 1)
-    rights[R_SMALL] = jnp.where(((row == col) & (row < 6)) | ((row == col + 6) & (row >= 6) & (row < 12)), 1.0, 0.0).astype(BF16)
-
     normed, inverse = normed_rows(x1s[...])
-    back, gain_sum, bias_sum = norm_back(accs[...], normed, inverse, gains[0, 2:3, :])
+    back, gain_sum, bias_sum = norm_back(accs[...], normed, inverse, norms[2:3, :])
+    sums[pl.ds(6, 2), :] = jnp.zeros((2, 1024), F32)
     sums[pl.ds(2, 1), :] = gain_sum
     sums[pl.ds(5, 1), :] = bias_sum
     grad_x1 = gys[...] + back
@@ -409,8 +409,8 @@
         rights[R_ATT + k, pl.ds(0, ROWS_ALL), :] = column(grad_attn, k)
     gatt[...] = mm_nt(grad_attn, wo[0]).astype(BF16)
 
-    def attend_back(v, carry):
-        rows = pl.ds(pl.multiple_of(v * 64, 64), 64)
+    def attend_back(v):
+        rows = pl.ds(v * 64, 64)
         for g in range(2):
             cols = pl.ds(COLS * g, COLS)
             q_stack = head_stack(qs[rows, cols])
@@ -429,16 +429,16 @@
                 rights[base + 2 * v] = mm_tn(factors[0], stack).astype(BF16)
                 rights[base + 2 * v + 1] = mm_tn(factors[1], stack).astype(BF16)
                 rights[base + 6, rows, :] = mm_tn(factors[2], stack)[:64].astype(BF16)
-        return carry
-
-    lax.fori_loop(0, 3, attend_back, 0)
+
+    for v in range(3):
+        attend_back(v)
 
     grad_in = sum(mm_nt(rights[R_QUERY + g, pl.ds(0, ROWS_ALL), :], wq[0, :, pl.ds(COLS * g, COLS)]) for g in range(2))
     grad_in = grad_in * 0.125
     for k in range(4):
         grad_in += mm_nt(rights[R_KV + 6 + 7 * k, pl.ds(0, ROWS_ALL), :], wkv[0, :, pl.ds(COLS * k, COLS)])
     normed, inverse = normed_rows(xs[...])
-    back, gain_sum, bias_sum = norm_back(grad_in, normed, inverse, gains[0, 1:2, :])
+    back, gain_sum, bias_sum = norm_back(grad_in, normed, inverse, norms[1:2, :])
     sums[pl.ds(1, 1), :] = gain_sum
     sums[pl.ds(4, 1), :] = bias_sum
     accs[...] = gys[...] + back
@@ -446,7 +446,7 @@
     @pl.when(section == 1)
     def _():
         to_other(accs, gys, g_sem).start()
-        turn_forward()
+        turn_act()
 
     @pl.when(section == 0)
     def _():
@@ -468,7 +468,7 @@
             for k in range(4):
                 rights[R_PRE + 4 * s + k, pl.ds(0, ROWS_ALL), :] = piece[k].astype(BF16)
 
-        taken(G_PRE, use_pre)
+        taken(G_PRE, use_pre, True)
 
     def media_away(i):
         return pltpu.make_async_remote_copy(
@@ -487,11 +487,11 @@
             media_away(i - 2).wait_send()
             media_home(i - 2).wait()
         normed, inverse = normed_rows(m_buf[i % 2].astype(F32))
-        media_in = normed * gains[0, 0:1, :] + biases[0, 0:1, :]
+        media_in = normed * norms[0:1, :] + norms[3:4, :]
         grad_media = mm_nt(rights[R_KV + i], wkv[0, :, pl.ds(0, COLS)])
         for k in range(1, 4):
             grad_media += mm_nt(rights[R_KV + 7 * k + i], wkv[0, :, pl.ds(COLS * k, COLS)])
-        back, gain_sum, bias_sum = norm_back(grad_media, normed, inverse, gains[0, 0:1, :])
+        back, gain_sum, bias_sum = norm_back(grad_media, normed, inverse, norms[0:1, :])
         if i == 0:
             sums[pl.ds(0, 1), :] = gain_sum
             sums[pl.ds(3, 1), :] = bias_sum
@@ -505,12 +505,30 @@
         for k in range(4):
             lefts[i, k] = turned(column(media_in, k).astype(BF16).astype(F32))
 
-    def small_left():
-        total = sums[pl.ds(0, 6), :]
-        high = total.astype(BF16).astype(F32)
-        block = jnp.concatenate([high, total - high, jnp.zeros((244, 1024), F32)], 0)
-        for k in range(4):
-            lefts[L_SMALL, k] = turned(column(block, k))
+    places, steps = (x, y, z), (16, 4, 1)
+
+    def small_copy(axis, shift):
+        place = (places[axis] + shift) % 4
+        source = sums.at[:, pl.ds(pl.multiple_of(COLS * place, COLS), COLS)] if axis == 0 else small_sum.at[axis - 1]
+        return pltpu.make_async_remote_copy(
+            src_ref=source, dst_ref=small_got.at[axis, shift - 1], send_sem=s_send.at[axis, shift - 1], recv_sem=s_recv.at[axis, shift - 1],
+            device_id={"dp": me + (place - places[axis]) * steps[axis]}, device_id_type=MESH,
+        )
+
+    def small_give(axis):
+        for shift in (1, 2, 3):
+            small_copy(axis, shift).start()
+
+    def small_take(axis):
+        total = sums[:, pl.ds(pl.multiple_of(COLS * x, COLS), COLS)] if axis == 0 else small_sum[axis - 1]
+        for shift in (1, 2, 3):
+            small_copy(axis, shift).wait()
+            total += small_got[axis, shift - 1]
+        if axis < 2:
+            small_sum[axis] = total
+        else:
+            columns[...] = jnp.concatenate([total, jnp.zeros((120, COLS), F32)], 0).T
+            out_small[...] = columns[pl.ds(pl.multiple_of(16 * (4 * y + z), 16), 16), :]
 
     def factors(what, which):
         if what == "up":
@@ -521,8 +539,6 @@
             return [(L_ATT + s, R_ATT + 2 * which + s) for s in range(2)]
         if what == "query":
             return [(L_LATENT, R_QUERY + which)]
-        if what == "small":
-            return [(L_SMALL, R_SMALL)]
         return [(k, R_KV + 7 * which + k) for k in range(7)]
 
     own = (own1, own2, own3)
@@ -604,11 +620,9 @@
             out_query[:, cols] = total * 0.125
         elif what == "keyval":
             out_keyval[:, cols] = total
-        elif what == "out":
+        else:
             out_out[:, pl.ds(512 * which, COLS)] = total[:8]
             out_out[:, pl.ds(512 * which + COLS, COLS)] = total[8:]
-        else:
-            out_small[...] = total
 
     for k in range(4):
         lefts[L_LATENT, k] = turned(lin[:, pl.ds(COLS * k, COLS)].astype(F32))
@@ -622,15 +636,24 @@
                     ring_copy(lane, t, 0, 0, way).start()
         if t == 0:
             media_back(0)
-            turn_pre()
             media_back(1)
         if t == 1:
             media_back(2)
             media_back(3)
+
+            @pl.when(section == 1)
+            def _():
+                turn_ff(True)
+
+            turn_pre()
         if t == 2:
             media_back(4)
             media_back(5)
-            small_left()
+            small_give(0)
+        if t in (3, 4, 5):
+            small_take(t - 3)
+            if t < 5:
+                small_give(t - 2)
         for lane in range(3):
             for stage in range(2):
                 half = RING_ROWS[stage] // 2
@@ -720,7 +743,7 @@
         to_other(sent, latents_grad, l_sem).wait_recv()
 
 
-def run_resampler(latents, media, frame_count, gains, biases, w_query, w_keyval, w_out, w_up, w_down, cotangent):
+def run_resampler(latents, media, norms, w_query, w_keyval, w_out, w_up, w_down, cotangent):
     vmem = pl.BlockSpec(memory_space=pltpu.VMEM)
     hbm = pl.BlockSpec(memory_space=pl.ANY)
 
@@ -731,10 +754,10 @@
     return pl.pallas_call(
         resampler_kernel,
         out_shape=[
-            sds(192, 512), sds(192, 512), sds(16, 256), sds(16, 512), sds(16, 1024), sds(8, 1024), sds(16, 4096), sds(64, 1024),
+            sds(192, 512), sds(192, 512), sds(16, 128), sds(16, 512), sds(16, 1024), sds(8, 1024), sds(16, 4096), sds(64, 1024),
             sds(6, 2, 256, 256), sds(6, 2, 256, 256), sds(4, 3, 4, 192, 256),
         ],
-        in_specs=[hbm, hbm, pl.BlockSpec(memory_space=pltpu.SMEM)] + [vmem] * 2 + [hbm] * 6,
+        in_specs=[hbm, hbm, vmem] + [hbm] * 6,
         out_specs=[vmem] * 8 + [hbm] * 3,
         scratch_shapes=[
             pltpu.VMEM((1, 1024, 512), BF16),
@@ -757,7 +780,7 @@
             pltpu.VMEM((DEEP, 512, 1024), BF16),
             pltpu.VMEM((2, 4, 192, 256), F32),
             pltpu.VMEM((18, 4, 256, 256), BF16),
-            pltpu.VMEM((67, 256, 256), BF16),
+            pltpu.VMEM((66, 256, 256), BF16),
         ]
         + [pltpu.VMEM((36, r, COLS), F32) for r in RING_ROWS]
         + [
@@ -769,12 +792,15 @@
             pltpu.VMEM((3, 3, 3, 16, COLS), F32),
             pltpu.VMEM((64, 1024), F32),
             pltpu.VMEM((3, 16, 1024), F32),
+            pltpu.VMEM((2, 8, COLS), F32),
+            pltpu.VMEM((3, 3, 8, COLS), F32),
+            pltpu.VMEM((COLS, 128), F32),
             dma((3,)), dma((3, 4)), dma((2,)), dma((2,)), dma((2,)), dma((2,)), dma((2,)), dma((6,)), dma((6,)), dma((6,)),
-            dma((4, 3)), dma((4, 3)), dma((2,)), dma((108,)), dma((108,)), dma((27,)), dma((27,)), dma((3,)), dma((3,)),
+            dma((4, 3)), dma((4, 3)), dma((2,)), dma((108,)), dma((108,)), dma((27,)), dma((27,)), dma((3,)), dma((3,)), dma((3, 3)), dma((3, 3)),
         ],
         compiler_params=pltpu.CompilerParams(collective_id=1, has_side_effects=True, vmem_limit_bytes=VMEM_BYTES),
         name="resampler",
-    )(latents, media, frame_count, gains, biases, w_query, w_keyval, w_out, w_up, w_down, cotangent)
+    )(latents, media, norms, w_query, w_keyval, w_out, w_up, w_down, cotangent)
 
 
 def results_kernel(mine, theirs, *refs):
@@ -805,9 +831,9 @@
         results_kernel,
         grid=(6,),
         out_shape=[sds(1536, 512), sds(1, 3, 16), sds(1, 3, 16)] + [sds(*a.shape) for a in rest],
-        in_specs=[part, part, pl.BlockSpec((16, COLS), lambda i: (0, 0))] + whole,
+        in_specs=[part, part, pl.BlockSpec((16, 128), lambda i: (0, 0))] + whole,
         out_specs=[pl.BlockSpec((COLS, 512), lambda i: (i, 0)), norms, norms] + whole,
-        compiler_params=pltpu.CompilerParams(vmem_limit_bytes=32 * 2**20),
+        compiler_params=pltpu.CompilerParams(vmem_limit_bytes=VMEM_BYTES),
         name="results",
     )(mine, theirs, small, *rest)
 
@@ -815,8 +841,10 @@
 def body(
     latents_in, media, frame_count, gains, biases, w_query, w_keyval, w_out, w_up, w_down, cotangent
 ):
+    frames = jnp.broadcast_to(64.0 * frame_count.astype(F32)[:, :1], (3, COLS)).reshape(1, 768)
+    norms = jnp.concatenate([gains[0], biases[0], jnp.pad(frames, ((0, 1), (0, 256)))], 0)
     resampled, latents_grad, small, query, keyval, out, up, down, mine, theirs, _ = run_resampler(
-        latents_in.reshape(192, 1024), media.reshape(1536, 1024), frame_count, gains, biases,
+        latents_in.reshape(192, 1024), media.reshape(1536, 1024), norms,
         w_query, w_keyval, w_out, w_up.reshape(4, 256, 4096), w_down.reshape(4096, 1024), cotangent.reshape(192, 1024),
     )
     media_grad, gains_grad, biases_grad, resampled, latents_grad, query, keyval, out, up, down = results(

time: 189 us -> 174 us (0.921)
  local copies, waits for them, and re-layouts: 15.8 us -> 3.26 us
  Pallas kernels: 172 us -> 168 us
    unnamed x25 -> x5, local copies, waits for them, and re-layouts: 15.8 us -> 3.26 us
    pallas_call x1, Pallas kernels: 168 us -> 161 us  [run_resampler(): pl.pallas_call(resampler_kernel, out_shape=[sds(192, 512), sds(192, 512),...]
    pallas_call x1, Pallas kernels: 3.28 us -> 6.93 us  [results(): pl.pallas_call(results_kernel, grid=(6,), out_shape=[sds(1536, 512), sds(...]
where the time goes in v5:
time: 174 us; the launch traced here: 173 us
  Pallas kernels  168 us (97%)
  local copies, waits for them, and re-layouts  3.26 us (2%)
    pallas_call x1, Pallas kernels, run_resampler(): pl.pallas_call(resampler_kernel, out_shape=[sds(192, 512), sds(192, 512),...  161 us
    pallas_call x1, Pallas kernels, results(): pl.pallas_call(results_kernel, grid=(6,), out_shape=[sds(1536, 512), sds(...  6.93 us

profile of v5, /device:TPU:0, one launch (start us, length us, event | category | flops | bytes accessed | tf_op | source)
XLA Modules:
  0.0 173.2 jit_solution(11987634985825770078)
XLA Ops:
  0.6 0.7 multiply_bitcast_fusion
  1.3 0.1 broadcast_bitcast_fusion
  1.4 0.7 copy_bitcast_fusion
  2.1 0.6 select_maximum_fusion.norms
  2.7 161.1 %resampler.1 = (f32[192,512]{1,0:T(8,128)}, f32[192,512]{1,0:T(8,128)}, f32[16,128]{1,0:T(8,128)}, f32[16,512]{1,0:T(8,128)}, f32[16,1024]{1,0:T(8,128)}, /*inde...) custom-call(bf16[192,1024]{1,0:T(8,128)(2,1)} %bitcast.32, ...), custom_call_target="tpu_custom_call" | custom-call | tf_op jit(solution)/shard_map/resampler/pallas_call | solution.py:754
  163.8 6.9 %results.1 = (f32[1536,512]{1,0:T(8,128)}, f32[1,3,16]{2,1,0:T(4,128)}, f32[1,3,16]{2,1,0:T(4,128)}, f32[192,512]{1,0:T(8,128)}, f32[192,512]{1,0:T(8,128)}, /*i...) custom-call(f32[6,2,256,256]{3,2,1,0:T(8,128)} %get-tuple-element.30.mi, ...), custom_call_target="tpu_custom_call" | custom-call | tf_op jit(solution)/shard_map/results/pallas_call | solution.py:830
  170.7 1.2 copy.24
  172.0 1.2 copy.25
  (1 shorter events, 0.0 us)

commit v6 on v5

--- a/solution.py
+++ b/solution.py
@@ -24,32 +24,33 @@
 R_PRE, R_OUT, R_ATT, R_QUERY, R_KV = 0, 16, 32, 36, 38
 PLAN = (
     (
-        ("down", 0, (A, C)),
         ("query", 0, (A, B, C)),
         ("query", 1, (A, B, C)),
+        ("down", 0, (A, C)),
         ("keyval", 0, (A, B, C)),
         ("keyval", 2, (A, B, C)),
         ("down", 1, (A, C)),
     ),
     (
         ("out", 0, (B, C, A)),
-        ("out", 1, (B, C, A)),
+        None,
         ("up", 0, (B, C)),
+        ("up", 1, (B, C)),
         ("keyval", 1, (B, C, A)),
-        ("up", 1, (B, C)),
         None,
     ),
     (
+        ("out", 1, (C, B, A)),
         ("down", 2, (C, A)),
-        ("down", 3, (C, A)),
         ("up", 2, (C, B)),
         ("up", 3, (C, B)),
         ("keyval", 3, (C, B, A)),
-        None,
+        ("down", 3, (C, A)),
     ),
 )
 GROUPS = 6
-TICKS = GROUPS + 4
+TICKS = GROUPS + 3
+STRAIGHT = 4
 WIDE = 4
 DEEP = 3
 WU_BASE = 34
@@ -105,10 +106,10 @@
 
 def resampler_kernel(
     latents, media, norms, w_query, w_keyval, w_out, w_up, w_down, cotangent,
-    resampled, latents_grad, out_small, out_query, out_keyval, out_out, out_up, out_down, m_own, m_got, land,
+    resampled, latents_grad, out_small, out_query, out_keyval, out_out, out_up, out_down, m_sum, m_own, m_got, land,
     wq, wkv, wo, xs, x1s, gys, accs, lin, ffin, qs, att, gatt, pres, sums, sent, m_stage, m_buf, wd, gave,
-    lefts, rights, own1, own2, own3, far1, far2, mine1, summed1, near2, last, up_sum, up_got, small_sum, small_got, columns,
-    a_sem, w_sem, b_sem, x_sem, g_sem, r_sem, l_sem, m_send, m_recv, m_local, e_send, e_recv, c_sem, t_send, t_recv, z_send, z_recv, u_send, u_recv, s_send, s_recv,
+    lefts, rights, own1, own2, own3, far1, far2, mine1, summed1, near2, last, straight, up_sum, up_got, small_sum, small_got, columns,
+    a_sem, w_sem, b_sem, x_sem, g_sem, r_sem, l_sem, m_send, m_recv, m_local, e_send, e_recv, c_sem, t_send, t_recv, z_send, z_recv, d_send, d_recv, u_send, u_recv, s_send, s_recv,
 ):
     section = lax.axis_index("section")
     other = 1 - section
@@ -135,6 +136,7 @@
     greeted = [(axis, shift) for axis in (A, B, C) for shift in (1, 2, 3)]
     for axis, shift in greeted:
         pl.semaphore_signal(barrier, inc=1, device_id={"dp": peer(axis, shift)}, device_id_type=MESH)
+
     pl.semaphore_wait(barrier, 1 + len(greeted))
 
     def to_other(source, target, sem):
@@ -146,8 +148,12 @@
     def up_block(step):
         return WU_BASE + 8 * (step % WIDE)
 
-    def weights(step):
-        copies = [pltpu.make_async_copy(w_down.at[pl.ds(pl.multiple_of(step * 512, 512), 512), :], wd.at[step % DEEP], w_sem.at[2, step % DEEP])]
+    def down_rows(step):
+        rows = pl.ds(pl.multiple_of(step * 512, 512), 512)
+        return [pltpu.make_async_copy(w_down.at[rows, :], wd.at[step % DEEP], w_sem.at[2, step % DEEP])]
+
+    def up_columns(step):
+        copies = []
         for k in range(2):
             cols = pl.ds(pl.multiple_of(step * 512 + COLS * k, COLS), COLS)
             copies.append(
@@ -155,21 +161,19 @@
             )
         return copies
 
-    def fetch(step):
-        for c in weights(step):
-            c.start()
-
     def fetch_first():
         for step in range(DEEP - 1):
-            fetch(step)
+            for c in down_rows(step) + up_columns(step):
+                c.start()
 
     def fetch_next(step):
         @pl.when(step + DEEP - 1 < FF_STEPS)
         def _():
-            fetch(step + DEEP - 1)
+            for c in down_rows(step + DEEP - 1) + up_columns(step + DEEP - 1):
+                c.start()
 
     def fetched(step):
-        for c in weights(step):
+        for c in down_rows(step) + up_columns(step):
             c.wait()
 
     def media_rows(i):
@@ -199,7 +203,7 @@
     def taken(kind, use, late=False):
         def held(s):
             if late:
-                return own1.at[pl.ds(8 + 12 * (s % 2), 4), pl.ds(0, ROWS_ALL), :]
+                return own1.at[pl.ds(24 + 4 * (s % 2), 4), pl.ds(0, ROWS_ALL), :]
             return m_stage.at[s % 2, :, pl.ds(0, ROWS_ALL), :]
 
         def load(s):
@@ -335,9 +339,7 @@
 
         taken(FF_IN, use_ff, late)
 
-    def turn_act():
-        for k in range(4):
-            lefts[L_ACT, k] = turned(own1[18 + 4 * coords[B] + k, pl.ds(0, ROWS_ALL), :])
+    def turn_att():
         for i in range(4):
             part = jnp.concatenate([att[:, pl.ds(128 * i, 128)].astype(F32), jnp.zeros((64, 128), F32)], 0)
             part = part.T.reshape(16, 8, 256)
@@ -345,6 +347,9 @@
             lefts[L_ATT, i] = jnp.concatenate([part, none], 1).reshape(256, 256).astype(BF16)
             lefts[L_ATT + 1, i] = jnp.concatenate([none, part], 1).reshape(256, 256).astype(BF16)
 
+    def turn_act():
+        for k in range(4):
+            lefts[L_ACT, k] = turned(own1[18 + 4 * coords[B] + k, pl.ds(0, ROWS_ALL), :])
         def use_act(s, piece):
             for k in range(4):
                 lefts[L_ACT + s, k] = turned(piece[k])
@@ -356,6 +361,7 @@
         to_other(accs, xs, x_sem).start()
         turn_ff(False)
         turn_act()
+        turn_att()
         to_other(accs, xs, x_sem).wait_send()
         to_other(accs, gys, g_sem).wait_recv()
         to_rows(gave.at[1], gys[...].astype(BF16).astype(F32))
@@ -446,7 +452,6 @@
     @pl.when(section == 1)
     def _():
         to_other(accs, gys, g_sem).start()
-        turn_act()
 
     @pl.when(section == 0)
     def _():
@@ -458,7 +463,6 @@
         for k in range(4):
             rights[R_OUT + 4 * s + k, pl.ds(0, ROWS_ALL), :] = piece[k].astype(BF16)
 
-    taken(G_OUT, use_out)
 
     def turn_pre():
         for k in range(4):
@@ -505,6 +509,29 @@
         for k in range(4):
             lefts[i, k] = turned(column(media_in, k).astype(BF16).astype(F32))
 
+    def media_parts(i):
+        return (
+            pltpu.make_async_copy(m_own.at[i], m_stage.at[i % 2, pl.ds(0, 2)], m_local.at[i]),
+            pltpu.make_async_copy(m_got.at[i], m_stage.at[i % 2, pl.ds(2, 2)], m_send.at[i]),
+        )
+
+    def media_done(i):
+        return pltpu.make_async_copy(m_stage.at[i % 2, pl.ds(0, 2)], m_sum.at[i], m_local.at[i])
+
+    def media_sum(first):
+        for i in (first, first + 1):
+            if i >= 2:
+                media_done(i - 2).wait()
+            media_away(i).wait_recv()
+            for c in media_parts(i):
+                c.start()
+        for i in (first, first + 1):
+            for c in media_parts(i):
+                c.wait()
+            for k in range(2):
+                m_stage[i % 2, k] += m_stage[i % 2, 2 + k]
+            media_done(i).start()
+
     places, steps = (x, y, z), (16, 4, 1)
 
     def small_copy(axis, shift):
@@ -544,15 +571,15 @@
     own = (own1, own2, own3)
 
     def spot(lane, group):
-        return (lane * 3 + group % 3) * 4
+        return (group % 3 * 3 + lane) * 4
 
     def pieces(what, axes, i, b, c):
         if what == "down":
             block = {A: by_section(i, b), C: by_section(b, i)}
             return block[axes[0]], block[axes[1]] * 4 + c
         block = {A: by_section(i, c), B: by_section(b, i), C: by_section(c, b)}
-        second, third = {A: (B, C), B: (C, A), C: (B, A)}[axes[0]]
-        return block[axes[0]], block[second] * 4 + block[third]
+        first, second, third = axes if len(axes) == 3 else axes + (A,)
+        return block[first], block[second] * 4 + block[third]
 
     def terms(lane, group):
         what, which, axes = PLAN[lane][group]
@@ -588,6 +615,15 @@
             device_id={"dp": peer(axis, shift)}, device_id_type=MESH,
         )
 
+    def straight_copy(lane, group, shift):
+        axis = PLAN[lane][group][2][1]
+        sem = (lane * 2 + group - STRAIGHT) * 3 + shift - 1
+        return pltpu.make_async_remote_copy(
+            src_ref=own2.at[spot(lane, group) + at(axis, shift)], dst_ref=straight.at[lane, group - STRAIGHT, shift - 1],
+            send_sem=d_send.at[sem], recv_sem=d_recv.at[sem],
+            device_id={"dp": peer(axis, shift)}, device_id_type=MESH,
+        )
+
     def last_turn(lane, group):
         return sum(1 for g in range(group) if runs(lane, g, 2)) % 3
 
@@ -626,6 +662,11 @@
 
     for k in range(4):
         lefts[L_LATENT, k] = turned(lin[:, pl.ds(COLS * k, COLS)].astype(F32))
+
+    @pl.when(section == 1)
+    def _():
+        turn_att()
+
     media_rows(0).start()
     ups = 0
     for t in range(TICKS):
@@ -635,79 +676,104 @@
                 for way in range(2):
                     ring_copy(lane, t, 0, 0, way).start()
         if t == 0:
+
+            @pl.when(section == 1)
+            def _():
+                turn_act()
+
+            taken(G_OUT, use_out)
             media_back(0)
-            media_back(1)
         if t == 1:
-            media_back(2)
-            media_back(3)
 
             @pl.when(section == 1)
             def _():
                 turn_ff(True)
 
             turn_pre()
+            media_back(1)
+            media_back(2)
         if t == 2:
+            media_back(3)
             media_back(4)
             media_back(5)
             small_give(0)
+        if t in (4, 5, 6):
+            if t == 4:
+                for i in (4, 5):
+                    media_away(i).wait_send()
+                    media_home(i).wait()
+            media_sum(2 * t - 8)
         if t in (3, 4, 5):
             small_take(t - 3)
             if t < 5:
                 small_give(t - 2)
         for lane in range(3):
-            for stage in range(2):
-                half = RING_ROWS[stage] // 2
-                group = t - 1 - 2 * stage
-                if runs(lane, group, stage):
-                    axis = PLAN[lane][group][2][stage]
-                    for way in range(2):
-                        ring_copy(lane, group, stage, 0, way).wait()
-                        arrived = far1[lane, way, group % 3] if stage == 0 else far2[lane, way, group % 2]
-                        own[stage][spot(lane, group) + at(axis, 1 if way == 0 else 3), pl.ds(way * half, half), :] += arrived
-                group = t - 2 - 2 * stage
-                if runs(lane, group, stage):
+            group = t - 1
+            if runs(lane, group, 0):
+                axis = PLAN[lane][group][2][0]
+                for way in range(2):
+                    ring_copy(lane, group, 0, 0, way).wait()
+                    own1[spot(lane, group) + at(axis, 1 if way == 0 else 3), pl.ds(way * 128, 128), :] += far1[lane, way, group % 3]
+            group = t - 2
+            if runs(lane, group, 0):
+                for way in range(2):
+                    ring_copy(lane, group, 0, 1, way).wait()
+                    ring_copy(lane, group, 0, 2, way).wait()
+                mine = spot(lane, group) + at(PLAN[lane][group][2][0], 0)
+                three, two = group % 3, group % 2
+                total = [
+                    own1[mine, pl.ds(0, 128), :] + summed1[lane, 0, two] + mine1[lane, 1, three],
+                    own1[mine, pl.ds(128, 128), :] + mine1[lane, 0, three] + summed1[lane, 1, two],
+                ]
+                for k in range(4):
+                    own2[spot(lane, group) + k] = total[k // 2][64 * (k % 2) : 64 * (k % 2) + 64]
+            group = t - 3
+            if runs(lane, group, 1) and group < STRAIGHT:
+                axis = PLAN[lane][group][2][1]
+                for way in range(2):
+                    ring_copy(lane, group, 1, 0, way).wait()
+                    own2[spot(lane, group) + at(axis, 1 if way == 0 else 3), pl.ds(way * 32, 32), :] += far2[lane, way, group % 2]
+            for group in (t - 3, t - 4):
+                if runs(lane, group, 1) and (group >= STRAIGHT) == (group == t - 3):
                     what, which, axes = PLAN[lane][group]
-                    for way in range(2):
-                        ring_copy(lane, group, stage, 1, way).wait()
-                        if stage == 0:
-                            ring_copy(lane, group, stage, 2, way).wait()
-                    mine = spot(lane, group) + at(axes[stage], 0)
-                    rows = RING_ROWS[stage + 1]
-                    if stage == 0:
-                        three, two = group % 3, group % 2
-                        total = [
-                            own1[mine, pl.ds(0, 128), :] + summed1[lane, 0, two] + mine1[lane, 1, three],
-                            own1[mine, pl.ds(128, 128), :] + mine1[lane, 0, three] + summed1[lane, 1, two],
-                        ]
+                    total = own2[spot(lane, group) + at(axes[1], 0)]
+                    if group < STRAIGHT:
+                        for way in range(2):
+                            ring_copy(lane, group, 1, 1, way).wait()
+                            total += near2[lane, way, group % 2]
+                    else:
+                        for shift in (1, 2, 3):
+                            straight_copy(lane, group, shift).wait()
+                            total += straight[lane, group - STRAIGHT, shift - 1]
+                    if len(axes) == 3:
                         for k in range(4):
-                            own2[spot(lane, group) + k] = total[k // 2][rows * (k % 2) : rows * (k % 2) + rows]
+                            own3[spot(lane, group) + k] = total[16 * k : 16 * k + 16]
                     else:
-                        total = own2[mine] + near2[lane, 0, group % 2] + near2[lane, 1, group % 2]
-                        if len(axes) == 3:
-                            for k in range(4):
-                                own3[spot(lane, group) + k] = total[rows * k : rows * k + rows]
-                        else:
-                            finish(what, which, total)
-                            if what == "up":
-                                ups += 1
-            group = t - 5
-            if runs(lane, group, 2):
-                what, which, axes = PLAN[lane][group]
-                total = own3[spot(lane, group) + at(axes[2], 0)]
-                for shift in (1, 2, 3):
-                    last_copy(lane, group, shift).wait()
-                    total += last[lane, last_turn(lane, group), shift - 1]
-                finish(what, which, total)
+                        finish(what, which, total)
+                        if what == "up":
+                            ups += 1
+            for group in (t - 4, t - 5):
+                if runs(lane, group, 2) and (group >= STRAIGHT) == (group == t - 4):
+                    what, which, axes = PLAN[lane][group]
+                    total = own3[spot(lane, group) + at(axes[2], 0)]
+                    for shift in (1, 2, 3):
+                        last_copy(lane, group, shift).wait()
+                        total += last[lane, last_turn(lane, group), shift - 1]
+                    finish(what, which, total)
         for lane in range(3):
             for way in range(2):
                 if runs(lane, t - 1, 0):
                     ring_copy(lane, t - 1, 0, 2, way).start()
-                if runs(lane, t - 2, 1):
+                if runs(lane, t - 2, 1) and t - 2 < STRAIGHT:
                     ring_copy(lane, t - 2, 1, 0, way).start()
-                if runs(lane, t - 3, 1):
+                if runs(lane, t - 3, 1) and t - 3 < STRAIGHT:
                     ring_copy(lane, t - 3, 1, 1, way).start()
-            if runs(lane, t - 4, 2):
-                for shift in (1, 2, 3):
+            for shift in (1, 2, 3):
+                if runs(lane, t - 2, 1) and t - 2 >= STRAIGHT:
+                    straight_copy(lane, t - 2, shift).start()
+                if runs(lane, t - 3, 2) and t - 3 >= STRAIGHT:
+                    last_copy(lane, t - 3, shift).start()
+                if runs(lane, t - 4, 2) and t - 4 < STRAIGHT:
                     last_copy(lane, t - 4, shift).start()
             for way in range(2):
                 if runs(lane, t, 0):
@@ -726,10 +792,7 @@
         out_up[:, cols] = part
 
     for i in (4, 5):
-        media_away(i).wait_send()
-        media_home(i).wait()
-    for i in range(6):
-        media_away(i).wait_recv()
+        media_done(i).wait()
 
     @pl.when(section == 0)
     def _():
@@ -755,10 +818,10 @@
         resampler_kernel,
         out_shape=[
             sds(192, 512), sds(192, 512), sds(16, 128), sds(16, 512), sds(16, 1024), sds(8, 1024), sds(16, 4096), sds(64, 1024),
-            sds(6, 2, 256, 256), sds(6, 2, 256, 256), sds(4, 3, 4, 192, 256),
+            sds(6, 2, 256, 256), sds(6, 2, 256, 256), sds(6, 2, 256, 256), sds(4, 3, 4, 192, 256),
         ],
         in_specs=[hbm, hbm, vmem] + [hbm] * 6,
-        out_specs=[vmem] * 8 + [hbm] * 3,
+        out_specs=[vmem] * 8 + [hbm] * 4,
         scratch_shapes=[
             pltpu.VMEM((1, 1024, 512), BF16),
             pltpu.VMEM((1, 1024, 1024), BF16),
@@ -790,52 +853,57 @@
             pltpu.VMEM((3, 2, 2, 128, COLS), F32),
             pltpu.VMEM((3, 2, 2, 64, COLS), F32),
             pltpu.VMEM((3, 3, 3, 16, COLS), F32),
+            pltpu.VMEM((3, 2, 3, 64, COLS), F32),
             pltpu.VMEM((64, 1024), F32),
             pltpu.VMEM((3, 16, 1024), F32),
             pltpu.VMEM((2, 8, COLS), F32),
             pltpu.VMEM((3, 3, 8, COLS), F32),
             pltpu.VMEM((COLS, 128), F32),
             dma((3,)), dma((3, 4)), dma((2,)), dma((2,)), dma((2,)), dma((2,)), dma((2,)), dma((6,)), dma((6,)), dma((6,)),
-            dma((4, 3)), dma((4, 3)), dma((2,)), dma((108,)), dma((108,)), dma((27,)), dma((27,)), dma((3,)), dma((3,)), dma((3, 3)), dma((3, 3)),
+            dma((4, 3)), dma((4, 3)), dma((2,)), dma((108,)), dma((108,)), dma((27,)), dma((27,)), dma((18,)), dma((18,)), dma((3,)), dma((3,)), dma((3, 3)), dma((3, 3)),
         ],
         compiler_params=pltpu.CompilerParams(collective_id=1, has_side_effects=True, vmem_limit_bytes=VMEM_BYTES),
         name="resampler",
     )(latents, media, norms, w_query, w_keyval, w_out, w_up, w_down, cotangent)
 
 
-def results_kernel(mine, theirs, *refs):
-    given, made = refs[:8], refs[8:]
-    total = mine[0] + theirs[0]
-    made[0][:, pl.ds(0, COLS)] = total[0]
-    made[0][:, pl.ds(COLS, COLS)] = total[1]
-
-    @pl.when(pl.program_id(0) == 0)
-    def _():
-        for source, target in zip(given[1:], made[3:]):
-            target[...] = source[...]
-        columns = given[0][...].T
-        made[1][0] = columns[:3]
-        made[2][0] = columns[3:6]
-
-
-def results(mine, theirs, small, resampled, latents_grad, query, keyval, out, up, down):
-    rest = [resampled, latents_grad, query, keyval, out, up, down]
-    whole = [pl.BlockSpec(a.shape, lambda i: (0, 0)) for a in rest]
+def results_kernel(small, media, *refs):
+    given, (media_grad, gains_grad, biases_grad), made, held, sem = refs[:7], refs[7:10], refs[10:17], refs[17:25], refs[25]
+    moves = []
+    for i in range(6):
+        for k in range(2):
+            moves.append((media.at[i, k], held[7].at[i, k], media_grad.at[pl.ds(COLS * i, COLS), pl.ds(COLS * k, COLS)]))
+    moves += list(zip(given, held, made))
+    loads = [pltpu.make_async_copy(a, b, sem.at[0, n]) for n, (a, b, _) in enumerate(moves)]
+    stores = [pltpu.make_async_copy(b, c, sem.at[1, n]) for n, (_, b, c) in enumerate(moves)]
+    for c in loads:
+        c.start()
+    columns = jnp.concatenate([small[...], jnp.zeros((112, 128), F32)], 0).T
+    gains_grad[0] = columns[:3, :16]
+    biases_grad[0] = columns[3:6, :16]
+    for a, b in zip(loads, stores):
+        a.wait()
+        b.start()
+    for c in stores:
+        c.wait()
+
+
+def results(media, small, *rest):
+    vmem = pl.BlockSpec(memory_space=pltpu.VMEM)
+    hbm = pl.BlockSpec(memory_space=pl.ANY)
 
     def sds(*shape):
         return jax.ShapeDtypeStruct(shape, F32)
 
-    part = pl.BlockSpec((1, 2, COLS, COLS), lambda i: (i, 0, 0, 0))
-    norms = pl.BlockSpec((1, 3, 16), lambda i: (0, 0, 0))
     return pl.pallas_call(
         results_kernel,
-        grid=(6,),
         out_shape=[sds(1536, 512), sds(1, 3, 16), sds(1, 3, 16)] + [sds(*a.shape) for a in rest],
-        in_specs=[part, part, pl.BlockSpec((16, 128), lambda i: (0, 0))] + whole,
-        out_specs=[pl.BlockSpec((COLS, 512), lambda i: (i, 0)), norms, norms] + whole,
+        in_specs=[vmem] + [hbm] * 8,
+        out_specs=[hbm, vmem, vmem] + [hbm] * 7,
+        scratch_shapes=[pltpu.VMEM(a.shape, F32) for a in rest + (media,)] + [pltpu.SemaphoreType.DMA((2, 19))],
         compiler_params=pltpu.CompilerParams(vmem_limit_bytes=VMEM_BYTES),
         name="results",
-    )(mine, theirs, small, *rest)
+    )(small, media, *rest)
 
 
 def body(
@@ -843,12 +911,12 @@
 ):
     frames = jnp.broadcast_to(64.0 * frame_count.astype(F32)[:, :1], (3, COLS)).reshape(1, 768)
     norms = jnp.concatenate([gains[0], biases[0], jnp.pad(frames, ((0, 1), (0, 256)))], 0)
-    resampled, latents_grad, small, query, keyval, out, up, down, mine, theirs, _ = run_resampler(
+    resampled, latents_grad, small, query, keyval, out, up, down, media_sum, _, _, _ = run_resampler(
         latents_in.reshape(192, 1024), media.reshape(1536, 1024), norms,
         w_query, w_keyval, w_out, w_up.reshape(4, 256, 4096), w_down.reshape(4096, 1024), cotangent.reshape(192, 1024),
     )
     media_grad, gains_grad, biases_grad, resampled, latents_grad, query, keyval, out, up, down = results(
-        mine, theirs, small, resampled, latents_grad, query, keyval, out, up, down
+        media_sum, small, resampled, latents_grad, query, keyval, out, up, down
     )
     return (
         resampled.reshape(3, 1, 64, 512),

time: 174 us -> 167 us (0.960)
  Pallas kernels: 168 us -> 161 us
    pallas_call x1, Pallas kernels: 161 us -> 156 us  [run_resampler(): pl.pallas_call(resampler_kernel, out_shape=[sds(192, 512), sds(192, 512),...]
where the time goes in v6:
time: 167 us
  Pallas kernels  161 us (96%)
  local copies, waits for them, and re-layouts  3.25 us (2%)
    pallas_call x1, Pallas kernels, run_resampler(): pl.pallas_call(resampler_kernel, out_shape=[sds(192, 512), sds(192, 512),...  156 us
    pallas_call x1, Pallas kernels, results(): pl.pallas_call(results_kernel, out_shape=[sds(1536, 512), sds(1, 3, 16),...  5.6 us

profile of v6, /device:TPU:0, one launch (start us, length us, event | category | flops | bytes accessed | tf_op | source)
XLA Modules:
  0.0 166.6 jit_solution(13127955365251671042)
XLA Ops:
  0.6 0.7 multiply_bitcast_fusion
  1.3 0.1 broadcast_bitcast_fusion
  1.4 0.7 copy_bitcast_fusion
  2.1 0.6 select_maximum_fusion.norms
  2.7 155.8 %resampler.1 = (f32[192,512]{1,0:T(8,128)}, f32[192,512]{1,0:T(8,128)}, f32[16,128]{1,0:T(8,128)}, f32[16,512]{1,0:T(8,128)}, f32[16,1024]{1,0:T(8,128)}, /*inde...) custom-call(bf16[192,1024]{1,0:T(8,128)(2,1)} %bitcast.32, ...), custom_call_target="tpu_custom_call" | custom-call | tf_op jit(solution)/shard_map/resampler/pallas_call | solution.py:817
  158.6 5.6 %results.1 = (f32[1536,512]{1,0:T(8,128)}, f32[1,3,16]{2,1,0:T(4,128)}, f32[1,3,16]{2,1,0:T(4,128)}, f32[192,512]{1,0:T(8,128)}, f32[192,512]{1,0:T(8,128)}, /*i...) custom-call(f32[16,128]{1,0:T(8,128)} %get-tuple-element.29.small, ...), custom_call_target="tpu_custom_call" | custom-call | tf_op jit(solution)/shard_map/results/pallas_call | solution.py:898
  164.2 1.2 copy.24
  165.4 1.2 copy.25
  (1 shorter events, 0.0 us)

commit v7 on v6

--- a/solution.py
+++ b/solution.py
@@ -775,6 +775,7 @@
                     last_copy(lane, t - 3, shift).start()
                 if runs(lane, t - 4, 2) and t - 4 < STRAIGHT:
                     last_copy(lane, t - 4, shift).start()
+        for lane in range(3):
             for way in range(2):
                 if runs(lane, t, 0):
                     ring_copy(lane, t, 0, 1, way).start()

time: 167 us -> 165 us (0.988)
  Pallas kernels: 161 us -> 159 us
    pallas_call x1, Pallas kernels: 156 us -> 154 us  [run_resampler(): pl.pallas_call(resampler_kernel, out_shape=[sds(192, 512), sds(192, 512),...]
where the time goes in v7:
time: 165 us
  Pallas kernels  159 us (96%)
  local copies, waits for them, and re-layouts  3.25 us (2%)
    pallas_call x1, Pallas kernels, run_resampler(): pl.pallas_call(resampler_kernel, out_shape=[sds(192, 512), sds(192, 512),...  154 us
    pallas_call x1, Pallas kernels, results(): pl.pallas_call(results_kernel, out_shape=[sds(1536, 512), sds(1, 3, 16),...  5.6 us

profile of v7, /device:TPU:0, one launch (start us, length us, event | category | flops | bytes accessed | tf_op | source)
XLA Modules:
  0.0 164.5 jit_solution(7629613921800297066)
XLA Ops:
  0.6 0.7 multiply_bitcast_fusion
  1.3 0.1 broadcast_bitcast_fusion
  1.4 0.7 copy_bitcast_fusion
  2.1 0.6 select_maximum_fusion.norms
  2.7 153.7 %resampler.1 = (f32[192,512]{1,0:T(8,128)}, f32[192,512]{1,0:T(8,128)}, f32[16,128]{1,0:T(8,128)}, f32[16,512]{1,0:T(8,128)}, f32[16,1024]{1,0:T(8,128)}, /*inde...) custom-call(bf16[192,1024]{1,0:T(8,128)(2,1)} %bitcast.32, ...), custom_call_target="tpu_custom_call" | custom-call | tf_op jit(solution)/shard_map/resampler/pallas_call | solution.py:818
  156.5 5.6 %results.1 = (f32[1536,512]{1,0:T(8,128)}, f32[1,3,16]{2,1,0:T(4,128)}, f32[1,3,16]{2,1,0:T(4,128)}, f32[192,512]{1,0:T(8,128)}, f32[192,512]{1,0:T(8,128)}, /*i...) custom-call(f32[16,128]{1,0:T(8,128)} %get-tuple-element.29.small, ...), custom_call_target="tpu_custom_call" | custom-call | tf_op jit(solution)/shard_map/results/pallas_call | solution.py:899
  162.1 1.2 copy.24
  163.3 1.2 copy.25
  (1 shorter events, 0.0 us)
